TPU v7x, 256 devices: a whole 4x4x8 slice. The times are simulated.
256 devices in a mesh: gx: 32 (over y, z), gy: 8 (over x, core).
Axes of the slice: x: 4, y: 4, z: 8, core: 2. Of those that a mesh axis runs over, the one named last changes fastest.
Arguments:
- source: float32 [16, 512, 2048], P(None, 'gx', 'gy'), may hold values from -540 to 540
Outputs:
- pressure: float32 [16, 512, 2048], P(None, 'gx', 'gy')
All inputs are finite; a program needn't handle non-finite values.
Results may differ from a plain program's by a relative error of at most 0.00085.
Values sent between devices are 32-bit elements; how exact they have to be, the bound alone decides.
No kernel may reach another device: no remote copies, remote signals or barrier semaphores. Data moves between devices by JAX's collectives and lax.ppermute only.
A program may use at most 128 MiB of HBM per device.

v0:
```python
import math

import jax
import jax.numpy as jnp
import numpy as np
from jax import lax
from jax.sharding import PartitionSpec as P

NODES_FINE = 8
NODES_MID = 4
NODES_COARSE = 2
CHEB_DEGREE = 3
CG_ITERS = 8


mass_coef = 0.000125
cheb_ratio = 0.1
highest = lax.Precision.HIGHEST


def with_halo(cells, sides, width):
    for axis, dim in sides:
        count = lax.axis_size(axis)
        head = lax.slice_in_dim(cells, 0, width, axis=dim)
        tail = lax.slice_in_dim(cells, cells.shape[dim] - width, cells.shape[dim], axis=dim)
        cells = jnp.concatenate(
            [
                lax.ppermute(tail, axis, [(i, (i + 1) % count) for i in range(count)]),
                cells,
                lax.ppermute(head, axis, [((i + 1) % count, i) for i in range(count)]),
            ],
            axis=dim,
        )
    return cells


def legendre_pair(points, order):
    previous = 0.0 * points + 1.0
    current = points * 1.0
    for degree in range(2, order + 1):
        previous, current = (
            current,
            ((2.0 * degree - 1.0) * points * current - (degree - 1.0) * previous) / degree,
        )
    return (previous, current)


def gll_tables(order):
    count_nodes = order + 1
    points = -np.cos(math.pi * np.arange(count_nodes) / order)
    for sweep in range(60):
        previous, values_at = legendre_pair(points, order)
        points = points - (points * values_at - previous) / (count_nodes * values_at)
    previous, values_at = legendre_pair(points, order)
    weights = 2.0 / (order * (order + 1) * values_at * values_at)
    spacing = points[:, None] - points[None, :]
    safe_spacing = np.where(spacing == 0.0, 1.0, spacing)
    derivative = values_at[:, None] / (values_at[None, :] * safe_spacing)
    derivative = derivative * (1.0 - np.eye(count_nodes))
    corner_value = order * (order + 1) / 4.0
    end_values = np.concatenate(
        [np.array([-corner_value]), np.zeros(count_nodes - 2), np.array([corner_value])]
    )
    return (points, weights, derivative + np.eye(count_nodes) * end_values[None, :])


def interp_table(fine_order, coarse_order):
    fine_points = gll_tables(fine_order)[0]
    coarse_points = gll_tables(coarse_order)[0]
    numer = fine_points[:, None, None] - coarse_points[None, None, :]
    denom = coarse_points[None, :, None] - coarse_points[None, None, :]
    same_node = np.eye(len(coarse_points))[None, :, :] > 0.5
    ratio = np.where(same_node, 1.0, numer / np.where(same_node, 1.0, denom))
    return ratio.prod(axis=2)


def element_bound(order):
    points, weights, derivative = gll_tables(order)
    mass = np.eye(order + 1) * weights[None, :]
    stiff = np.dot(derivative.T, np.dot(mass, derivative))
    full = 0.5 * (
        np.kron(np.kron(mass, mass), stiff)
        + np.kron(np.kron(mass, stiff), mass)
        + np.kron(np.kron(stiff, mass), mass)
    ) + mass_coef * np.kron(np.kron(mass, mass), mass)
    diagonal_entries = np.sum(full * np.eye(full.shape[0]), axis=1)
    ratio = np.abs(full).sum(axis=1) / diagonal_entries
    return float(ratio.max())


def tiled(table, length):
    return jnp.tile(jnp.asarray(table, dtype=jnp.float32), length // table.shape[0])


def layer_share(length, count_nodes):
    position = jnp.arange(length)
    node_index = position % count_nodes
    layer_index = position // count_nodes
    shared = (node_index == 0) & (layer_index > 0) | (node_index == count_nodes - 1) & (
        layer_index < length // count_nodes - 1
    )
    return jnp.where(shared, 0.5, 1.0).astype(jnp.float32)


def plane_share(length, count_nodes):
    node_index = jnp.arange(length) % count_nodes
    return jnp.where((node_index == 0) | (node_index == count_nodes - 1), 0.5, 1.0).astype(
        jnp.float32
    )


def node_masks(length, count_nodes):
    node_index = jnp.arange(length) % count_nodes
    return (node_index == 0, node_index == count_nodes - 1)


def fold_pair(center, before, after, lead_mask, tail_mask):
    return center + jnp.where(lead_mask, before, 0.0) + jnp.where(tail_mask, after, 0.0)


def fold_depth(field_in, count_nodes):
    zero_plane = jnp.zeros_like(field_in[:1])
    before = jnp.concatenate([zero_plane, field_in[:-1]], axis=0)
    after = jnp.concatenate([field_in[1:], zero_plane], axis=0)
    lead_mask, tail_mask = node_masks(field_in.shape[0], count_nodes)
    return fold_pair(field_in, before, after, lead_mask[:, None, None], tail_mask[:, None, None])


def assemble(field_in, count_nodes):
    rows_lead, rows_tail = node_masks(field_in.shape[1], count_nodes)
    cols_lead, cols_tail = node_masks(field_in.shape[2], count_nodes)
    rows_lead = rows_lead[:, None]
    rows_tail = rows_tail[:, None]
    framed = with_halo(field_in, (("gx", 1), ("gy", 2)), 1)
    across = fold_pair(
        framed[:, 1:-1, :], framed[:, :-2, :], framed[:, 2:, :], rows_lead, rows_tail
    )
    summed = fold_pair(
        across[:, :, 1:-1], across[:, :, :-2], across[:, :, 2:], cols_lead, cols_tail
    )
    return fold_depth(summed, count_nodes)


def along_depth(field_in, matrix):
    count_in = matrix.shape[1]
    blocks = field_in.reshape(
        field_in.shape[0] // count_in, count_in, field_in.shape[1], field_in.shape[2]
    )
    result = jnp.einsum("oi,eixy->eoxy", matrix, blocks, precision=highest)
    return result.reshape(-1, field_in.shape[1], field_in.shape[2])


def along_rows(field_in, matrix):
    count_in = matrix.shape[1]
    blocks = field_in.reshape(
        field_in.shape[0], field_in.shape[1] // count_in, count_in, field_in.shape[2]
    )
    result = jnp.einsum("oi,zeiy->zeoy", matrix, blocks, precision=highest)
    return result.reshape(field_in.shape[0], -1, field_in.shape[2])


def along_columns(field_in, matrix):
    count_in = matrix.shape[1]
    elements = field_in.shape[2] // count_in
    group = math.gcd(elements, max(1, 128 // count_in))
    blocked = jnp.kron(jnp.eye(group, dtype=jnp.float32), matrix)
    pieces = field_in.reshape(
        field_in.shape[0], field_in.shape[1], elements // group, group * count_in
    )
    result = jnp.einsum("oi,zxbi->zxbo", blocked, pieces, precision=highest)
    return result.reshape(field_in.shape[0], field_in.shape[1], -1)


def level_core(order, shape):
    points, weights, derivative = gll_tables(order)
    count_nodes = order + 1
    stiff_diag = np.sum(weights[:, None] * derivative * derivative, axis=0)
    depth_w = tiled(weights, shape[0])
    rows_w = tiled(weights, shape[1])
    cols_w = tiled(weights, shape[2])
    depth_k = tiled(stiff_diag, shape[0])
    rows_k = tiled(stiff_diag, shape[1])
    cols_k = tiled(stiff_diag, shape[2])
    weight_cube = depth_w[:, None, None] * rows_w[None, :, None] * cols_w[None, None, :]
    local_diag = (
        0.5
        * (
            depth_w[:, None, None] * rows_k[None, :, None] * cols_w[None, None, :]
            + depth_w[:, None, None] * rows_w[None, :, None] * cols_k[None, None, :]
            + depth_k[:, None, None] * rows_w[None, :, None] * cols_w[None, None, :]
        )
        + mass_coef * weight_cube
    )
    shares = (
        layer_share(shape[0], count_nodes),
        plane_share(shape[1], count_nodes),
        plane_share(shape[2], count_nodes),
    )
    return (
        count_nodes,
        jnp.asarray(derivative, dtype=jnp.float32),
        weight_cube,
        local_diag,
        shares,
    )


def build_level(order, shape):
    count_nodes, derivative, weight_cube, local_diag, shares = level_core(order, shape)
    inverse_diag = 1.0 / assemble(local_diag, count_nodes)
    return (count_nodes, derivative, weight_cube, inverse_diag, shares, element_bound(order))


def apply_share(field_in, level):
    shares = level[4]
    return field_in * shares[0][:, None, None] * shares[1][None, :, None] * shares[2][None, None, :]


def local_op(field_in, level):
    derivative = level[1]
    weight_cube = level[2]
    gradient = along_rows(field_in, derivative)
    total = along_rows(weight_cube * gradient, derivative.T)
    gradient = along_columns(field_in, derivative)
    total = total + along_columns(weight_cube * gradient, derivative.T)
    gradient = along_depth(field_in, derivative)
    total = total + along_depth(weight_cube * gradient, derivative.T)
    return 0.5 * total + mass_coef * (weight_cube * field_in)


def apply_op(field_in, level):
    return assemble(local_op(field_in, level), level[0])


def restrict(field_in, table):
    matrix = table.T
    return along_columns(along_rows(along_depth(field_in, matrix), matrix), matrix)


def prolong(field_in, table):
    return along_columns(along_rows(along_depth(field_in, table), table), table)


def smooth_level(level, solution, rhs, start_zero):
    upper = level[5]
    lower = cheb_ratio * upper
    center = 0.5 * (upper + lower)
    half_width = 0.5 * (upper - lower)
    inverse_diag = level[3]
    if start_zero:
        residual = rhs
    else:
        residual = rhs - apply_op(solution, level)
    sigma_one = center / half_width
    rho_now = 1.0 / sigma_one
    direction = inverse_diag * residual / center
    for index in range(CHEB_DEGREE):
        solution = solution + direction
        if index + 1 < CHEB_DEGREE:
            residual = residual - apply_op(direction, level)
            rho_next = 1.0 / (2.0 * sigma_one - rho_now)
            direction = rho_next * rho_now * direction + 2.0 * rho_next / half_width * (
                inverse_diag * residual
            )
            rho_now = rho_next
    return solution


def weighted_norm(residual, level):
    return lax.psum(jnp.sum(apply_share(residual * residual, level)), ("gx", "gy"))


def weighted_curvature(direction, image, level):
    return lax.psum(jnp.sum(apply_share(direction * image, level)), ("gx", "gy"))


def coarse_solve(rhs, level):
    solution = jnp.zeros_like(rhs)
    residual = rhs
    direction = rhs
    norm_now = weighted_norm(residual, level)
    for index in range(CG_ITERS):
        image = apply_op(direction, level)
        alpha = norm_now / weighted_curvature(direction, image, level)
        solution = solution + alpha * direction
        residual = residual - alpha * image
        if index + 1 < CG_ITERS:
            norm_next = weighted_norm(residual, level)
            direction = residual + norm_next / norm_now * direction
            norm_now = norm_next
    return solution


def local(source):
    depth_len, rows_len, cols_len = source.shape
    layer_count = depth_len // NODES_FINE
    rows_elems = rows_len // NODES_FINE
    cols_elems = cols_len // NODES_FINE
    fine = build_level(NODES_FINE - 1, source.shape)
    middle = build_level(
        NODES_MID - 1, (layer_count * NODES_MID, rows_elems * NODES_MID, cols_elems * NODES_MID)
    )
    coarse = build_level(
        NODES_COARSE - 1,
        (layer_count * NODES_COARSE, rows_elems * NODES_COARSE, cols_elems * NODES_COARSE),
    )
    fine_table = jnp.asarray(interp_table(NODES_FINE - 1, NODES_MID - 1), dtype=jnp.float32)
    coarse_table = jnp.asarray(interp_table(NODES_MID - 1, NODES_COARSE - 1), dtype=jnp.float32)
    rhs_fine = assemble(0.125 * fine[2] * source, fine[0])
    fine_x = smooth_level(fine, jnp.zeros_like(rhs_fine), rhs_fine, True)
    fine_r = rhs_fine - apply_op(fine_x, fine)
    rhs_mid = assemble(restrict(apply_share(fine_r, fine), fine_table), middle[0])
    mid_x = smooth_level(middle, jnp.zeros_like(rhs_mid), rhs_mid, True)
    mid_r = rhs_mid - apply_op(mid_x, middle)
    rhs_coarse = assemble(restrict(apply_share(mid_r, middle), coarse_table), coarse[0])
    coarse_x = coarse_solve(rhs_coarse, coarse)
    mid_x = smooth_level(middle, mid_x + prolong(coarse_x, coarse_table), rhs_mid, False)
    return smooth_level(fine, fine_x + prolong(mid_x, fine_table), rhs_fine, False)


def solution(mesh):
    return jax.shard_map(
        local,
        mesh=mesh,
        in_specs=(P(None, "gx", "gy"),),
        out_specs=P(None, "gx", "gy"),
        check_vma=False,
    )
```

profile of v0, /device:TPU:1, one launch (start us, length us, event | category | flops | bytes accessed | tf_op | source)
XLA Modules:
  0.0 1557.6 jit_solution(5132635952596894682)
XLA Ops:
  6.8 6.5 collective-permute-start.5
  13.4 4.8 collective-permute-start.1
  34.1 4.8 collective-permute-start.17
  55.2 5.0 collective-permute-start.9
  71.5 5.4 collective-permute-start.13
  88.6 5.5 collective-permute-start.21
  140.0 5.1 collective-permute-start.33
  153.6 5.2 collective-permute-start.37
  161.1 4.9 collective-permute-start.39
  190.2 5.1 collective-permute-start.45
  202.5 81.3 %all-reduce.50 = (f32[]{:T(128)}, f32[]{:T(128)}) all-reduce(f32[]{:T(128)} %get-tuple-element.6, f32[]{:T(128)} %get-tuple-element.5), channel_id=1, replica_groups=mesh['gx'=32,'gy'=8] {'gx','gy'}, use_global_device_ids=true, to_apply=%region_1.2 | all-reduce | flops 2 | bytes 16 | tf_op jit(solution)/shard_map/psum | solution.py:270
  285.9 72.7 %psum.114 = f32[]{:T(128)} all-reduce(f32[]{:T(128)} %multiply_reduce_fusion.13), channel_id=1, replica_groups=mesh['gx'=32,'gy'=8] {'gx','gy'}, use_global_device_ids=true, to_apply=%region_5.6 | all-reduce | flops 1 | bytes 8 | tf_op jit(solution)/shard_map/psum | solution.py:270
  373.4 78.6 %psum.115 = f32[]{:T(128)} all-reduce(f32[]{:T(128)} %get-tuple-element.33), channel_id=1, replica_groups=mesh['gx'=32,'gy'=8] {'gx','gy'}, use_global_device_ids=true, to_apply=%region_7.8 | all-reduce | flops 1 | bytes 8 | tf_op jit(solution)/shard_map/psum | solution.py:274
  454.0 72.5 %psum.116 = f32[]{:T(128)} all-reduce(f32[]{:T(128)} %get-tuple-element.31), channel_id=1, replica_groups=mesh['gx'=32,'gy'=8] {'gx','gy'}, use_global_device_ids=true, to_apply=%region_9.10 | all-reduce | flops 1 | bytes 8 | tf_op jit(solution)/shard_map/psum | solution.py:270
  541.5 78.2 %psum.117 = f32[]{:T(128)} all-reduce(f32[]{:T(128)} %get-tuple-element.29), channel_id=1, replica_groups=mesh['gx'=32,'gy'=8] {'gx','gy'}, use_global_device_ids=true, to_apply=%region_11.12 | all-reduce | flops 1 | bytes 8 | tf_op jit(solution)/shard_map/psum | solution.py:274
  621.7 72.4 %psum.118 = f32[]{:T(128)} all-reduce(f32[]{:T(128)} %get-tuple-element.27), channel_id=1, replica_groups=mesh['gx'=32,'gy'=8] {'gx','gy'}, use_global_device_ids=true, to_apply=%region_13.14 | all-reduce | flops 1 | bytes 8 | tf_op jit(solution)/shard_map/psum | solution.py:270
  709.1 78.1 %psum.119 = f32[]{:T(128)} all-reduce(f32[]{:T(128)} %get-tuple-element.25), channel_id=1, replica_groups=mesh['gx'=32,'gy'=8] {'gx','gy'}, use_global_device_ids=true, to_apply=%region_15.16 | all-reduce | flops 1 | bytes 8 | tf_op jit(solution)/shard_map/psum | solution.py:274
  789.3 72.5 %psum.120 = f32[]{:T(128)} all-reduce(f32[]{:T(128)} %get-tuple-element.23), channel_id=1, replica_groups=mesh['gx'=32,'gy'=8] {'gx','gy'}, use_global_device_ids=true, to_apply=%region_17.18 | all-reduce | flops 1 | bytes 8 | tf_op jit(solution)/shard_map/psum | solution.py:270
  876.9 78.5 %psum.121 = f32[]{:T(128)} all-reduce(f32[]{:T(128)} %get-tuple-element.21), channel_id=1, replica_groups=mesh['gx'=32,'gy'=8] {'gx','gy'}, use_global_device_ids=true, to_apply=%region_19.20 | all-reduce | flops 1 | bytes 8 | tf_op jit(solution)/shard_map/psum | solution.py:274
  957.3 72.4 %psum.122 = f32[]{:T(128)} all-reduce(f32[]{:T(128)} %get-tuple-element.19), channel_id=1, replica_groups=mesh['gx'=32,'gy'=8] {'gx','gy'}, use_global_device_ids=true, to_apply=%region_21.22 | all-reduce | flops 1 | bytes 8 | tf_op jit(solution)/shard_map/psum | solution.py:270
  1044.8 78.1 %psum.123 = f32[]{:T(128)} all-reduce(f32[]{:T(128)} %get-tuple-element.17), channel_id=1, replica_groups=mesh['gx'=32,'gy'=8] {'gx','gy'}, use_global_device_ids=true, to_apply=%region_23.24 | all-reduce | flops 1 | bytes 8 | tf_op jit(solution)/shard_map/psum | solution.py:274
  1125.0 72.5 %psum.124 = f32[]{:T(128)} all-reduce(f32[]{:T(128)} %get-tuple-element.15), channel_id=1, replica_groups=mesh['gx'=32,'gy'=8] {'gx','gy'}, use_global_device_ids=true, to_apply=%region_25.26 | all-reduce | flops 1 | bytes 8 | tf_op jit(solution)/shard_map/psum | solution.py:270
  1212.4 78.2 %psum.125 = f32[]{:T(128)} all-reduce(f32[]{:T(128)} %get-tuple-element.13), channel_id=1, replica_groups=mesh['gx'=32,'gy'=8] {'gx','gy'}, use_global_device_ids=true, to_apply=%region_27.28 | all-reduce | flops 1 | bytes 8 | tf_op jit(solution)/shard_map/psum | solution.py:274
  1292.7 72.4 %psum.126 = f32[]{:T(128)} all-reduce(f32[]{:T(128)} %multiply_reduce_fusion.1), channel_id=1, replica_groups=mesh['gx'=32,'gy'=8] {'gx','gy'}, use_global_device_ids=true, to_apply=%region_29.30 | all-reduce | flops 1 | bytes 8 | tf_op jit(solution)/shard_map/psum | solution.py:270
  1380.8 78.3 %psum.127 = f32[]{:T(128)} all-reduce(f32[]{:T(128)} %multiply_reduce_fusion), channel_id=1, replica_groups=mesh['gx'=32,'gy'=8] {'gx','gy'}, use_global_device_ids=true, to_apply=%region_31.32 | all-reduce | flops 1 | bytes 8 | tf_op jit(solution)/shard_map/psum | solution.py:274
  1474.9 5.1 collective-permute-start.81
  1487.8 5.4 collective-permute-start.85
  1508.6 5.4 collective-permute-start.89
  1524.1 5.3 collective-permute-start.93
  1531.3 5.2 collective-permute-start.95
  1541.4 5.4 collective-permute-start.97
  1548.0 6.1 collective-permute-start.99
  (713 shorter events, 307.3 us)
Async XLA Ops:
  4.3 29.9 %collective-permute-start.4 = (f32[16,1,256]{2,1,0:T(1,128)S(1)}, f32[16,1,256]{2,1,0:T(1,128)S(1)}, u32[]{:S(2)}, u32[]{:S(2)}) collective-permute-start(f32[16,1,256]{2,1,0:T(1,128)S(1)} %get-tuple-element.88), channel_id=1, source_target_pairs={{0,8},{8,16},{16,24},{24,32},{32,40},{40,48},{48,56},{56,64},{64,7... | collective-permute-start | bytes 49160 | tf_op jit(solution)/shard_map/ppermute | solution.py:28
  6.8 32.2 %collective-permute-start.5 = (f32[16,1,256]{2,1,0:T(1,128)S(1)}, f32[16,1,256]{2,1,0:T(1,128)S(1)}, u32[]{:S(2)}, u32[]{:S(2)}) collective-permute-start(f32[16,1,256]{2,1,0:T(1,128)S(1)} %get-tuple-element.89), channel_id=1, source_target_pairs={{8,0},{16,8},{24,16},{32,24},{40,32},{48,40},{56,48},{64,56},{72,6... | collective-permute-start | bytes 49160 | tf_op jit(solution)/shard_map/ppermute | solution.py:30
  13.3 29.1 %collective-permute-start = (f32[16,1,256]{2,1,0:T(1,128)S(1)}, f32[16,1,256]{2,1,0:T(1,128)S(1)}, u32[]{:S(2)}, u32[]{:S(2)}) collective-permute-start(f32[16,1,256]{2,1,0:T(1,128)S(1)} %get-tuple-element.84), channel_id=1, source_target_pairs={{0,8},{8,16},{16,24},{24,32},{32,40},{40,48},{48,56},{56,64},{64,7... | collective-permute-start | bytes 49160 | tf_op jit(solution)/shard_map/ppermute | solution.py:28
  13.4 29.0 %collective-permute-start.1 = (f32[16,1,256]{2,1,0:T(1,128)S(1)}, f32[16,1,256]{2,1,0:T(1,128)S(1)}, u32[]{:S(2)}, u32[]{:S(2)}) collective-permute-start(f32[16,1,256]{2,1,0:T(1,128)S(1)} %get-tuple-element.85), channel_id=1, source_target_pairs={{8,0},{16,8},{24,16},{32,24},{40,32},{48,40},{56,48},{64,56},{72,6... | collective-permute-start | bytes 49160 | tf_op jit(solution)/shard_map/ppermute | solution.py:30
  22.0 82.4 %collective-permute-start.16 = (f32[8,1,128]{2,1,0:T(1,128)}, f32[8,1,128]{2,1,0:T(1,128)}, u32[]{:S(2)}, u32[]{:S(2)}) collective-permute-start(f32[8,1,128]{2,1,0:T(1,128)} %get-tuple-element.132), channel_id=1, source_target_pairs={{0,8},{8,16},{16,24},{24,32},{32,40},{40,48},{48,56},{56,64},{64,7... | collective-permute-start | bytes 12296 | tf_op jit(solution)/shard_map/ppermute | solution.py:28
  34.1 70.2 %collective-permute-start.17 = (f32[8,1,128]{2,1,0:T(1,128)}, f32[8,1,128]{2,1,0:T(1,128)}, u32[]{:S(2)}, u32[]{:S(2)}) collective-permute-start(f32[8,1,128]{2,1,0:T(1,128)} %get-tuple-element.133), channel_id=1, source_target_pairs={{8,0},{16,8},{24,16},{32,24},{40,32},{48,40},{56,48},{64,56},{72,6... | collective-permute-start | bytes 12296 | tf_op jit(solution)/shard_map/ppermute | solution.py:30
  71.4 6.5 collective-permute-start.12
  71.5 6.4 collective-permute-start.13
  88.6 12.3 collective-permute-start.20
  88.6 12.3 collective-permute-start.21
  110.3 9.2 collective-permute-start.24
  110.3 9.2 collective-permute-start.25
  115.2 7.4 collective-permute-start.18
  115.7 6.8 collective-permute-start.19
  131.6 6.2 collective-permute-start.30
  139.7 6.3 collective-permute-start.32
  153.6 6.2 collective-permute-start.36
  161.0 7.9 collective-permute-start.38
  161.1 7.9 collective-permute-start.39
  175.0 6.2 collective-permute-start.40
  1487.7 6.2 collective-permute-start.84
  1487.8 6.2 collective-permute-start.85
  1494.7 7.1 collective-permute-start.86
  1495.4 6.4 collective-permute-start.87
  1508.4 6.5 collective-permute-start.88
  1508.6 6.4 collective-permute-start.89
  1530.4 7.0 collective-permute-start.94
  1531.3 6.3 collective-permute-start.95
  1541.3 6.5 collective-permute-start.96
  1541.4 6.4 collective-permute-start.97
  1548.0 7.0 collective-permute-start.98
  1548.0 7.2 collective-permute-start.99
  (120 other events, 5275.6 us)
where the time goes:
time: 1570 us; the launch traced here: 1560 us
  blocking collectives  1140 us (73%)
  starting transfers between devices  217 us (14%)
  waiting for transfers between devices  61.8 us (4%)
  other arithmetic  48.2 us (3%)
  matrix products  40.8 us (3%)
  local copies, waits for them, and re-layouts  30 us (2%)
  between operations  23.1 us (1%)
    psum x8, blocking collectives, weighted_norm(): lax.psum(jnp.sum(apply_share(residual * residual, level)), ('gx', 'gy'))  589 us
    psum x7, blocking collectives, weighted_curvature(): lax.psum(jnp.sum(apply_share(direction * image, level)), ('gx', 'gy'))  548 us
    ppermute x50, starting transfers between devices, with_halo(): lax.ppermute(head, axis, [((i + 1) % count, i) for i in range(count)])  174 us
    ppermute x50, starting transfers between devices, with_halo(): lax.ppermute(tail, axis, [(i, (i + 1) % count) for i in range(count)])  42.9 us
  transfers between devices with their start and end apart: 100, of which 60 were waited for; matrix products, arithmetic and copies ran while one was open for 3% of the time, Pallas kernels for 0%

commit v1 on v0

v1 whole, which is shorter than its diff:
```python
import math

import jax
import jax.numpy as jnp
import ml_dtypes
import numpy as np
from jax import lax
from jax.experimental import pallas as pl
from jax.experimental.pallas import tpu as pltpu
from jax.sharding import PartitionSpec as P

CG_ITERS = 8
mass_coef = 0.000125
cheb_ratio = 0.1
f32 = jnp.float32
bf16 = jnp.bfloat16
MB = 1024 * 1024


def legendre_pair(points, order):
    previous = 0.0 * points + 1.0
    current = points * 1.0
    for degree in range(2, order + 1):
        previous, current = (
            current,
            ((2.0 * degree - 1.0) * points * current - (degree - 1.0) * previous) / degree,
        )
    return (previous, current)


def gll_tables(order):
    count_nodes = order + 1
    points = -np.cos(math.pi * np.arange(count_nodes) / order)
    for sweep in range(60):
        previous, values_at = legendre_pair(points, order)
        points = points - (points * values_at - previous) / (count_nodes * values_at)
    previous, values_at = legendre_pair(points, order)
    weights = 2.0 / (order * (order + 1) * values_at * values_at)
    spacing = points[:, None] - points[None, :]
    safe_spacing = np.where(spacing == 0.0, 1.0, spacing)
    derivative = values_at[:, None] / (values_at[None, :] * safe_spacing)
    derivative = derivative * (1.0 - np.eye(count_nodes))
    corner_value = order * (order + 1) / 4.0
    end_values = np.concatenate(
        [np.array([-corner_value]), np.zeros(count_nodes - 2), np.array([corner_value])]
    )
    return (points, weights, derivative + np.eye(count_nodes) * end_values[None, :])


def interp_table(fine_order, coarse_order):
    fine_points = gll_tables(fine_order)[0]
    coarse_points = gll_tables(coarse_order)[0]
    numer = fine_points[:, None, None] - coarse_points[None, None, :]
    denom = coarse_points[None, :, None] - coarse_points[None, None, :]
    same_node = np.eye(len(coarse_points))[None, :, :] > 0.5
    ratio = np.where(same_node, 1.0, numer / np.where(same_node, 1.0, denom))
    return ratio.prod(axis=2)


def element_bound(order):
    points, weights, derivative = gll_tables(order)
    mass = np.eye(order + 1) * weights[None, :]
    stiff = np.dot(derivative.T, np.dot(mass, derivative))
    full = 0.5 * (
        np.kron(np.kron(mass, mass), stiff)
        + np.kron(np.kron(mass, stiff), mass)
        + np.kron(np.kron(stiff, mass), mass)
    ) + mass_coef * np.kron(np.kron(mass, mass), mass)
    diagonal_entries = np.sum(full * np.eye(full.shape[0]), axis=1)
    ratio = np.abs(full).sum(axis=1) / diagonal_entries
    return float(ratio.max())


def sum_matrix(elements, n, cyclic):
    out = np.eye(elements * n)
    for e in range(elements):
        if cyclic or e + 1 < elements:
            a, b = e * n + n - 1, ((e + 1) % elements) * n
            out[a, b] += 1.0
            out[b, a] += 1.0
    return out


def blocks(matrix, count):
    return np.kron(np.eye(count), matrix)


class Level:
    def __init__(self, order):
        n = self.n = order + 1
        _, w, dm = gll_tables(order)
        self.w = w
        self.k = dm.T @ np.diag(w) @ dm
        self.sum_z = sum_matrix(2, n, False)
        self.k_z = self.sum_z @ blocks(self.k, 2)
        self.w_z = self.sum_z @ np.tile(w, 2)
        self.w_p = w.copy()
        self.w_p[0] += w[-1]
        self.w_p[-1] += w[0]
        kd = np.diag(self.k).copy()
        kd_p = kd.copy()
        kd_p[0] += kd[-1]
        kd_p[-1] += kd[0]
        kd_z = self.sum_z @ np.tile(kd, 2)
        wz, wp = self.w_z, self.w_p
        diag = 0.5 * (
            np.einsum("z,r,c->zrc", wz, kd_p, wp)
            + np.einsum("z,r,c->zrc", wz, wp, kd_p)
            + np.einsum("z,r,c->zrc", kd_z, wp, wp)
        ) + mass_coef * np.einsum("z,r,c->zrc", wz, wp, wp)
        self.dinv = 1.0 / diag
        upper = element_bound(order)
        lower = cheb_ratio * upper
        center, half = 0.5 * (upper + lower), 0.5 * (upper - lower)
        sigma = center / half
        rho = 1.0 / sigma
        self.first = 1.0 / center
        self.steps = []
        for _ in range(2):
            rho2 = 1.0 / (2.0 * sigma - rho)
            self.steps.append((float(rho2 * rho), 2.0 * rho2 / half))
            rho = rho2
        self.m_p = np.ones(n)
        self.m_p[0] = self.m_p[-1] = 0.5
        self.m_z = np.ones(2 * n)
        self.m_z[n - 1] = self.m_z[n] = 0.5


def hi_lo(matrix):
    matrix = np.asarray(matrix, np.float64)
    hi = matrix.astype(ml_dtypes.bfloat16)
    lo = (matrix - hi.astype(np.float64)).astype(ml_dtypes.bfloat16)
    return hi, lo


def packed_left(matrix):
    hi, lo = hi_lo(matrix)
    return np.block([[hi, hi], [lo, np.zeros_like(lo)]])


def packed_right(matrix):
    hi, lo = hi_lo(matrix)
    return np.block([[hi, lo], [hi, np.zeros_like(lo)]])


FINE, MID, COARSE = Level(7), Level(3), Level(1)
J_FINE, J_MID = interp_table(7, 3), interp_table(3, 1)


def pattern(level, lanes):
    d = level.dinv.reshape(2 * level.n * level.n, level.n)
    return np.tile(d, (1, lanes // level.n))


def fine_constants():
    n = 8
    m1 = (
        0.5 * (np.kron(FINE.k_z, np.diag(FINE.w)) + np.kron(np.diag(FINE.w_z), FINE.k))
        + mass_coef * np.kron(np.diag(FINE.w_z), np.diag(FINE.w))
    )
    dinv = pattern(FINE, 128)
    return dict(
        m1=packed_left(m1),
        kc=packed_right(blocks(FINE.k, 16).T),
        wc=np.tile(FINE.w_p, 16)[None, :].astype(np.float32),
        cf=np.repeat(0.5 * np.kron(FINE.w_z, FINE.w_p)[:, None], 128, axis=1).astype(np.float32),
        d1=(FINE.first * dinv).astype(np.float32),
        d2=(FINE.steps[0][1] * dinv).astype(np.float32),
        d3=(FINE.steps[1][1] * dinv).astype(np.float32),
    )


def mid_operator(rows):
    n = 4
    s = sum_matrix(rows, n, False)
    k_r = s @ blocks(MID.k, rows)
    w_r = np.tile(MID.w_p, rows)
    k_r, w_r = k_r.reshape(rows, n, rows, n), np.diag(w_r).reshape(rows, n, rows, n)
    kz, wz = MID.k_z, np.diag(MID.w_z)
    t = (
        0.5 * np.einsum("zy,eafb->ezafyb", kz, w_r)
        + 0.5 * np.einsum("zy,eafb->ezafyb", wz, k_r)
        + mass_coef * np.einsum("zy,eafb->ezafyb", wz, w_r)
    )
    return t.reshape(rows * 32, rows * 32)


def mid_sum(rows):
    s = sum_matrix(rows, 4, False).reshape(rows, 4, rows, 4)
    return np.einsum("zy,eafb->ezafyb", MID.sum_z, s).reshape(rows * 32, rows * 32)


def mid_constants(rows):
    dinv = np.tile(pattern(MID, 256), (rows, 1))
    kc = sum_matrix(64, 4, True) @ blocks(MID.k, 64)
    kh, kl = hi_lo(kc.T)
    return dict(
        kh=kh,
        kl=kl,
        wc=np.tile(MID.w_p, 64)[None, :].astype(np.float32),
        cf=np.tile(
            np.repeat(0.5 * np.kron(MID.w_z, MID.w_p)[:, None], 256, axis=1), (rows, 1)
        ).astype(np.float32),
        d1=(MID.first * dinv).astype(np.float32),
        d2=(MID.steps[0][1] * dinv).astype(np.float32),
        d3=(MID.steps[1][1] * dinv).astype(np.float32),
    )


def dot(a, b):
    return jnp.dot(a, b, preferred_element_type=f32)


def split(u):
    h = u.astype(bf16)
    return h, (u - h.astype(f32)).astype(bf16)


def dot_left(ch, cl, u):
    h, l = split(u)
    return dot(ch, h) + dot(ch, l) + dot(cl, h)


def dot_right(u, ch, cl):
    h, l = split(u)
    return dot(h, ch) + dot(l, ch) + dot(h, cl)


def wide(tile):
    return jnp.concatenate([tile, tile, tile], axis=-1)


def row_sum(before, here, after):
    lanes = here.shape[-1]
    cube = (16, 8, lanes)
    node = lax.broadcasted_iota(jnp.int32, cube, 1)
    b = pltpu.roll(before.reshape(cube), 1, 1)
    a = pltpu.roll(after.reshape(cube), 7, 1)
    out = here.reshape(cube) + jnp.where(node == 0, b, 0.0) + jnp.where(node == 7, a, 0.0)
    return out.reshape(128, lanes)


def col_sum(y):
    lanes = y.shape[-1]
    node = lax.broadcasted_iota(jnp.int32, y.shape, 1) % 8
    b = pltpu.roll(y, 1, 1)
    a = pltpu.roll(y, lanes - 1, 1)
    return y + jnp.where(node == 0, b, 0.0) + jnp.where(node == 7, a, 0.0)


def fine_apply(us, c):
    parts = [split(u) for u in us]
    m1 = c["m1"][...]
    t = []
    for h, l in parts:
        y = dot(m1, jnp.concatenate([h, l], axis=0))
        t.append(y[:128] + y[128:])
    kc = c["kc"][...]
    wc, cf = wide(c["wc"][...]), wide(c["cf"][...])
    out = []
    for e in range(1, len(us) - 1):
        h, l = parts[e]
        y = []
        for k in range(3):
            s = slice(128 * k, 128 * k + 128)
            z = dot(jnp.concatenate([h[:, s], l[:, s]], axis=1), kc)
            y.append(z[:, :128] + z[:, 128:])
        y = col_sum(jnp.concatenate(y, axis=1))
        out.append(wc * row_sum(t[e - 1], t[e], t[e + 1]) + cf * y)
    return out


def mid_apply(m_h, m_l, u, lo, hi, c):
    h, l = split(u)
    t = dot(m_h, h) + dot(m_h, l) + dot(m_l, h)
    kh, kl = c["kh"][...], c["kl"][...]
    y = dot(h[lo:hi], kh) + dot(l[lo:hi], kh) + dot(h[lo:hi], kl)
    return c["wc"][...] * t + c["cf"][: hi - lo] * y


def call(body, outs, consts, args, vmem=40 * MB):
    names = sorted(consts)

    def kernel(*refs):
        c = dict(zip(names, refs[: len(names)]))
        ins = refs[len(names) : len(names) + len(args)]
        body(c, ins, refs[len(names) + len(args) :])

    spec = pl.BlockSpec(memory_space=pltpu.VMEM)
    return pl.pallas_call(
        kernel,
        out_shape=[jax.ShapeDtypeStruct(s, f32) for s in outs],
        in_specs=[spec] * (len(names) + len(args)),
        out_specs=[spec] * len(outs),
        compiler_params=pltpu.CompilerParams(vmem_limit_bytes=vmem),
    )(*[jnp.asarray(consts[k]) for k in names], *args)


def restrict_rows(level, table, rows):
    z = blocks(table.T, 2) @ np.diag(level.m_z)
    r = table.T @ np.diag(level.m_p)
    return blocks(np.kron(z, r), rows)


def pre_fine(blk, p1, m1, p2, m2):
    consts = fine_constants()
    consts["w"] = np.repeat(0.125 * np.kron(np.tile(FINE.w, 2), FINE.w)[:, None], 128, axis=1).astype(
        np.float32
    ) * np.tile(FINE.w, 16)[None, :].astype(np.float32)
    consts["rh"], consts["rl"] = hi_lo(restrict_rows(FINE, J_FINE, 2))
    consts["ch"], consts["cl"] = hi_lo(blocks(J_FINE.T @ np.diag(FINE.m_p), 32).T)

    def body(c, ins, outs):
        blk, p1, m1, p2, m2 = ins
        w = wide(c["w"][...])
        src = [m2[:128], m1[0], m1[1], blk[0], blk[1], p1[0], p1[1], p2[:128]]
        src = [w * s for s in src]
        lanes = 384
        node = lax.broadcasted_iota(jnp.int32, (16, 8, lanes), 1)
        w_end = w.reshape(16, 8, lanes)[:, 0:1, :]
        low = jnp.broadcast_to(m2[128:].reshape(16, 1, lanes) * w_end, (16, 8, lanes))
        top = jnp.broadcast_to(p2[128:].reshape(16, 1, lanes) * w_end, (16, 8, lanes))
        src = [low.reshape(128, lanes)] + src + [top.reshape(128, lanes)]
        b = []
        for e in range(1, 9):
            y = col_sum(row_sum(src[e - 1], src[e], src[e + 1]))
            mid = y[56:64] + y[64:72]
            b.append(jnp.concatenate([y[:56], mid, mid, y[72:]], axis=0))
        d1, d2, d3 = wide(c["d1"][...]), wide(c["d2"][...]), wide(c["d3"][...])
        d = [d1 * v for v in b]
        x = [d[3], d[4]]
        g = fine_apply(d, c)
        r = [v - a for v, a in zip(b[1:-1], g)]
        d = [FINE.steps[0][0] * v + d2 * a for v, a in zip(d[1:-1], r)]
        x = [x[0] + d[2], x[1] + d[3]]
        g = fine_apply(d, c)
        r = [v - a for v, a in zip(r[1:-1], g)]
        d = [FINE.steps[1][0] * v + d3 * a for v, a in zip(d[1:-1], r)]
        x = [x[0] + d[1], x[1] + d[2]]
        g = fine_apply(d, c)
        r = [v - a for v, a in zip(r[1:-1], g)]
        x0, r0, rhs = outs
        for e in range(2):
            x0[e] = x[e][:, :256]
            r0[e] = r[e]
        own = jnp.concatenate([r[0][:, :256], r[1][:, :256]], axis=0)
        rows = dot_left(c["rh"][...], c["rl"][...], own)
        rhs[...] = dot_right(rows, c["ch"][...], c["cl"][...])

    return call(
        body,
        [(2, 128, 256), (2, 128, 384), (64, 128)],
        consts,
        (blk, p1, m1, p2, m2),
    )


def pre_mid(blk, p1, m1, p2, m2):
    consts = mid_constants(8)
    consts["mh"], consts["ml"] = hi_lo(mid_operator(8))
    consts["sh"] = mid_sum(10)[32:-32].astype(ml_dtypes.bfloat16)
    consts["sc"] = sum_matrix(64, 4, True).T.astype(ml_dtypes.bfloat16)
    z = np.zeros((3, 8))
    zz = blocks(J_MID.T, 2) @ np.diag(MID.m_z)
    z[0], z[1], z[2] = zz[0], zz[1] + zz[2], zz[3]
    r1 = J_MID.T @ np.diag(MID.m_p)
    rr = np.zeros((2, 8, 4, 2, 8, 4))[:, 0, 0]
    rdr = np.zeros((4, 4, 2, 8, 4))
    for e in range(2):
        for k in range(2):
            rdr[e + k, :3, e] += np.einsum("zy,b->zyb", z, r1[k])
    consts["rh"], consts["rl"] = hi_lo(rdr.reshape(16, 64))
    rc = np.zeros((256, 32))
    for v in range(32):
        rc[4 * v : 4 * v + 4, v] += r1[0]
        left = (4 * v - 4) % 256
        rc[left : left + 4, v] += r1[1]
    consts["ch"], consts["cl"] = hi_lo(np.tile(rc, (1, 12)))

    def body(c, ins, outs):
        blk, p1, m1, p2, m2 = ins
        u = jnp.concatenate([m2[...], m1[...], blk[...], p1[...], p2[...]], axis=0)
        h, l = split(u)
        sh, sc = c["sh"][...], c["sc"][...]
        u = dot(sh, h) + dot(sh, l)
        h, l = split(u)
        b = dot(h, sc) + dot(l, sc)
        mh, ml = c["mh"][...], c["ml"][...]
        d = c["d1"][...] * b
        x = d
        r = b - mid_apply(mh, ml, d, 0, 256, c)
        d = MID.steps[0][0] * d + c["d2"][...] * r
        x = x + d
        r = r - mid_apply(mh, ml, d, 0, 256, c)
        d = MID.steps[1][0] * d + c["d3"][...] * r
        x = x + d
        r = r - mid_apply(mh, ml, d, 0, 256, c)
        x1, r1, chunk = outs
        x1[...] = x[64:192]
        own = r[96:160]
        r1[...] = own
        rows = dot_left(c["rh"][...], c["rl"][...], own)
        t = dot_right(rows, c["ch"][...], c["cl"][...])
        q = lax.broadcasted_iota(jnp.int32, t.shape, 0)
        lane = lax.broadcasted_iota(jnp.int32, t.shape, 1) // 32
        t = jnp.sum(jnp.where(q == lane, t, 0.0), axis=0, keepdims=True)
        chunk[...] = jnp.broadcast_to(t, chunk.shape)

    return call(
        body,
        [(128, 256), (64, 256), (256, 384)],
        consts,
        (blk, p1, m1, p2, m2),
    )


def coarse_solve(gathered):
    kz = np.zeros((4, 4))
    kz[:3, :3] = [[0.5, -0.5, 0.0], [-0.5, 1.0, -0.5], [0.0, -0.5, 0.5]]
    wz = np.array([1.0, 2.0, 1.0, 0.0])
    near = np.eye(32, k=1) + np.eye(32, k=-1)
    inner = 2.0 * np.kron(kz, np.eye(32)) + np.kron(np.diag(wz), 2.0 * np.eye(32) - 0.5 * near)
    up, down = np.zeros((32, 32)), np.zeros((32, 32))
    up[0, 31] = -0.5
    down[31, 0] = -0.5
    matrix = np.concatenate([inner, np.kron(np.diag(wz), up), np.kron(np.diag(wz), down)], axis=0)
    consts = dict(
        m=matrix.astype(ml_dtypes.bfloat16),
        wz=np.repeat(wz, 32)[None, :].astype(np.float32),
    )

    def body(c, ins, outs):
        (g,) = ins
        (x_out,) = outs
        m, wz = c["m"][...], c["wz"][...]

        def after(u):
            return jnp.concatenate([u[8:], u[:8]], axis=0)

        def before(u):
            return jnp.concatenate([u[-8:], u[:-8]], axis=0)

        def shifted(u, by):
            return pltpu.roll(u.reshape(32, 8, 128), by, 1).reshape(256, 128)

        def columns(u):
            a = u.astype(bf16)
            rest = u - a.astype(f32)
            b = rest.astype(bf16)
            e = (rest - b.astype(f32)).astype(bf16)
            t = None
            for part in (a, b, e):
                wide_part = part.astype(f32)
                v = dot(
                    jnp.concatenate(
                        [
                            part,
                            shifted(wide_part, 7).astype(bf16),
                            shifted(wide_part, 1).astype(bf16),
                        ],
                        axis=1,
                    ),
                    m,
                )
                t = v if t is None else t + v
            return t

        half = -0.5 * wz
        mass = 4.0 * mass_coef * wz

        def apply(p):
            p0, p1 = p
            return (
                columns(p0) + half * (p1 + before(p1)) + mass * p0,
                columns(p1) + half * (p0 + after(p0)) + mass * p1,
            )

        def inner_product(a, b):
            s = jnp.sum(a[0] * b[0] + a[1] * b[1], axis=0, keepdims=True)
            return jnp.sum(s, axis=1, keepdims=True)

        r = (g[:, 0:128] + before(g[:, 256:384]), g[:, 128:256])
        p = r
        x = (jnp.zeros_like(r[0]), jnp.zeros_like(r[1]))
        norm = inner_product(r, r)
        for it in range(CG_ITERS):
            q = apply(p)
            alpha = norm / inner_product(p, q)
            x = tuple(a + alpha * b for a, b in zip(x, p))
            if it + 1 < CG_ITERS:
                r = tuple(a - alpha * b for a, b in zip(r, q))
                new = inner_product(r, r)
                beta = new / norm
                p = tuple(a + beta * b for a, b in zip(r, p))
                norm = new
        x_out[:, 0:128] = x[0]
        x_out[:, 128:256] = x[1]

    return call(body, [(256, 256)], consts, (gathered,))[0]


def post(x2, mid_x, mid_r, fine_x, fine_r):
    consts = {"f_" + k: v for k, v in fine_constants().items()}
    consts.update({"m_" + k: v for k, v in mid_constants(12).items()})
    mh, ml = hi_lo(mid_operator(14)[32:-32])
    consts["m_mh"], consts["m_ml"] = mh, ml
    jc = np.zeros((3, 3, 4, 32, 256))
    for e in range(64):
        element = e if e < 48 else e - 64
        for k in range(2):
            v = element + k
            dev, col = v // 32 + 1, v % 32
            for z in range(3):
                jc[z, dev, z, col, 4 * e : 4 * e + 4] = J_MID[:, k]
    jc = jc.reshape(3, 384, 256)
    jc = np.concatenate([jc[0], jc[1], jc[2]], axis=1)
    consts["vch"], consts["vcl"] = hi_lo(jc)
    jz = np.zeros((8, 3))
    jz[:4, :2] += J_MID
    jz[4:, 1:] += J_MID
    jdr = np.zeros((14, 8, 4, 3, 16))
    for e in range(14):
        for k in range(2):
            jdr[e, :, :, :, e + k] += np.einsum("zp,a->zap", jz, J_MID[:, k])
    consts["vdh"], consts["vdl"] = hi_lo(jdr.reshape(448, 48))
    fc = np.zeros((256, 384))
    for e in range(48):
        src = e if e < 40 else e + 16
        fc[4 * src : 4 * src + 4, 8 * e : 8 * e + 8] = J_FINE.T
    consts["fch"], consts["fcl"] = hi_lo(fc)
    consts["fdh"], consts["fdl"] = hi_lo(np.kron(blocks(J_FINE, 2), J_FINE))

    def body(c, ins, outs):
        x2, mid_x, mid_r, fine_x, fine_r = ins[:5]
        out, twice, rows = outs[0], outs[1], outs[2]
        i, j = lax.axis_index("gx"), lax.axis_index("gy")
        f = {k[2:]: v for k, v in c.items() if k.startswith("f_")}
        m = {k[2:]: v for k, v in c.items() if k.startswith("m_")}
        twice[0:256] = x2[...]
        twice[256:512] = x2[...]
        first = lax.rem(i + 29, 32)
        picked = twice[pl.ds(pl.multiple_of(first * 8, 8), 64), :].reshape(8, 8, 256)
        sub = lax.broadcasted_iota(jnp.int32, (8, 8, 256), 1)
        for d in range(3):
            own = lax.rem(j + 7 + d, 8)
            v = jnp.sum(jnp.where(sub == own, picked, 0.0), axis=1)
            for k in range(2):
                rows[8 * k : 8 * k + 8, 128 * d : 128 * d + 128] = v[:, 128 * k : 128 * k + 128]
        y = dot_right(rows[...], c["vch"][...], c["vcl"][...])
        y = jnp.concatenate([y[:, :256], y[:, 256:512], y[:, 512:]], axis=0)
        e2 = dot_left(c["vdh"][...], c["vdl"][...], y)
        mh, ml = c["m_mh"], c["m_ml"]
        r = mid_r[...] - mid_apply(mh[...], ml[...], e2, 32, 416, m)
        d = m["d1"][...] * r
        x = mid_x[...] + e2[96:352] + d[64:320]
        r = r[32:352] - mid_apply(mh[:320, :384], ml[:320, :384], d, 32, 352, m)
        d = MID.steps[0][0] * d[32:352] + m["d2"][:320] * r
        x = x + d[32:288]
        r = r[32:288] - mid_apply(mh[:256, :320], ml[:256, :320], d, 32, 288, m)
        d = MID.steps[1][0] * d[32:288] + m["d3"][:256] * r
        x = x + d
        x = dot_right(x, c["fch"][...], c["fcl"][...])
        fdh, fdl = c["fdh"][...], c["fdl"][...]
        e1 = [dot_left(fdh, fdl, x[32 * e : 32 * e + 32]) for e in range(8)]
        g = fine_apply(e1, f)
        r = [fine_r[e] - g[e] for e in range(6)]
        d1, d2, d3 = wide(f["d1"][...]), wide(f["d2"][...]), wide(f["d3"][...])
        d = [d1 * v for v in r]
        x = [fine_x[e] + (e1[3 + e] + d[2 + e])[:, :256] for e in range(2)]
        g = fine_apply(d, f)
        r = [v - a for v, a in zip(r[1:-1], g)]
        d = [FINE.steps[0][0] * v + d2 * a for v, a in zip(d[1:-1], r)]
        x = [x[e] + d[1 + e][:, :256] for e in range(2)]
        g = fine_apply(d, f)
        r = [v - a for v, a in zip(r[1:-1], g)]
        d = [FINE.steps[1][0] * v + d3 * a for v, a in zip(d[1:-1], r)]
        for e in range(2):
            v = (x[e] + d[e][:, :256]).reshape(16, 8, 256)
            out[:, 8 * e : 8 * e + 8, :] = v

    order = [2 * (q % 8) + q // 8 for q in range(16)]
    for name in ("vdh", "vdl"):
        t = consts[name].reshape(448, 3, 16)
        consts[name] = np.ascontiguousarray(t[:, :, order]).reshape(448, 48)

    names = sorted(consts)
    args = (x2, mid_x, mid_r, fine_x, fine_r)

    def kernel(*refs):
        body(
            dict(zip(names, refs[: len(names)])),
            refs[len(names) : len(names) + len(args)],
            refs[len(names) + len(args) :],
        )

    spec = pl.BlockSpec(memory_space=pltpu.VMEM)
    return pl.pallas_call(
        kernel,
        out_shape=jax.ShapeDtypeStruct((16, 16, 256), f32),
        in_specs=[spec] * (len(names) + len(args)),
        out_specs=spec,
        scratch_shapes=[pltpu.VMEM((512, 256), f32), pltpu.VMEM((16, 384), f32)],
        compiler_params=pltpu.CompilerParams(vmem_limit_bytes=48 * MB),
    )(*[jnp.asarray(consts[k]) for k in names], *args)


def fetch(value, axis, offset):
    count = lax.axis_size(axis)
    return lax.ppermute(value, axis, [((i + offset) % count, i) for i in range(count)])


def with_columns(low, high):
    right = fetch(low, "gy", 1)
    left = fetch(high, "gy", -1)
    lane = lax.broadcasted_iota(jnp.int32, right.shape, right.ndim - 1)
    return jnp.where(lane < 64, right, left)


def local(source):
    s = source.reshape(16, 2, 8, 256).transpose(1, 0, 2, 3).reshape(2, 128, 256)
    blk = jnp.concatenate([s, with_columns(s[:, :, :128], s[:, :, 128:])], axis=2)
    faces = blk.reshape(2, 16, 8, 384)
    up = jnp.concatenate([blk[0], faces[1, :, 0]], axis=0)
    down = jnp.concatenate([blk[1], faces[0, :, 7]], axis=0)
    p1, m1 = fetch(blk, "gx", 1), fetch(blk, "gx", -1)
    p2, m2 = fetch(up, "gx", 2), fetch(down, "gx", -2)
    x0, r0, rhs = pre_fine(blk, p1, m1, p2, m2)

    blk = jnp.concatenate([rhs, with_columns(rhs, rhs)], axis=1)
    p1, m1 = fetch(blk, "gx", 1), fetch(blk, "gx", -1)
    p2, m2 = fetch(blk, "gx", 2), fetch(blk, "gx", -2)
    x1, r1, chunk = pre_mid(blk, p1, m1, p2, m2)

    gathered = lax.all_to_all(chunk, ("gx", "gy"), 0, 0, tiled=True)
    r0p, r0m = fetch(r0, "gx", 1), fetch(r0, "gx", -1)
    fine_r = jnp.concatenate([r0m, r0, r0p], axis=0)
    both = jnp.concatenate([r1, x1[32:]], axis=0)
    bothm = jnp.concatenate([r1, x1[:96]], axis=0)
    fp, fm = fetch(both, "gx", 1), fetch(bothm, "gx", -1)
    r2p, r2m = fetch(r1, "gx", 2), fetch(r1, "gx", -2)
    r3p, r3m = fetch(r1[:32], "gx", 3), fetch(r1[32:], "gx", -3)
    mid_r = jnp.concatenate([r3m, r2m, fm[:64], r1, fp[:64], r2p, r3p], axis=0)
    mid_x = jnp.concatenate([fm[64 : 64 + 96], x1[32:96], fp[64 : 64 + 96]], axis=0)
    x2 = coarse_solve(gathered)
    return post(x2, mid_x, mid_r, x0, fine_r)


def solution(mesh):
    return jax.shard_map(
        local,
        mesh=mesh,
        in_specs=(P(None, "gx", "gy"),),
        out_specs=P(None, "gx", "gy"),
        check_vma=False,
    )
```

time: 1570 us -> 138 us (0.09)
  blocking collectives: 1140 us -> 0 us
  starting transfers between devices: 217 us -> 68.9 us
  other arithmetic: 48.2 us -> 2.49 us
  matrix products: 40.8 us -> 0 us
  waiting for transfers between devices: 61.8 us -> 28.8 us
  between operations: 23.1 us -> 0.81 us
  Pallas kernels: 0 us -> 20.2 us
    psum x15 -> x0, blocking collectives: 1140 us -> none  [the longest x8 589 us: weighted_norm(): lax.psum(jnp.sum(apply_share(residual * residual, level)), ('gx', 'gy'))]
    ppermute x100 -> x20, starting transfers between devices: 217 us -> 53.1 us  [fetch(): lax.ppermute(value, axis, [((i + offset) % count, i) for i in range(count)])]
    dot_general x132 -> x0, matrix products: 40.8 us -> none  [the longest x44 14.1 us: along_depth(): result = jnp.einsum('oi,eixy->eoxy', matrix, blocks, precision=highest)]
    ppermute x100 -> x20, waiting for transfers between devices: 61.8 us -> 28.8 us  [fetch(): lax.ppermute(value, axis, [((i + offset) % count, i) for i in range(count)])]
    pallas_call x0 -> x4, Pallas kernels: none -> 20.2 us  [the longest x3 11.9 us: call(): pl.pallas_call(kernel, out_shape=[jax.ShapeDtypeStruct(s, f32) for s in o...]
    mul x18 -> x0, local copies, waits for them, and re-layouts: 17 us -> none  [the longest x10 16.3 us: along_columns(): blocked = jnp.kron(jnp.eye(group, dtype=jnp.float32), matrix)]
    all_to_all x0 -> x1, starting transfers between devices: none -> 15.8 us  [local(): gathered = lax.all_to_all(chunk, ('gx', 'gy'), 0, 0, tiled=True)]
  transfers between devices with their start and end apart: 100 -> 21, of which waited for: 60 -> 7; matrix products, arithmetic and copies ran while one was open for 3% -> 3% of each run, Pallas kernels for 0% -> 1%
where the time goes in v1:
time: 138 us; the launch traced here: 137 us
  starting transfers between devices  68.9 us (50%)
  waiting for transfers between devices  28.8 us (21%)
  Pallas kernels  20.2 us (15%)
  local copies, waits for them, and re-layouts  16.1 us (12%)
  other arithmetic  2.49 us (2%)
    ppermute x20, starting transfers between devices, fetch(): lax.ppermute(value, axis, [((i + offset) % count, i) for i in range(count)])  53.1 us
    ppermute x20, waiting for transfers between devices, fetch(): lax.ppermute(value, axis, [((i + offset) % count, i) for i in range(count)])  28.8 us
    all_to_all x1, starting transfers between devices, local(): gathered = lax.all_to_all(chunk, ('gx', 'gy'), 0, 0, tiled=True)  15.8 us
    unnamed x108, local copies, waits for them, and re-layouts  13.8 us
    pallas_call x3, Pallas kernels, call(): pl.pallas_call(kernel, out_shape=[jax.ShapeDtypeStruct(s, f32) for s in o...  11.9 us
    pallas_call x1, Pallas kernels, post(): pl.pallas_call(kernel, out_shape=jax.ShapeDtypeStruct((16, 16, 256), f32)...  8.32 us
  transfers between devices with their start and end apart: 21, of which 7 were waited for; matrix products, arithmetic and copies ran while one was open for 3% of the time, Pallas kernels for 1%

profile of v1, /device:TPU:1, one launch (start us, length us, event | category | flops | bytes accessed | tf_op | source)
XLA Modules:
  0.0 137.3 jit_solution(5639270469646681628)
XLA Ops:
  0.0 1.0 copy_bitcast_fusion.1
  1.1 3.3 %collective-permute-start = (f32[2,128,128]{2,1,0:T(8,128)S(1)}, f32[2,128,128]{2,1,0:T(8,128)S(1)}, u32[]{:S(2)}, u32[]{:S(2)}) collective-permute-start(f32[2,128,128]{2,1,0:T(8,128)S(1)} %get-tuple-element.22), channel_id=1, source_target_pairs={{1,0},{2,1},{3,2},{4,3},{5,4},{6,5},{7,6},{0,7},{9,8},{10,9},{11,1... | collective-permute-start | bytes 393224 | tf_op jit(solution)/shard_map/ppermute | solution.py:609
  4.5 1.8 %collective-permute-done = f32[2,128,128]{2,1,0:T(8,128)S(1)} collective-permute-done((f32[2,128,128]{2,1,0:T(8,128)S(1)}, f32[2,128,128]{2,1,0:T(8,128)S(1)}, u32[]{:S(2)}, u32[]{:S(2)}) %collective-permute-start) | collective-permute-done | bytes 131104 | tf_op jit(solution)/shard_map/ppermute | solution.py:609
  6.6 8.1 %collective-permute-start.2 = (f32[2,128,384]{2,1,0:T(8,128)S(1)}, f32[2,128,384]{2,1,0:T(8,128)S(1)}, u32[]{:S(2)}, u32[]{:S(2)}) collective-permute-start(f32[2,128,384]{2,1,0:T(8,128)S(1)} %pad_maximum_fusion.1.refs_12_), channel_id=1, source_target_pairs={{8,0},{16,8},{24,16},{32,24},{40,32},{48,40},{56,48},{64,56},{72,6... | collective-permute-start | bytes 1179656 | tf_op jit(solution)/shard_map/ppermute | solution.py:609
  15.1 5.7 %collective-permute-start.4 = (f32[144,384]{1,0:T(8,128)S(1)}, f32[144,384]{1,0:T(8,128)S(1)}, u32[]{:S(2)}, u32[]{:S(2)}) collective-permute-start(f32[144,384]{1,0:T(8,128)S(1)} %pad_maximum_fusion.3), channel_id=1, source_target_pairs={{16,0},{24,8},{32,16},{40,24},{48,32},{56,40},{64,48},{72,56},{80,... | collective-permute-start | bytes 663560 | tf_op jit(solution)/shard_map/ppermute | solution.py:609
  20.8 6.3 %collective-permute-done.5.refs_16_ = f32[144,384]{1,0:T(8,128)S(1)} collective-permute-done((f32[144,384]{1,0:T(8,128)S(1)}, f32[144,384]{1,0:T(8,128)S(1)}, u32[]{:S(2)}, u32[]{:S(2)}) %collective-permute-start.5) | collective-permute-done | bytes 221216 | tf_op jit(solution)/shard_map/ppermute | solution.py:609
  27.1 3.6 %collective-permute-done.4.refs_15_ = f32[144,384]{1,0:T(8,128)S(1)} collective-permute-done((f32[144,384]{1,0:T(8,128)S(1)}, f32[144,384]{1,0:T(8,128)S(1)}, u32[]{:S(2)}, u32[]{:S(2)}) %collective-permute-start.4) | collective-permute-done | bytes 221216 | tf_op jit(solution)/shard_map/ppermute | solution.py:609
  30.8 4.2 %shard_map.496 = (f32[2,128,256]{2,1,0:T(8,128)S(1)}, f32[2,128,384]{2,1,0:T(8,128)S(1)}, f32[64,128]{1,0:T(8,128)S(1)}) custom-call(f32[128,128]{1,0:T(8,128)S(1)} %copy-done.18, bf16[256,128]{1,0:T(8,128)(2,1)S(1)} %copy-done.37, bf16[256,128]{1,0:T(8,128)(2,1)S(1)} %copy-done.38, f32[128,128]{1,0:T(8,128)S(1)} %copy-done.20, f32[128,128]{1,0:T(8,128)S(1)} %copy-done.22, ...), custom_call_target="tpu_custom_call" | custom-call | tf_op jit(solution)/shard_map/pallas_call | solution.py:290
  35.8 5.9 %collective-permute-start.6 = (f32[64,128]{1,0:T(8,128)S(1)}, f32[64,128]{1,0:T(8,128)S(1)}, u32[]{:S(2)}, u32[]{:S(2)}) collective-permute-start(f32[64,128]{1,0:T(8,128)S(1)} %get-tuple-element.11), channel_id=1, source_target_pairs={{1,0},{2,1},{3,2},{4,3},{5,4},{6,5},{7,6},{0,7},{9,8},{10,9},{11,1... | collective-permute-start | bytes 98312 | tf_op jit(solution)/shard_map/ppermute | solution.py:609
  41.9 1.6 %collective-permute-done.6 = f32[64,128]{1,0:T(8,128)S(1)} collective-permute-done((f32[64,128]{1,0:T(8,128)S(1)}, f32[64,128]{1,0:T(8,128)S(1)}, u32[]{:S(2)}, u32[]{:S(2)}) %collective-permute-start.6) | collective-permute-done | bytes 32800 | tf_op jit(solution)/shard_map/ppermute | solution.py:609
  43.5 5.8 %collective-permute-start.10 = (f32[64,256]{1,0:T(8,128)S(1)}, f32[64,256]{1,0:T(8,128)S(1)}, u32[]{:S(2)}, u32[]{:S(2)}) collective-permute-start(f32[64,256]{1,0:T(8,128)S(1)} %pad_maximum_fusion.7.refs_15_), channel_id=1, source_target_pairs={{16,0},{24,8},{32,16},{40,24},{48,32},{56,40},{64,48},{72,56},{80,... | collective-permute-start | bytes 196616 | tf_op jit(solution)/shard_map/ppermute | solution.py:609
  49.3 4.7 %collective-permute-start.8 = (f32[64,256]{1,0:T(8,128)S(1)}, f32[64,256]{1,0:T(8,128)S(1)}, u32[]{:S(2)}, u32[]{:S(2)}) collective-permute-start(f32[64,256]{1,0:T(8,128)S(1)} %pad_maximum_fusion.7.refs_15_), channel_id=1, source_target_pairs={{8,0},{16,8},{24,16},{32,24},{40,32},{48,40},{56,48},{64,56},{72,6... | collective-permute-start | bytes 196616 | tf_op jit(solution)/shard_map/ppermute | solution.py:609
  54.0 4.8 %collective-permute-start.19 = (f32[2,128,384]{2,1,0:T(8,128)S(1)}, f32[2,128,384]{2,1,0:T(8,128)}, u32[]{:S(2)}, u32[]{:S(2)}) collective-permute-start(f32[2,128,384]{2,1,0:T(8,128)S(1)} %get-tuple-element.16), channel_id=1, source_target_pairs={{8,0},{16,8},{24,16},{32,24},{40,32},{48,40},{56,48},{64,56},{72,6... | collective-permute-start | bytes 1179656 | tf_op jit(solution)/shard_map/ppermute | solution.py:609
  58.8 2.5 %collective-permute-done.9.refs_17_ = f32[64,256]{1,0:T(8,128)S(1)} collective-permute-done((f32[64,256]{1,0:T(8,128)S(1)}, f32[64,256]{1,0:T(8,128)S(1)}, u32[]{:S(2)}, u32[]{:S(2)}) %collective-permute-start.9) | collective-permute-done | bytes 65568 | tf_op jit(solution)/shard_map/ppermute | solution.py:609
  61.4 2.1 %shard_map.497 = (f32[128,256]{1,0:T(8,128)S(1)}, f32[64,256]{1,0:T(8,128)S(1)}, f32[256,384]{1,0:T(8,128)S(1)}) custom-call(f32[256,256]{1,0:T(8,128)S(1)} %copy-done.14, bf16[256,384]{1,0:T(8,128)(2,1)S(1)} %copy-done.26, bf16[256,384]{1,0:T(8,128)(2,1)S(1)} %copy-done.27, f32[256,256]{1,0:T(8,128)S(1)} %copy-done.15, f32[256,256]{1,0:T(8,128)S(1)} %copy-done.16, ...), custom_call_target="tpu_custom_call" | custom-call | tf_op jit(solution)/shard_map/pallas_call | solution.py:290
  63.6 5.7 %collective-permute-start.16 = (f32[64,256]{1,0:T(8,128)S(1)}, f32[64,256]{1,0:T(8,128)S(1)}, u32[]{:S(2)}, u32[]{:S(2)}) collective-permute-start(f32[64,256]{1,0:T(8,128)S(1)} %get-tuple-element.13), channel_id=1, source_target_pairs={{16,0},{24,8},{32,16},{40,24},{48,32},{56,40},{64,48},{72,56},{80,... | collective-permute-start | bytes 196616 | tf_op jit(solution)/shard_map/ppermute | solution.py:609
  69.4 1.2 copy.62
  70.6 15.8 %all-to-all-start = ((f32[256,1,384]{2,1,0:T(1,128)}), f32[256,1,384]{2,1,0:T(1,128)}, u32[]{:S(2)}, u32[]{:S(2)}) async-start(f32[256,1,384]{2,1,0:T(1,128)} %copy.62), calls=%async_computation | async-start | bytes 786432 | tf_op jit(solution)/shard_map/all_to_all | solution.py:634
  86.5 1.6 %collective-permute-start.12 = (f32[160,256]{1,0:T(8,128)S(1)}, f32[160,256]{1,0:T(8,128)S(1)}, u32[]{:S(2)}, u32[]{:S(2)}) collective-permute-start(f32[160,256]{1,0:T(8,128)S(1)} %get-tuple-element.27), channel_id=1, source_target_pairs={{248,0},{0,8},{8,16},{16,24},{24,32},{32,40},{40,48},{48,56},{56,6... | collective-permute-start | bytes 491528 | tf_op jit(solution)/shard_map/ppermute | solution.py:609
  88.0 5.2 %collective-permute-start.13 = (f32[160,256]{1,0:T(8,128)S(1)}, f32[160,256]{1,0:T(8,128)S(1)}, u32[]{:S(2)}, u32[]{:S(2)}) collective-permute-start(f32[160,256]{1,0:T(8,128)S(1)} %get-tuple-element.28), channel_id=1, source_target_pairs={{8,0},{16,8},{24,16},{32,24},{40,32},{48,40},{56,48},{64,56},{72,6... | collective-permute-start | bytes 491528 | tf_op jit(solution)/shard_map/ppermute | solution.py:609
  93.3 10.3 %collective-permute-done.12 = f32[160,256]{1,0:T(8,128)S(1)} collective-permute-done((f32[160,256]{1,0:T(8,128)S(1)}, f32[160,256]{1,0:T(8,128)S(1)}, u32[]{:S(2)}, u32[]{:S(2)}) %collective-permute-start.12) | collective-permute-done | bytes 163872 | tf_op jit(solution)/shard_map/ppermute | solution.py:609
  103.6 1.9 %collective-permute-start.17 = (f32[32,256]{1,0:T(8,128)S(1)}, f32[32,256]{1,0:T(8,128)S(1)}, u32[]{:S(2)}, u32[]{:S(2)}) collective-permute-start(f32[32,256]{1,0:T(8,128)S(1)} %get-tuple-element.25), channel_id=1, source_target_pairs={{24,0},{32,8},{40,16},{48,24},{56,32},{64,40},{72,48},{80,56},{88,... | collective-permute-start | bytes 98312 | tf_op jit(solution)/shard_map/ppermute | solution.py:609
  105.5 2.6 %collective-permute-done.17 = f32[32,256]{1,0:T(8,128)S(1)} collective-permute-done((f32[32,256]{1,0:T(8,128)S(1)}, f32[32,256]{1,0:T(8,128)S(1)}, u32[]{:S(2)}, u32[]{:S(2)}) %collective-permute-start.17) | collective-permute-done | bytes 32800 | tf_op jit(solution)/shard_map/ppermute | solution.py:609
  108.2 2.3 %pad_maximum_fusion.refs_28_ = f32[6,128,384]{2,1,0:T(8,128)} fusion(f32[2,128,384]{2,1,0:T(8,128)} %collective-permute-done.19, f32[2,128,384]{2,1,0:T(8,128)S(1)} %get-tuple-element.16, f32[2,128,384]{2,1,0:T(8,128)} %collective-permute-done.18), kind=kLoop, calls=%fused_computation | loop fusion | flops 589824 | bytes 2359296 | tf_op jit(solution)/shard_map/concatenate | solution.py:636
  110.6 1.1 copy.67
  112.6 5.6 %shard_map.498.refs_24_ = f32[256,256]{1,0:T(8,128)S(1)} custom-call(bf16[384,128]{1,0:T(8,128)(2,1)S(1)} %copy-done.36, f32[1,128]{1,0:T(1,128)S(1)} %copy-done.48, f32[256,384]{1,0:T(8,128)S(1)} %bitcast.21), custom_call_target="tpu_custom_call" | custom-call | tf_op jit(solution)/shard_map/pallas_call | solution.py:290
  118.3 1.0 copy-done.9
  119.3 1.0 copy-done.10
  120.3 1.0 copy-done.11
  123.8 0.9 copy-done.29
  124.7 0.9 copy-done.30
  129.0 8.3 %shard_map.499 = f32[16,16,256]{2,1,0:T(8,128)} custom-call(f32[128,128]{1,0:T(8,128)S(1)} %copy-done.19, f32[128,128]{1,0:T(8,128)S(1)} %copy-done.21, f32[128,128]{1,0:T(8,128)S(1)} %copy-done.23, f32[128,128]{1,0:T(8,128)S(1)} %copy-done.25, bf16[256,256]{1,0:T(8,128)(2,1)S(1)} %copy-done.4, bf16[256,256]{1,0:T(8,128)(2,1)S(1)} %copy-done.5, ...), custom_call_target="tpu_custom_call" | custom-call | tf_op jit(solution)/shard_map/pallas_call | solution.py:597
  (144 shorter events, 8.6 us)
Async XLA Ops:
  1.1 5.3 %collective-permute-start = (f32[2,128,128]{2,1,0:T(8,128)S(1)}, f32[2,128,128]{2,1,0:T(8,128)S(1)}, u32[]{:S(2)}, u32[]{:S(2)}) collective-permute-start(f32[2,128,128]{2,1,0:T(8,128)S(1)} %get-tuple-element.22), channel_id=1, source_target_pairs={{1,0},{2,1},{3,2},{4,3},{5,4},{6,5},{7,6},{0,7},{9,8},{10,9},{11,1... | collective-permute-start | bytes 393224 | tf_op jit(solution)/shard_map/ppermute | solution.py:609
  4.3 2.0 %collective-permute-start.1 = (f32[2,128,128]{2,1,0:T(8,128)S(1)}, f32[2,128,128]{2,1,0:T(8,128)S(1)}, u32[]{:S(2)}, u32[]{:S(2)}) collective-permute-start(f32[2,128,128]{2,1,0:T(8,128)S(1)} %get-tuple-element.21), channel_id=1, source_target_pairs={{7,0},{0,1},{1,2},{2,3},{3,4},{4,5},{5,6},{6,7},{15,8},{8,9},{9,10... | collective-permute-start | bytes 393224 | tf_op jit(solution)/shard_map/ppermute | solution.py:609
  6.6 24.1 %collective-permute-start.2 = (f32[2,128,384]{2,1,0:T(8,128)S(1)}, f32[2,128,384]{2,1,0:T(8,128)S(1)}, u32[]{:S(2)}, u32[]{:S(2)}) collective-permute-start(f32[2,128,384]{2,1,0:T(8,128)S(1)} %pad_maximum_fusion.1.refs_12_), channel_id=1, source_target_pairs={{8,0},{16,8},{24,16},{32,24},{40,32},{48,40},{56,48},{64,56},{72,6... | collective-permute-start | bytes 1179656 | tf_op jit(solution)/shard_map/ppermute | solution.py:609
  14.7 16.0 %collective-permute-start.3 = (f32[2,128,384]{2,1,0:T(8,128)S(1)}, f32[2,128,384]{2,1,0:T(8,128)S(1)}, u32[]{:S(2)}, u32[]{:S(2)}) collective-permute-start(f32[2,128,384]{2,1,0:T(8,128)S(1)} %pad_maximum_fusion.1.refs_12_), channel_id=1, source_target_pairs={{248,0},{0,8},{8,16},{16,24},{24,32},{32,40},{40,48},{48,56},{56,6... | collective-permute-start | bytes 1179656 | tf_op jit(solution)/shard_map/ppermute | solution.py:609
  14.8 12.4 %collective-permute-start.5 = (f32[144,384]{1,0:T(8,128)S(1)}, f32[144,384]{1,0:T(8,128)S(1)}, u32[]{:S(2)}, u32[]{:S(2)}) collective-permute-start(f32[144,384]{1,0:T(8,128)S(1)} %pad_maximum_fusion.4), channel_id=1, source_target_pairs={{240,0},{248,8},{0,16},{8,24},{16,32},{24,40},{32,48},{40,56},{48,... | collective-permute-start | bytes 663560 | tf_op jit(solution)/shard_map/ppermute | solution.py:609
  14.9 46.4 %copy-start.2 = (bf16[256,256]{1,0:T(8,128)(2,1)S(1)}, bf16[256,256]{1,0:T(8,128)(2,1)}, u32[]{:S(2)}) copy-start(bf16[256,256]{1,0:T(8,128)(2,1)} %constant.107.clone.refs_6_.refs_15_) | copy-start | bytes 393220
  14.9 46.4 %copy-start.3 = (bf16[256,256]{1,0:T(8,128)(2,1)S(1)}, bf16[256,256]{1,0:T(8,128)(2,1)}, u32[]{:S(2)}) copy-start(bf16[256,256]{1,0:T(8,128)(2,1)} %constant.108.clone.refs_7_.refs_16_) | copy-start | bytes 393220
  14.9 46.4 %copy-start.14 = (f32[256,256]{1,0:T(8,128)S(1)}, f32[256,256]{1,0:T(8,128)}, u32[]{:S(2)}) copy-start(f32[256,256]{1,0:T(8,128)} %constant.101.clone.refs_0_) | copy-start | bytes 786436
  14.9 46.4 %copy-start.15 = (f32[256,256]{1,0:T(8,128)S(1)}, f32[256,256]{1,0:T(8,128)}, u32[]{:S(2)}) copy-start(f32[256,256]{1,0:T(8,128)} %constant.104.clone.refs_3_) | copy-start | bytes 786436
  14.9 46.4 %copy-start.16 = (f32[256,256]{1,0:T(8,128)S(1)}, f32[256,256]{1,0:T(8,128)}, u32[]{:S(2)}) copy-start(f32[256,256]{1,0:T(8,128)} %constant.105.clone.refs_4_) | copy-start | bytes 786436
  14.9 46.4 %copy-start.17 = (f32[256,256]{1,0:T(8,128)S(1)}, f32[256,256]{1,0:T(8,128)}, u32[]{:S(2)}) copy-start(f32[256,256]{1,0:T(8,128)} %constant.106.clone.refs_5_) | copy-start | bytes 786436
  15.0 46.4 %copy-start.26 = (bf16[256,384]{1,0:T(8,128)(2,1)S(1)}, bf16[256,384]{1,0:T(8,128)(2,1)}, u32[]{:S(2)}) copy-start(bf16[256,384]{1,0:T(8,128)(2,1)} %constant.102.clone.refs_1_) | copy-start | bytes 589828
  15.0 46.4 %copy-start.27 = (bf16[256,384]{1,0:T(8,128)(2,1)S(1)}, bf16[256,384]{1,0:T(8,128)(2,1)}, u32[]{:S(2)}) copy-start(bf16[256,384]{1,0:T(8,128)(2,1)} %constant.103.clone.refs_2_) | copy-start | bytes 589828
  15.0 46.4 %copy-start.28 = (bf16[256,320]{1,0:T(8,128)(2,1)S(1)}, bf16[256,320]{1,0:T(8,128)(2,1)}, u32[]{:S(2)}) copy-start(bf16[256,320]{1,0:T(8,128)(2,1)} %constant.114.clone.refs_13_) | copy-start | bytes 491524
  15.0 46.4 %copy-start.31 = (bf16[256,256]{1,0:T(8,128)(2,1)S(1)}, bf16[256,256]{1,0:T(8,128)(2,1)}, u32[]{:S(2)}) copy-start(bf16[256,256]{1,0:T(8,128)(2,1)} %constant.109.clone.refs_8_) | copy-start | bytes 393220
  15.0 46.4 %copy-start.32 = (bf16[256,256]{1,0:T(8,128)(2,1)S(1)}, bf16[256,256]{1,0:T(8,128)(2,1)}, u32[]{:S(2)}) copy-start(bf16[256,256]{1,0:T(8,128)(2,1)} %constant.110.clone.refs_9_) | copy-start | bytes 393220
  15.1 15.6 %collective-permute-start.4 = (f32[144,384]{1,0:T(8,128)S(1)}, f32[144,384]{1,0:T(8,128)S(1)}, u32[]{:S(2)}, u32[]{:S(2)}) collective-permute-start(f32[144,384]{1,0:T(8,128)S(1)} %pad_maximum_fusion.3), channel_id=1, source_target_pairs={{16,0},{24,8},{32,16},{40,24},{48,32},{56,40},{64,48},{72,56},{80,... | collective-permute-start | bytes 663560 | tf_op jit(solution)/shard_map/ppermute | solution.py:609
  35.8 7.7 %collective-permute-start.6 = (f32[64,128]{1,0:T(8,128)S(1)}, f32[64,128]{1,0:T(8,128)S(1)}, u32[]{:S(2)}, u32[]{:S(2)}) collective-permute-start(f32[64,128]{1,0:T(8,128)S(1)} %get-tuple-element.11), channel_id=1, source_target_pairs={{1,0},{2,1},{3,2},{4,3},{5,4},{6,5},{7,6},{0,7},{9,8},{10,9},{11,1... | collective-permute-start | bytes 98312 | tf_op jit(solution)/shard_map/ppermute | solution.py:609
  41.7 1.7 %collective-permute-start.7 = (f32[64,128]{1,0:T(8,128)S(1)}, f32[64,128]{1,0:T(8,128)S(1)}, u32[]{:S(2)}, u32[]{:S(2)}) collective-permute-start(f32[64,128]{1,0:T(8,128)S(1)} %get-tuple-element.11), channel_id=1, source_target_pairs={{7,0},{0,1},{1,2},{2,3},{3,4},{4,5},{5,6},{6,7},{15,8},{8,9},{9,10... | collective-permute-start | bytes 98312 | tf_op jit(solution)/shard_map/ppermute | solution.py:609
  43.5 10.5 %collective-permute-start.10 = (f32[64,256]{1,0:T(8,128)S(1)}, f32[64,256]{1,0:T(8,128)S(1)}, u32[]{:S(2)}, u32[]{:S(2)}) collective-permute-start(f32[64,256]{1,0:T(8,128)S(1)} %pad_maximum_fusion.7.refs_15_), channel_id=1, source_target_pairs={{16,0},{24,8},{32,16},{40,24},{48,32},{56,40},{64,48},{72,56},{80,... | collective-permute-start | bytes 196616 | tf_op jit(solution)/shard_map/ppermute | solution.py:609
  49.3 9.5 %collective-permute-start.11 = (f32[64,256]{1,0:T(8,128)S(1)}, f32[64,256]{1,0:T(8,128)S(1)}, u32[]{:S(2)}, u32[]{:S(2)}) collective-permute-start(f32[64,256]{1,0:T(8,128)S(1)} %pad_maximum_fusion.7.refs_15_), channel_id=1, source_target_pairs={{240,0},{248,8},{0,16},{8,24},{16,32},{24,40},{32,48},{40,56},{48,... | collective-permute-start | bytes 196616 | tf_op jit(solution)/shard_map/ppermute | solution.py:609
  49.3 9.5 %collective-permute-start.8 = (f32[64,256]{1,0:T(8,128)S(1)}, f32[64,256]{1,0:T(8,128)S(1)}, u32[]{:S(2)}, u32[]{:S(2)}) collective-permute-start(f32[64,256]{1,0:T(8,128)S(1)} %pad_maximum_fusion.7.refs_15_), channel_id=1, source_target_pairs={{8,0},{16,8},{24,16},{32,24},{40,32},{48,40},{56,48},{64,56},{72,6... | collective-permute-start | bytes 196616 | tf_op jit(solution)/shard_map/ppermute | solution.py:609
  53.9 7.4 %collective-permute-start.9 = (f32[64,256]{1,0:T(8,128)S(1)}, f32[64,256]{1,0:T(8,128)S(1)}, u32[]{:S(2)}, u32[]{:S(2)}) collective-permute-start(f32[64,256]{1,0:T(8,128)S(1)} %pad_maximum_fusion.7.refs_15_), channel_id=1, source_target_pairs={{248,0},{0,8},{8,16},{16,24},{24,32},{32,40},{40,48},{48,56},{56,6... | collective-permute-start | bytes 196616 | tf_op jit(solution)/shard_map/ppermute | solution.py:609
  54.0 54.2 %collective-permute-start.18 = (f32[2,128,384]{2,1,0:T(8,128)S(1)}, f32[2,128,384]{2,1,0:T(8,128)}, u32[]{:S(2)}, u32[]{:S(2)}) collective-permute-start(f32[2,128,384]{2,1,0:T(8,128)S(1)} %get-tuple-element.16), channel_id=1, source_target_pairs={{248,0},{0,8},{8,16},{16,24},{24,32},{32,40},{40,48},{48,56},{56,6... | collective-permute-start | bytes 1179656 | tf_op jit(solution)/shard_map/ppermute | solution.py:609
  54.0 54.2 %collective-permute-start.19 = (f32[2,128,384]{2,1,0:T(8,128)S(1)}, f32[2,128,384]{2,1,0:T(8,128)}, u32[]{:S(2)}, u32[]{:S(2)}) collective-permute-start(f32[2,128,384]{2,1,0:T(8,128)S(1)} %get-tuple-element.16), channel_id=1, source_target_pairs={{8,0},{16,8},{24,16},{32,24},{40,32},{48,40},{56,48},{64,56},{72,6... | collective-permute-start | bytes 1179656 | tf_op jit(solution)/shard_map/ppermute | solution.py:609
  63.5 24.5 %collective-permute-start.15 = (f32[64,256]{1,0:T(8,128)S(1)}, f32[64,256]{1,0:T(8,128)S(1)}, u32[]{:S(2)}, u32[]{:S(2)}) collective-permute-start(f32[64,256]{1,0:T(8,128)S(1)} %get-tuple-element.13), channel_id=1, source_target_pairs={{240,0},{248,8},{0,16},{8,24},{16,32},{24,40},{32,48},{40,56},{48,... | collective-permute-start | bytes 196616 | tf_op jit(solution)/shard_map/ppermute | solution.py:609
  63.6 41.9 %collective-permute-start.16 = (f32[64,256]{1,0:T(8,128)S(1)}, f32[64,256]{1,0:T(8,128)S(1)}, u32[]{:S(2)}, u32[]{:S(2)}) collective-permute-start(f32[64,256]{1,0:T(8,128)S(1)} %get-tuple-element.13), channel_id=1, source_target_pairs={{16,0},{24,8},{32,16},{40,24},{48,32},{56,40},{64,48},{72,56},{80,... | collective-permute-start | bytes 196616 | tf_op jit(solution)/shard_map/ppermute | solution.py:609
  69.3 17.1 %collective-permute-start.14 = (f32[32,256]{1,0:T(8,128)S(1)}, f32[32,256]{1,0:T(8,128)S(1)}, u32[]{:S(2)}, u32[]{:S(2)}) collective-permute-start(f32[32,256]{1,0:T(8,128)S(1)} %get-tuple-element.26), channel_id=1, source_target_pairs={{232,0},{240,8},{248,16},{0,24},{8,32},{16,40},{24,48},{32,56},{40... | collective-permute-start | bytes 98312 | tf_op jit(solution)/shard_map/ppermute | solution.py:609
  70.6 40.0 %all-to-all-start = ((f32[256,1,384]{2,1,0:T(1,128)}), f32[256,1,384]{2,1,0:T(1,128)}, u32[]{:S(2)}, u32[]{:S(2)}) async-start(f32[256,1,384]{2,1,0:T(1,128)} %copy.62), calls=%async_computation | async-start | bytes 786432 | tf_op jit(solution)/shard_map/all_to_all | solution.py:634
  86.5 17.1 %collective-permute-start.12 = (f32[160,256]{1,0:T(8,128)S(1)}, f32[160,256]{1,0:T(8,128)S(1)}, u32[]{:S(2)}, u32[]{:S(2)}) collective-permute-start(f32[160,256]{1,0:T(8,128)S(1)} %get-tuple-element.27), channel_id=1, source_target_pairs={{248,0},{0,8},{8,16},{16,24},{24,32},{32,40},{40,48},{48,56},{56,6... | collective-permute-start | bytes 491528 | tf_op jit(solution)/shard_map/ppermute | solution.py:609
  88.0 17.4 %collective-permute-start.13 = (f32[160,256]{1,0:T(8,128)S(1)}, f32[160,256]{1,0:T(8,128)S(1)}, u32[]{:S(2)}, u32[]{:S(2)}) collective-permute-start(f32[160,256]{1,0:T(8,128)S(1)} %get-tuple-element.28), channel_id=1, source_target_pairs={{8,0},{16,8},{24,16},{32,24},{40,32},{48,40},{56,48},{64,56},{72,6... | collective-permute-start | bytes 491528 | tf_op jit(solution)/shard_map/ppermute | solution.py:609
  103.6 4.6 %collective-permute-start.17 = (f32[32,256]{1,0:T(8,128)S(1)}, f32[32,256]{1,0:T(8,128)S(1)}, u32[]{:S(2)}, u32[]{:S(2)}) collective-permute-start(f32[32,256]{1,0:T(8,128)S(1)} %get-tuple-element.25), channel_id=1, source_target_pairs={{24,0},{32,8},{40,16},{48,24},{56,32},{64,40},{72,48},{80,56},{88,... | collective-permute-start | bytes 98312 | tf_op jit(solution)/shard_map/ppermute | solution.py:609
  (39 other events, 558.4 us)

commit v2 on v1

v2 whole, which is shorter than its diff:
```python
import math

import jax
import jax.numpy as jnp
import ml_dtypes
import numpy as np
from jax import lax
from jax.experimental import pallas as pl
from jax.experimental.pallas import tpu as pltpu
from jax.sharding import PartitionSpec as P

CG_ITERS = 8
mass_coef = 0.000125
cheb_ratio = 0.1
f32 = jnp.float32
bf16 = jnp.bfloat16
MB = 1024 * 1024


def legendre_pair(points, order):
    previous = 0.0 * points + 1.0
    current = points * 1.0
    for degree in range(2, order + 1):
        previous, current = (
            current,
            ((2.0 * degree - 1.0) * points * current - (degree - 1.0) * previous) / degree,
        )
    return (previous, current)


def gll_tables(order):
    count_nodes = order + 1
    points = -np.cos(math.pi * np.arange(count_nodes) / order)
    for sweep in range(60):
        previous, values_at = legendre_pair(points, order)
        points = points - (points * values_at - previous) / (count_nodes * values_at)
    previous, values_at = legendre_pair(points, order)
    weights = 2.0 / (order * (order + 1) * values_at * values_at)
    spacing = points[:, None] - points[None, :]
    safe_spacing = np.where(spacing == 0.0, 1.0, spacing)
    derivative = values_at[:, None] / (values_at[None, :] * safe_spacing)
    derivative = derivative * (1.0 - np.eye(count_nodes))
    corner_value = order * (order + 1) / 4.0
    end_values = np.concatenate(
        [np.array([-corner_value]), np.zeros(count_nodes - 2), np.array([corner_value])]
    )
    return (points, weights, derivative + np.eye(count_nodes) * end_values[None, :])


def interp_table(fine_order, coarse_order):
    fine_points = gll_tables(fine_order)[0]
    coarse_points = gll_tables(coarse_order)[0]
    numer = fine_points[:, None, None] - coarse_points[None, None, :]
    denom = coarse_points[None, :, None] - coarse_points[None, None, :]
    same_node = np.eye(len(coarse_points))[None, :, :] > 0.5
    ratio = np.where(same_node, 1.0, numer / np.where(same_node, 1.0, denom))
    return ratio.prod(axis=2)


def element_bound(order):
    points, weights, derivative = gll_tables(order)
    mass = np.eye(order + 1) * weights[None, :]
    stiff = np.dot(derivative.T, np.dot(mass, derivative))
    full = 0.5 * (
        np.kron(np.kron(mass, mass), stiff)
        + np.kron(np.kron(mass, stiff), mass)
        + np.kron(np.kron(stiff, mass), mass)
    ) + mass_coef * np.kron(np.kron(mass, mass), mass)
    diagonal_entries = np.sum(full * np.eye(full.shape[0]), axis=1)
    ratio = np.abs(full).sum(axis=1) / diagonal_entries
    return float(ratio.max())


def sum_matrix(elements, n, cyclic):
    out = np.eye(elements * n)
    for e in range(elements):
        if cyclic or e + 1 < elements:
            a, b = e * n + n - 1, ((e + 1) % elements) * n
            out[a, b] += 1.0
            out[b, a] += 1.0
    return out


def blocks(matrix, count):
    return np.kron(np.eye(count), matrix)


class Level:
    def __init__(self, order):
        n = self.n = order + 1
        _, w, dm = gll_tables(order)
        self.w = w
        self.k = dm.T @ np.diag(w) @ dm
        self.sum_z = sum_matrix(2, n, False)
        self.k_z = self.sum_z @ blocks(self.k, 2)
        self.w_z = self.sum_z @ np.tile(w, 2)
        self.w_p = w.copy()
        self.w_p[0] += w[-1]
        self.w_p[-1] += w[0]
        kd = np.diag(self.k).copy()
        kd_p = kd.copy()
        kd_p[0] += kd[-1]
        kd_p[-1] += kd[0]
        kd_z = self.sum_z @ np.tile(kd, 2)
        wz, wp = self.w_z, self.w_p
        diag = 0.5 * (
            np.einsum("z,r,c->zrc", wz, kd_p, wp)
            + np.einsum("z,r,c->zrc", wz, wp, kd_p)
            + np.einsum("z,r,c->zrc", kd_z, wp, wp)
        ) + mass_coef * np.einsum("z,r,c->zrc", wz, wp, wp)
        self.dinv = 1.0 / diag
        upper = element_bound(order)
        lower = cheb_ratio * upper
        center, half = 0.5 * (upper + lower), 0.5 * (upper - lower)
        sigma = center / half
        rho = 1.0 / sigma
        self.first = 1.0 / center
        self.steps = []
        for _ in range(2):
            rho2 = 1.0 / (2.0 * sigma - rho)
            self.steps.append((float(rho2 * rho), 2.0 * rho2 / half))
            rho = rho2
        self.m_p = np.ones(n)
        self.m_p[0] = self.m_p[-1] = 0.5
        self.m_z = np.ones(2 * n)
        self.m_z[n - 1] = self.m_z[n] = 0.5


def hi_lo(matrix):
    matrix = np.asarray(matrix, np.float64)
    hi = matrix.astype(ml_dtypes.bfloat16)
    lo = (matrix - hi.astype(np.float64)).astype(ml_dtypes.bfloat16)
    return hi, lo


def packed_left(matrix):
    hi, lo = hi_lo(matrix)
    return np.block([[hi, hi], [lo, np.zeros_like(lo)]])


def packed_right(matrix):
    hi, lo = hi_lo(matrix)
    return np.block([[hi, lo], [hi, np.zeros_like(lo)]])


FINE, MID, COARSE = Level(7), Level(3), Level(1)
J_FINE, J_MID = interp_table(7, 3), interp_table(3, 1)


def pattern(level, lanes):
    d = level.dinv.reshape(2 * level.n * level.n, level.n)
    return np.tile(d, (1, lanes // level.n))


def closed_operator(level, rows):
    n = level.n
    k_r = sum_matrix(rows, n, False) @ blocks(level.k, rows)
    k_r[0, 0] += level.k[-1, -1]
    k_r[-1, -1] += level.k[0, 0]
    return tensor_rows(level, k_r.reshape(rows, n, rows, n), rows)


def tensor_rows(level, k_r, rows):
    n = level.n
    w_r = np.diag(np.tile(level.w_p, rows)).reshape(rows, n, rows, n)
    kz, wz = level.k_z, np.diag(level.w_z)
    t = (
        0.5 * np.einsum("zy,eafb->ezafyb", kz, w_r)
        + 0.5 * np.einsum("zy,eafb->ezafyb", wz, k_r)
        + mass_coef * np.einsum("zy,eafb->ezafyb", wz, w_r)
    )
    return t.reshape(rows * 2 * n * n, rows * 2 * n * n)


def window_operator(level, rows):
    n = level.n
    k_r = sum_matrix(rows, n, False) @ blocks(level.k, rows)
    size = 2 * n * n
    return tensor_rows(level, k_r.reshape(rows, n, rows, n), rows)[size:-size]


def plane_matrix(n, low, high, count=2):
    t = np.zeros((2, 2 * n, count, 2 * n, n))
    for z in range(2 * n):
        t[0, z, 0, z] = low
        t[1, z, count - 1, z] = high
    return t.reshape(4 * n, count * 2 * n * n)


def inner_lines(level):
    low, high = level.k[0].copy(), level.k[-1].copy()
    low[0] = 0.0
    high[-1] = 0.0
    return low, high


def face_matrix(level, count=2):
    n = level.n
    first, last = np.eye(n)[0], np.eye(n)[-1]
    t = plane_matrix(n, first, last, count).T
    return t * np.tile(0.5 * level.w_z, 2)[None, :]


def pair(consts, name, matrix):
    consts[name + "h"], consts[name + "l"] = hi_lo(matrix)


def fine_constants():
    dinv = pattern(FINE, 128)
    return dict(
        kc=packed_right(blocks(FINE.k, 16).T),
        wc=np.tile(FINE.w_p, 16)[None, :].astype(np.float32),
        cf=np.repeat(0.5 * np.kron(FINE.w_z, FINE.w_p)[:, None], 128, axis=1).astype(np.float32),
        d1=(FINE.first * dinv).astype(np.float32),
        d2=(FINE.steps[0][1] * dinv).astype(np.float32),
        d3=(FINE.steps[1][1] * dinv).astype(np.float32),
    )


def own_constants():
    c = fine_constants()
    pair(c, "m", closed_operator(FINE, 2))
    pair(c, "pl", plane_matrix(8, *inner_lines(FINE)))
    pair(c, "pf", face_matrix(FINE))
    return c


def mid_constants():
    dinv = pattern(MID, 256)
    c = dict(
        wc=np.tile(MID.w_p, 64)[None, :].astype(np.float32),
        cf=np.repeat(0.5 * np.kron(MID.w_z, MID.w_p)[:, None], 256, axis=1).astype(np.float32),
        d1=(MID.first * dinv).astype(np.float32),
        d2=(MID.steps[0][1] * dinv).astype(np.float32),
        d3=(MID.steps[1][1] * dinv).astype(np.float32),
    )
    pair(c, "k", (sum_matrix(64, 4, True) @ blocks(MID.k, 64)).T)
    return c


def mid_own_constants():
    c = mid_constants()
    pair(c, "m", closed_operator(MID, 2))
    pair(c, "pl", plane_matrix(4, *inner_lines(MID)))
    pair(c, "pf", face_matrix(MID))
    return c


def dot(a, b):
    return jnp.dot(a, b, preferred_element_type=f32)


def split(u):
    h = u.astype(bf16)
    return h, (u - h.astype(f32)).astype(bf16)


def left(c, name, parts):
    h, l = parts
    th, tl = c[name + "h"][...], c[name + "l"][...]
    return dot(th, h) + dot(th, l) + dot(tl, h)


def right(c, name, parts):
    h, l = parts
    th, tl = c[name + "h"][...], c[name + "l"][...]
    return dot(h, th) + dot(l, th) + dot(h, tl)


def tiles(ref, rows, lanes):
    t = ref[...]
    if lanes > 1:
        t = jnp.concatenate([t] * lanes, axis=1)
    if rows > 1:
        t = jnp.concatenate([t] * rows, axis=0)
    return t


def row_sum(before, here, after):
    lanes = here.shape[-1]
    cube = (16, 8, lanes)
    node = lax.broadcasted_iota(jnp.int32, cube, 1)
    out = here.reshape(cube)
    if before is not None:
        out = out + jnp.where(node == 0, pltpu.roll(before.reshape(cube), 1, 1), 0.0)
    if after is not None:
        out = out + jnp.where(node == 7, pltpu.roll(after.reshape(cube), 7, 1), 0.0)
    return out.reshape(128, lanes)


def col_sum(y):
    lanes = y.shape[-1]
    node = lax.broadcasted_iota(jnp.int32, y.shape, 1) % 8
    b = pltpu.roll(y, 1, 1)
    a = pltpu.roll(y, lanes - 1, 1)
    return y + jnp.where(node == 0, b, 0.0) + jnp.where(node == 7, a, 0.0)


def col_stiff(parts, kc):
    h, l = parts
    y = []
    for k in range(h.shape[1] // 128):
        s = slice(128 * k, 128 * k + 128)
        z = dot(jnp.concatenate([h[:, s], l[:, s]], axis=1), kc)
        y.append(z[:, :128] + z[:, 128:])
    return col_sum(jnp.concatenate(y, axis=1))


def fine_own(parts, c, planes=None):
    lanes = parts[0].shape[1] // 128
    t = left(c, "m", parts)
    if planes is not None:
        t = t + left(c, "pf", split(planes))
    return tiles(c["wc"], 1, lanes) * t + tiles(c["cf"], 2, lanes) * col_stiff(parts, c["kc"][...])


def mid_apply(t, parts, c):
    y = right(c, "k", parts)
    return c["wc"][...] * t + tiles(c["cf"], t.shape[0] // 32, 1) * y


def mid_own(u, c, planes=None):
    parts = split(u)
    t = left(c, "m", parts)
    if planes is not None:
        t = t + left(c, "pf", split(planes))
    return mid_apply(t, parts, c)


class Table:
    def __init__(self, ref, at, shape, count):
        self.ref, self.at, self.shape, self.count = ref, at, shape, count

    def __getitem__(self, index):
        rows, lanes = self.shape
        step = rows + -rows % 16
        parts = [self.ref[self.at + step * k : self.at + step * k + rows] for k in range(self.count)]
        value = parts[0] if self.count == 1 else jnp.concatenate(parts, axis=1)
        value = value[:, :lanes]
        return value if index is Ellipsis else value[index]


def packed(consts):
    arrays, places = [], {}
    for kind in (np.float32, ml_dtypes.bfloat16):
        pieces, at = [], 0
        for name in sorted(consts):
            t = consts[name]
            if t.dtype != kind:
                continue
            rows, lanes = t.shape
            count = -(-lanes // 128)
            t = np.pad(t, ((0, -rows % 16), (0, count * 128 - lanes)))
            places[name] = (len(arrays), at, (rows, lanes), count)
            pieces += [t[:, 128 * k : 128 * k + 128] for k in range(count)]
            at += count * t.shape[0]
        if pieces:
            arrays.append(np.concatenate(pieces, axis=0))
    return arrays, places


def call(body, outs, consts, args, scratch=(), vmem=24):
    arrays, places = packed(consts)
    n, k = len(arrays), len(args)

    def kernel(*refs):
        c = {name: Table(refs[p[0]], *p[1:]) for name, p in places.items()}
        body(c, refs[n : n + k], refs[n + k :])

    spec = pl.BlockSpec(memory_space=pltpu.VMEM)
    return pl.pallas_call(
        kernel,
        out_shape=[jax.ShapeDtypeStruct(s, f32) for s in outs],
        in_specs=[spec] * (n + k),
        out_specs=[spec] * len(outs),
        scratch_shapes=list(scratch),
        compiler_params=pltpu.CompilerParams(vmem_limit_bytes=vmem * MB),
    )(*[jnp.asarray(a) for a in arrays], *args)


def fine_rhs(source, from_right, from_left):
    c = fine_constants()
    w = np.kron(np.tile(FINE.w, 2), FINE.w)[:, None] * np.tile(FINE.w, 16)[None, :]
    consts = dict(w=(0.125 * w).astype(np.float32), d1=c["d1"])
    pair(consts, "pl", plane_matrix(8, *inner_lines(FINE)))

    def body(c, ins, outs):
        source, from_right, from_left = ins
        b_out, low, high = outs
        w = tiles(c["w"], 1, 4)
        src = []
        for e in range(2):
            s = slice(8 * e, 8 * e + 8)
            src.append(
                jnp.concatenate(
                    [
                        source[:, s, :].reshape(128, 256),
                        from_right[:, s, :].reshape(128, 128),
                        from_left[:, s, :].reshape(128, 128),
                    ],
                    axis=1,
                )
                * w
            )
        b = []
        for y in (row_sum(None, src[0], src[1]), row_sum(src[0], src[1], None)):
            y = col_sum(y)
            inner = y[56:64] + y[64:72]
            b.append(jnp.concatenate([y[:56], inner, inner, y[72:]], axis=0))
        face0 = b[0].reshape(16, 8, 512)[:, 0, :]
        face1 = b[1].reshape(16, 8, 512)[:, 7, :]
        b = jnp.concatenate(b, axis=0)
        b_out[...] = b
        planes = left(c, "pl", split(tiles(c["d1"], 2, 4) * b))
        low[0:16] = face0
        low[16:32] = planes[:16]
        high[0:16] = face1
        high[16:32] = planes[16:]

    return call(
        body, [(256, 512), (32, 512), (32, 512)], consts, (source, from_right, from_left)
    )


def faced(low, high, at, rows):
    return jnp.concatenate([low[at : at + rows], high[at : at + rows]], axis=0)


def fine_middle(b, below, above):
    consts = own_constants()
    consts["f"] = plane_matrix(8, np.eye(8)[0], np.eye(8)[7]).T.astype(ml_dtypes.bfloat16)
    inside = np.ones(8)
    inside[0] = inside[7] = 0.0
    pair(consts, "q", plane_matrix(8, J_FINE[:, 0] * inside, J_FINE[:, 3] * inside))

    def body(c, ins, outs):
        b, below, above = ins
        x_out, r_out, d_out, low, high = outs
        h, l = split(faced(below, above, 0, 16))
        f = c["f"][...]
        b = b[...] + dot(f, h) + dot(f, l)
        d1, d2, d3 = (tiles(c[k], 2, 4) for k in ("d1", "d2", "d3"))
        d = d1 * b
        x = d
        r = b - fine_own(split(d), c, faced(below, above, 16, 16))
        d = FINE.steps[0][0] * d + d2 * r
        x_out[...] = (x + d)[:, :256]
        parts = split(d)
        plane1 = left(c, "pl", parts)
        r = r - fine_own(parts, c)
        d = FINE.steps[1][0] * d + d3 * r
        r_out[...] = r
        d_out[...] = d
        parts = split(d)
        plane2 = left(c, "pl", parts)
        row = lax.broadcasted_iota(jnp.int32, d.shape, 0)
        node = row % 8
        outer = ((row < 128) & (node == 0)) | ((row >= 128) & (node == 7))
        r = r - fine_own(split(jnp.where(outer, 0.0, d)), c)
        plane3 = left(c, "q", split(r))
        for k, plane in enumerate((plane1, plane2, plane3)):
            low[16 * k : 16 * k + 16] = plane[:16]
            high[16 * k : 16 * k + 16] = plane[16:]

    return call(
        body,
        [(256, 256), (256, 512), (256, 512), (48, 512), (48, 512)],
        consts,
        (b, below, above),
    )


def fine_last(x, r, d, below, above):
    consts = {"f_" + k: v for k, v in own_constants().items()}
    consts.update({"m_" + k: v for k, v in mid_own_constants().items()})
    kappa = float(np.sum(J_FINE[1:7, 0] * FINE.k[1:7, 0]))
    t = kappa * plane_matrix(8, np.eye(8)[0], np.eye(8)[7])
    pair(consts, "e", t * np.tile(0.5 * FINE.w_z, 2)[:, None])
    z = MID.sum_z @ blocks(J_FINE.T, 2) @ np.diag(FINE.m_z)
    rows = sum_matrix(2, 4, False) @ blocks(J_FINE.T @ np.diag(FINE.m_p), 2)
    rows[0, 0] += 0.5
    rows[-1, -1] += 0.5
    t = np.einsum("zy,eafb->ezafyb", z, rows.reshape(2, 4, 2, 8)).reshape(64, 256)
    pair(consts, "ra", t)
    t = np.zeros((2, 8, 4, 2, 16))
    t[0, :, 0, 0] = z
    t[1, :, 3, 1] = z
    pair(consts, "rp", t.reshape(64, 32))
    t = sum_matrix(64, 4, True) @ blocks(J_FINE.T @ np.diag(FINE.m_p), 64)
    pair(consts, "rc", t.T)

    def body(c, ins, outs):
        x, r, d, below, above = ins
        x0, r0, b_out, r1_out, low, high = outs
        f = {k[2:]: v for k, v in c.items() if k.startswith("f_")}
        m = {k[2:]: v for k, v in c.items() if k.startswith("m_")}
        wc = tiles(f["wc"], 1, 4)
        change = wc * left(f, "pf", split(faced(below, above, 0, 16)))
        r = r[...] - change
        d = d[...] - tiles(f["d3"], 2, 4) * change
        x0[...] = x[...] + d[:, :256]
        parts = split(d)
        r = r - fine_own(parts, f, faced(below, above, 16, 16))
        lane = lax.broadcasted_iota(jnp.int32, (256, 128), 1)
        r0[:, :256] = r[:, :256]
        r0[:, 256:] = jnp.where(lane < 64, r[:, 256:384], r[:, 384:])
        beyond = faced(below, above, 32, 16) - wc * left(c, "e", parts)
        b = left(c, "ra", split(r)) + left(c, "rp", split(beyond))
        b = right(c, "rc", split(b))
        b_out[...] = b
        d = tiles(m["d1"], 2, 1) * b
        plane1 = left(m, "pl", split(d))
        r = b - mid_own(d, m)
        r1_out[...] = r
        d = MID.steps[0][0] * d + tiles(m["d2"], 2, 1) * r
        plane2 = left(m, "pl", split(d))
        for k, plane in enumerate((plane1, plane2)):
            low[8 * k : 8 * k + 8] = plane[:8]
            high[8 * k : 8 * k + 8] = plane[8:]

    return call(
        body,
        [(256, 256), (256, 384), (64, 256), (64, 256), (16, 256), (16, 256)],
        consts,
        (x, r, d, below, above),
    )


def mid_last(b, r1, below, above):
    consts = mid_own_constants()
    top = np.zeros((3, 4))
    top[0, 0] = top[1, 1] = top[1, 2] = top[2, 3] = 1.0
    jz = top @ blocks(J_MID.T, 2)

    def down(z_part, r_part):
        t = np.zeros((4, 4, 2, 8, 4))
        for e in range(2):
            for k in range(2):
                t[e + k, :3, e] += np.einsum("zy,b->zyb", jz @ z_part, (J_MID.T @ r_part)[k])
        return t.reshape(16, 64)

    def across(part):
        t = np.zeros((256, 32))
        for v in range(32):
            t[4 * v : 4 * v + 4, v] += (J_MID.T @ part)[0]
            at = (4 * v - 4) % 256
            t[at : at + 4, v] += (J_MID.T @ part)[1]
        return np.tile(t, (1, 12))

    wz, wr = blocks(np.diag(MID.w), 2), np.diag(MID.w)
    kz = blocks(MID.k, 2)
    pair(consts, "sm", down(np.diag(MID.m_z), np.diag(MID.m_p)))
    pair(
        consts,
        "s1",
        0.5 * down(kz, wr) + 0.5 * down(wz, MID.k) + mass_coef * down(wz, wr),
    )
    pair(consts, "s2", 0.5 * down(wz, wr))
    pair(
        consts,
        "sc",
        np.concatenate([across(np.diag(MID.m_p)), -across(wr), -across(MID.k)], axis=0),
    )

    def body(c, ins, outs):
        b, r1, below, above = ins
        chunk, lo, hi, lo2, hi2 = outs
        d1, d2, d3 = (tiles(c[k], 2, 1) for k in ("d1", "d2", "d3"))
        d = d1 * b[...]
        x = d
        r = r1[...] - c["wc"][...] * left(c, "pf", split(faced(below, above, 0, 8)))
        d = MID.steps[0][0] * d + d2 * r
        x = x + d
        r = r - mid_own(d, c, faced(below, above, 8, 8))
        d = MID.steps[1][0] * d + d3 * r
        x = x + d
        parts = split(d)
        t = jnp.concatenate(
            [left(c, "sm", split(r)), left(c, "s1", parts), left(c, "s2", parts)], axis=1
        )
        t = right(c, "sc", split(t))
        q = lax.broadcasted_iota(jnp.int32, t.shape, 0)
        lane = lax.broadcasted_iota(jnp.int32, t.shape, 1) // 32
        t = jnp.sum(jnp.where(q == lane, t, 0.0), axis=0, keepdims=True)
        chunk[...] = jnp.broadcast_to(t, chunk.shape)
        plane1 = left(c, "pl", parts)
        r = r - mid_own(d, c)
        plane2 = left(c, "pl", split(d1 * r))
        for near, far, at in ((lo, lo2, 0), (hi, hi2, 1)):
            near[0:64] = r
            near[64:72] = plane1[8 * at : 8 * at + 8]
            near[72:104] = x[32 * at : 32 * at + 32]
            far[0:8] = plane1[8 * at : 8 * at + 8]
            far[8:16] = plane2[8 * at : 8 * at + 8]

    return call(
        body,
        [(256, 384), (104, 256), (104, 256), (16, 256), (16, 256)],
        consts,
        (b, r1, below, above),
    )


def coarse_constants():
    kz = np.zeros((4, 4))
    kz[:3, :3] = [[0.5, -0.5, 0.0], [-0.5, 1.0, -0.5], [0.0, -0.5, 0.5]]
    wz = np.array([1.0, 2.0, 1.0, 0.0])
    near = np.eye(32, k=1) + np.eye(32, k=-1)
    inner = 2.0 * np.kron(kz, np.eye(32)) + np.kron(np.diag(wz), 2.0 * np.eye(32) - 0.5 * near)
    up, down = np.zeros((32, 32)), np.zeros((32, 32))
    up[0, 31] = -0.5
    down[31, 0] = -0.5
    matrix = np.concatenate([inner, np.kron(np.diag(wz), up), np.kron(np.diag(wz), down)], axis=0)
    return dict(
        g_m=matrix.astype(ml_dtypes.bfloat16),
        g_wz=np.repeat(wz, 32)[None, :].astype(np.float32),
    )


def coarse_solve(g, c):
    m, wz = c["g_m"][...], c["g_wz"][...]

    def after(u):
        return jnp.concatenate([u[8:], u[:8]], axis=0)

    def before(u):
        return jnp.concatenate([u[-8:], u[:-8]], axis=0)

    def shifted(u, by):
        return pltpu.roll(u.reshape(32, 8, 128), by, 1).reshape(256, 128)

    def columns(u):
        a = u.astype(bf16)
        rest = u - a.astype(f32)
        b = rest.astype(bf16)
        e = (rest - b.astype(f32)).astype(bf16)
        t = None
        for part in (a, b, e):
            wide_part = part.astype(f32)
            v = dot(
                jnp.concatenate(
                    [
                        part,
                        shifted(wide_part, 7).astype(bf16),
                        shifted(wide_part, 1).astype(bf16),
                    ],
                    axis=1,
                ),
                m,
            )
            t = v if t is None else t + v
        return t

    half = -0.5 * wz
    mass = 4.0 * mass_coef * wz

    def apply(p):
        p0, p1 = p
        return (
            columns(p0) + half * (p1 + before(p1)) + mass * p0,
            columns(p1) + half * (p0 + after(p0)) + mass * p1,
        )

    def inner_product(a, b):
        s = jnp.sum(a[0] * b[0] + a[1] * b[1], axis=0, keepdims=True)
        return jnp.sum(s, axis=1, keepdims=True)

    r = (g[:, 0:128] + before(g[:, 256:384]), g[:, 128:256])
    p = r
    x = (jnp.zeros_like(r[0]), jnp.zeros_like(r[1]))
    norm = inner_product(r, r)
    for it in range(CG_ITERS):
        q = apply(p)
        alpha = norm / inner_product(p, q)
        x = tuple(a + alpha * b for a, b in zip(x, p))
        if it + 1 < CG_ITERS:
            r = tuple(a - alpha * b for a, b in zip(r, q))
            new = inner_product(r, r)
            beta = new / norm
            p = tuple(a + beta * b for a, b in zip(r, p))
            norm = new
    return jnp.concatenate(x, axis=1)


def second_smoothing(gathered, x0, r0, own_lo, own_hi, below, above, below2, above2):
    consts = coarse_constants()
    consts.update({"f_" + k: v for k, v in own_constants().items()})
    consts.update({"m_" + k: v for k, v in mid_constants().items()})
    pair(consts, "a", window_operator(MID, 10))
    pair(consts, "c", closed_operator(MID, 6))
    pair(consts, "p6", face_matrix(MID, 6))
    pair(consts, "p3", blocks(face_matrix(MID), 3))
    low, high = inner_lines(MID)
    pair(consts, "pl", plane_matrix(4, high, low))
    jc = np.zeros((3, 3, 4, 32, 256))
    for e in range(64):
        element = e if e < 48 else e - 64
        for k in range(2):
            v = element + k
            dev, col = v // 32 + 1, v % 32
            for z in range(3):
                jc[z, dev, z, col, 4 * e : 4 * e + 4] = J_MID[:, k]
    jc = jc.reshape(3, 384, 256)
    pair(consts, "vc", np.concatenate([jc[0], jc[1], jc[2]], axis=1))
    jz = np.zeros((8, 3))
    jz[:4, :2] += J_MID
    jz[4:, 1:] += J_MID
    jdr = np.zeros((10, 8, 4, 3, 16))
    for e in range(10):
        for k in range(2):
            jdr[e, :, :, :, e + k] += np.einsum("zp,a->zap", jz, J_MID[:, k])
    order = [2 * (q % 8) + q // 8 for q in range(16)]
    pair(consts, "vd", jdr[..., order].reshape(320, 48))
    fc = np.zeros((256, 384))
    for e in range(48):
        src = e if e < 40 else e + 16
        fc[4 * src : 4 * src + 4, 8 * e : 8 * e + 8] = J_FINE.T
    pair(consts, "fc", fc)
    fd = np.kron(blocks(J_FINE, 2), J_FINE)
    pair(consts, "fd", blocks(fd, 2))
    low, high = inner_lines(FINE)
    pair(consts, "fp", plane_matrix(8, high, low) @ blocks(fd, 2))

    def body(c, ins, outs):
        gathered, x0, r0, own_lo, own_hi, below, above, below2, above2 = ins
        s_out, r_out, d_out, low, high, twice, rows = outs
        i, j = lax.axis_index("gx"), lax.axis_index("gy")
        f = {k[2:]: v for k, v in c.items() if k.startswith("f_")}
        m = {k[2:]: v for k, v in c.items() if k.startswith("m_")}
        x2 = coarse_solve(gathered, c)
        twice[0:256] = x2
        twice[256:512] = x2
        first = lax.rem(i + 30, 32)
        picked = twice[pl.ds(pl.multiple_of(first * 8, 8), 64), :].reshape(8, 8, 256)
        sub = lax.broadcasted_iota(jnp.int32, (8, 8, 256), 1)
        for g in range(3):
            v = jnp.sum(jnp.where(sub == lax.rem(j + 7 + g, 8), picked, 0.0), axis=1)
            for k in range(2):
                rows[8 * k : 8 * k + 8, 128 * g : 128 * g + 128] = v[:, 128 * k : 128 * k + 128]
        y = right(c, "vc", split(rows[...]))
        y = jnp.concatenate([y[:, :256], y[:, 256:512], y[:, 512:]], axis=0)
        e2 = left(c, "vd", split(y))

        def window(u, size):
            h, l = split(u)
            th, tl = c["ah"][:size, : size + 64], c["al"][:size, : size + 64]
            t = dot(th, h) + dot(th, l) + dot(tl, h)
            return mid_apply(t, (h[32:-32], l[32:-32]), m)

        def table(name, count):
            return tiles(m[name], count, 1)

        planes = jnp.concatenate(
            [
                below2[:8],
                own_lo[64:72],
                below[64:72],
                above[64:72],
                own_hi[64:72],
                above2[:8],
            ],
            axis=0,
        )
        g = window(e2, 256)
        r = jnp.concatenate([below[:64], own_lo[:64], above[:64]], axis=0)
        r = r - m["wc"][...] * left(c, "p3", split(planes)) - g[32:224]
        d = table("d1", 6) * r
        x = jnp.concatenate([below[72:104], own_lo[72:104], own_hi[72:104], above[72:104]], axis=0)
        x = x + e2[96:224] + d[32:160]
        outer = jnp.concatenate([g[:32], g[224:]], axis=0) * table("d1", 2)
        planes = faced(below2, above2, 8, 8) - left(c, "pl", split(outer))
        parts = split(d)
        r = r - mid_apply(left(c, "c", parts) + left(c, "p6", split(planes)), parts, m)
        d = MID.steps[0][0] * d + table("d2", 6) * r
        x = x + d[32:160]
        r = r[32:160] - window(d, 128)
        d = MID.steps[1][0] * d[32:160] + table("d3", 4) * r
        x = x + d
        x = right(c, "fc", split(x))
        e1 = left(c, "fd", split(x[32:96]))
        planes = left(c, "fp", split(jnp.concatenate([x[:32], x[96:]], axis=0)))
        r = r0[...] - fine_own(split(e1), f, planes)
        d = tiles(f["d1"], 2, 3) * r
        s_out[...] = x0[...] + (e1 + d)[:, :256]
        parts = split(d)
        plane1 = left(f, "pl", parts)
        r = r - fine_own(parts, f)
        d = FINE.steps[0][0] * d + tiles(f["d2"], 2, 3) * r
        plane2 = left(f, "pl", split(d))
        r_out[...] = r
        d_out[...] = d
        for k, plane in enumerate((plane1, plane2)):
            low[16 * k : 16 * k + 16] = plane[:16]
            high[16 * k : 16 * k + 16] = plane[16:]

    return call(
        body,
        [(256, 256), (256, 384), (256, 384), (32, 384), (32, 384)],
        consts,
        (gathered, x0, r0, own_lo, own_hi, below, above, below2, above2),
        scratch=[pltpu.VMEM((512, 256), f32), pltpu.VMEM((16, 384), f32)],
    )


def last_step(s, r, d, below, above):
    consts = own_constants()

    def body(c, ins, outs):
        s, r, d, below, above = ins
        (out,) = outs
        change = tiles(c["wc"], 1, 3) * left(c, "pf", split(faced(below, above, 0, 16)))
        r = r[...] - change
        d = d[...] - tiles(c["d2"], 2, 3) * change
        r = r - fine_own(split(d), c, faced(below, above, 16, 16))
        v = s[...] + d[:, :256]
        d = FINE.steps[1][0] * d + tiles(c["d3"], 2, 3) * r
        v = v + d[:, :256]
        for e in range(2):
            out[:, 8 * e : 8 * e + 8, :] = v[128 * e : 128 * e + 128].reshape(16, 8, 256)

    return call(body, [(16, 16, 256)], consts, (s, r, d, below, above))[0]


def fetch(value, axis, offset):
    count = lax.axis_size(axis)
    return lax.ppermute(value, axis, [((i + offset) % count, i) for i in range(count)])


def both(low, high, offset=1):
    return fetch(high, "gx", -offset), fetch(low, "gx", offset)


def local(source):
    from_right = fetch(source[:, :, :128], "gy", 1)
    from_left = fetch(source[:, :, 128:], "gy", -1)
    b, low, high = fine_rhs(source, from_right, from_left)
    x, r, d, low, high = fine_middle(b, *both(low, high))
    x0, r0, b, r1, low, high = fine_last(x, r, d, *both(low, high))
    chunk, lo, hi, lo2, hi2 = mid_last(b, r1, *both(low, high))
    gathered = lax.all_to_all(chunk, ("gx", "gy"), 0, 0, tiled=True)
    s, r, d, low, high = second_smoothing(
        gathered, x0, r0, lo, hi, *both(lo, hi), *both(lo2, hi2, 2)
    )
    return last_step(s, r, d, *both(low, high))


def solution(mesh):
    return jax.shard_map(
        local,
        mesh=mesh,
        in_specs=(P(None, "gx", "gy"),),
        out_specs=P(None, "gx", "gy"),
        check_vma=False,
    )
```

time: 138 us -> 95.3 us (0.69)
  starting transfers between devices: 68.9 us -> 50.2 us
  waiting for transfers between devices: 28.8 us -> 16.4 us
  local copies, waits for them, and re-layouts: 16.1 us -> 8.98 us
  other arithmetic: 2.49 us -> 0 us
    ppermute x20 -> x14, waiting for transfers between devices: 28.8 us -> 10.9 us  [fetch(): lax.ppermute(value, axis, [((i + offset) % count, i) for i in range(count)])]
    ppermute x20 -> x14, starting transfers between devices: 53.1 us -> 38.2 us  [fetch(): lax.ppermute(value, axis, [((i + offset) % count, i) for i in range(count)])]
    pallas_call x1 -> x0, Pallas kernels: 8.32 us -> none  [post(): pl.pallas_call(kernel, out_shape=jax.ShapeDtypeStruct((16, 16, 256), f32)...]
    pallas_call x3 -> x6, Pallas kernels: 11.9 us -> 19.2 us  [call(): pl.pallas_call(kernel, out_shape=[jax.ShapeDtypeStruct(s, f32) for s in o...]
    unnamed x108 -> x27, local copies, waits for them, and re-layouts: 13.8 us -> 6.72 us
    all_to_all x1, waiting for transfers between devices: 0.01 us -> 5.54 us  [local(): gathered = lax.all_to_all(chunk, ('gx', 'gy'), 0, 0, tiled=True)]
    all_to_all x1, starting transfers between devices: 15.8 us -> 12 us  [local(): gathered = lax.all_to_all(chunk, ('gx', 'gy'), 0, 0, tiled=True)]
    concatenate x7 -> x0, other arithmetic: 2.43 us -> none  [the longest x1 2.31 us: local(): fine_r = jnp.concatenate([r0m, r0, r0p], axis=0)]
  transfers between devices with their start and end apart: 21 -> 15, of which waited for: 7 -> 7; matrix products, arithmetic and copies ran while one was open for 3% -> 0% of each run, Pallas kernels for 1% -> 0%
where the time goes in v2:
time: 95.3 us; the launch traced here: 94.9 us
  starting transfers between devices  50.2 us (53%)
  Pallas kernels  19.2 us (20%)
  waiting for transfers between devices  16.4 us (17%)
  local copies, waits for them, and re-layouts  8.98 us (9%)
    ppermute x14, starting transfers between devices, fetch(): lax.ppermute(value, axis, [((i + offset) % count, i) for i in range(count)])  38.2 us
    pallas_call x6, Pallas kernels, call(): pl.pallas_call(kernel, out_shape=[jax.ShapeDtypeStruct(s, f32) for s in o...  19.2 us
    all_to_all x1, starting transfers between devices, local(): gathered = lax.all_to_all(chunk, ('gx', 'gy'), 0, 0, tiled=True)  12 us
    ppermute x14, waiting for transfers between devices, fetch(): lax.ppermute(value, axis, [((i + offset) % count, i) for i in range(count)])  10.9 us
    unnamed x27, local copies, waits for them, and re-layouts  6.72 us
    all_to_all x1, waiting for transfers between devices, local(): gathered = lax.all_to_all(chunk, ('gx', 'gy'), 0, 0, tiled=True)  5.54 us
  transfers between devices with their start and end apart: 15, of which 7 were waited for; matrix products, arithmetic and copies ran while one was open for 0% of the time, Pallas kernels for 0%

profile of v2, /device:TPU:1, one launch (start us, length us, event | category | flops | bytes accessed | tf_op | source)
XLA Modules:
  0.0 94.9 jit_solution(9718479287566627823)
XLA Ops:
  0.0 1.1 %fusion = (f32[16,16,128]{2,1,0:T(8,128)S(1)}, f32[16,16,128]{2,1,0:T(8,128)S(1)}) fusion(f32[16,16,256]{2,1,0:T(8,128)} %refs_2_.1), kind=kLoop, calls=%fused_computation.1 | loop fusion | bytes 524288 | tf_op jit(solution)/shard_map/slice | solution.py:835
  1.1 2.6 %collective-permute-start.1 = (f32[16,16,128]{2,1,0:T(8,128)S(1)}, f32[16,16,128]{2,1,0:T(8,128)S(1)}, u32[]{:S(2)}, u32[]{:S(2)}) collective-permute-start(f32[16,16,128]{2,1,0:T(8,128)S(1)} %get-tuple-element.53), channel_id=1, source_target_pairs={{7,0},{0,1},{1,2},{2,3},{3,4},{4,5},{5,6},{6,7},{15,8},{8,9},{9,10... | collective-permute-start | bytes 393224 | tf_op jit(solution)/shard_map/ppermute | solution.py:826
  3.7 0.7 collective-permute-start
  4.4 1.3 %collective-permute-done.1.refs_4_ = f32[16,16,128]{2,1,0:T(8,128)S(1)} collective-permute-done((f32[16,16,128]{2,1,0:T(8,128)S(1)}, f32[16,16,128]{2,1,0:T(8,128)S(1)}, u32[]{:S(2)}, u32[]{:S(2)}) %collective-permute-start.1) | collective-permute-done | bytes 131104 | tf_op jit(solution)/shard_map/ppermute | solution.py:826
  5.7 2.7 %collective-permute-done.refs_3_ = f32[16,16,128]{2,1,0:T(8,128)S(1)} collective-permute-done((f32[16,16,128]{2,1,0:T(8,128)S(1)}, f32[16,16,128]{2,1,0:T(8,128)S(1)}, u32[]{:S(2)}, u32[]{:S(2)}) %collective-permute-start) | collective-permute-done | bytes 131104 | tf_op jit(solution)/shard_map/ppermute | solution.py:826
  8.4 0.9 copy-done.5
  9.4 0.9 copy-done.11
  10.3 0.8 copy-done.12
  11.0 0.6 shard_map.127
  11.6 1.4 %collective-permute-start.2 = (f32[32,512]{1,0:T(8,128)S(1)}, f32[32,512]{1,0:T(8,128)S(1)}, u32[]{:S(2)}, u32[]{:S(2)}) collective-permute-start(f32[32,512]{1,0:T(8,128)S(1)} %get-tuple-element.30), channel_id=1, source_target_pairs={{248,0},{0,8},{8,16},{16,24},{24,32},{32,40},{40,48},{48,56},{56,6... | collective-permute-start | bytes 196616 | tf_op jit(solution)/shard_map/ppermute | solution.py:826
  13.0 6.5 %collective-permute-start.3 = (f32[32,512]{1,0:T(8,128)S(1)}, f32[32,512]{1,0:T(8,128)S(1)}, u32[]{:S(2)}, u32[]{:S(2)}) collective-permute-start(f32[32,512]{1,0:T(8,128)S(1)} %get-tuple-element.31), channel_id=1, source_target_pairs={{8,0},{16,8},{24,16},{32,24},{40,32},{48,40},{56,48},{64,56},{72,6... | collective-permute-start | bytes 196616 | tf_op jit(solution)/shard_map/ppermute | solution.py:826
  19.5 2.3 %collective-permute-done.2.refs_3_ = f32[32,512]{1,0:T(8,128)S(1)} collective-permute-done((f32[32,512]{1,0:T(8,128)S(1)}, f32[32,512]{1,0:T(8,128)S(1)}, u32[]{:S(2)}, u32[]{:S(2)}) %collective-permute-start.2) | collective-permute-done | bytes 65568 | tf_op jit(solution)/shard_map/ppermute | solution.py:826
  21.7 1.0 %copy-done.3 = f32[528,128]{1,0:T(8,128)S(1)} copy-done((f32[528,128]{1,0:T(8,128)S(1)}, f32[528,128]{1,0:T(8,128)}, u32[]{:S(2)}) %copy-start.3) | copy-done | bytes 270360
  22.7 1.1 %copy-done.6 = bf16[2560,128]{1,0:T(8,128)(2,1)S(1)} copy-done((bf16[2560,128]{1,0:T(8,128)(2,1)S(1)}, bf16[2560,128]{1,0:T(8,128)(2,1)}, u32[]{:S(2)}) %copy-start.6) | copy-done | bytes 655384
  23.8 3.5 %shard_map.128 = (f32[256,256]{1,0:T(8,128)S(1)}, f32[256,512]{1,0:T(8,128)S(1)}, f32[256,512]{1,0:T(8,128)S(1)}, f32[48,512]{1,0:T(8,128)S(1)}, f32[48,512]{1,0:T(8,128)S(1)}) custom-call(f32[528,128]{1,0:T(8,128)S(1)} %copy-done.3, bf16[2560,128]{1,0:T(8,128)(2,1)S(1)} %copy-done.6, f32[256,512]{1,0:T(8,128)S(1)} %get-tuple-element.29.refs_2_, ...), custom_call_target="tpu_custom_call" | custom-call | tf_op jit(solution)/shard_map/pallas_call | solution.py:371
  27.3 4.8 %collective-permute-start.5 = (f32[48,512]{1,0:T(8,128)S(1)}, f32[48,512]{1,0:T(8,128)S(1)}, u32[]{:S(2)}, u32[]{:S(2)}) collective-permute-start(f32[48,512]{1,0:T(8,128)S(1)} %get-tuple-element.36), channel_id=1, source_target_pairs={{8,0},{16,8},{24,16},{32,24},{40,32},{48,40},{56,48},{64,56},{72,6... | collective-permute-start | bytes 294920 | tf_op jit(solution)/shard_map/ppermute | solution.py:826
  32.1 2.0 %collective-permute-done.4.refs_5_ = f32[48,512]{1,0:T(8,128)S(1)} collective-permute-done((f32[48,512]{1,0:T(8,128)S(1)}, f32[48,512]{1,0:T(8,128)S(1)}, u32[]{:S(2)}, u32[]{:S(2)}) %collective-permute-start.4) | collective-permute-done | bytes 98336 | tf_op jit(solution)/shard_map/ppermute | solution.py:826
  34.1 2.4 %shard_map.129 = (f32[256,256]{1,0:T(8,128)S(1)}, f32[256,384]{1,0:T(8,128)S(1)}, f32[64,256]{1,0:T(8,128)S(1)}, f32[64,256]{1,0:T(8,128)S(1)}, f32[16,256]{1,0:T(8,128)S(1)}, /*index=5*/f32[16,256]{1,0:T(8,128)S(1)}) custom-call(f32[816,128]{1,0:T(8,128)S(1)} %copy-done.9, bf16[6048,128]{1,0:T(8,128)(2,1)S(1)} %copy-done.1, ...), custom_call_target="tpu_custom_call" | custom-call | tf_op jit(solution)/shard_map/pallas_call | solution.py:371
  36.5 4.8 %collective-permute-start.7 = (f32[16,256]{1,0:T(8,128)S(1)}, f32[16,256]{1,0:T(8,128)S(1)}, u32[]{:S(2)}, u32[]{:S(2)}) collective-permute-start(f32[16,256]{1,0:T(8,128)S(1)} %get-tuple-element.40), channel_id=1, source_target_pairs={{8,0},{16,8},{24,16},{32,24},{40,32},{48,40},{56,48},{64,56},{72,6... | collective-permute-start | bytes 49160 | tf_op jit(solution)/shard_map/ppermute | solution.py:826
  41.3 1.1 %collective-permute-done.6.refs_4_ = f32[16,256]{1,0:T(8,128)S(1)} collective-permute-done((f32[16,256]{1,0:T(8,128)S(1)}, f32[16,256]{1,0:T(8,128)S(1)}, u32[]{:S(2)}, u32[]{:S(2)}) %collective-permute-start.6) | collective-permute-done | bytes 16416 | tf_op jit(solution)/shard_map/ppermute | solution.py:826
  42.4 1.1 %shard_map.130 = (f32[256,384]{1,0:T(8,128)S(1)}, f32[104,256]{1,0:T(8,128)S(1)}, f32[104,256]{1,0:T(8,128)S(1)}, f32[16,256]{1,0:T(8,128)S(1)}, f32[16,256]{1,0:T(8,128)S(1)}) custom-call(f32[288,128]{1,0:T(8,128)S(1)} %copy-done.10, bf16[6016,128]{1,0:T(8,128)(2,1)S(1)} %copy-done.2, f32[64,256]{1,0:T(8,128)S(1)} %get-tuple-element.37.refs_2_, ...), custom_call_target="tpu_custom_call" | custom-call | tf_op jit(solution)/shard_map/pallas_call | solution.py:371
  43.6 1.2 %copy.14 = f32[256,1,384]{2,1,0:T(1,128)} copy(f32[256,1,384]{2,0,1:T(8,128)S(1)} %bitcast.5) | data formatting | bytes 786432 | tf_op jit(solution)/shard_map/all_to_all | solution.py:840
  44.7 12.0 %all-to-all-start = ((f32[256,1,384]{2,1,0:T(1,128)}), f32[256,1,384]{2,1,0:T(1,128)S(1)}, u32[]{:S(2)}, u32[]{:S(2)}) async-start(f32[256,1,384]{2,1,0:T(1,128)} %copy.14), calls=%async_computation | async-start | bytes 786432 | tf_op jit(solution)/shard_map/all_to_all | solution.py:840
  56.8 6.9 %collective-permute-start.9 = (f32[104,256]{1,0:T(8,128)S(1)}, f32[104,256]{1,0:T(8,128)S(1)}, u32[]{:S(2)}, u32[]{:S(2)}) collective-permute-start(f32[104,256]{1,0:T(8,128)S(1)} %get-tuple-element.44.refs_5_), channel_id=1, source_target_pairs={{8,0},{16,8},{24,16},{32,24},{40,32},{48,40},{56,48},{64,56},{72,6... | collective-permute-start | bytes 319496 | tf_op jit(solution)/shard_map/ppermute | solution.py:826
  63.7 5.7 %collective-permute-start.11 = (f32[16,256]{1,0:T(8,128)S(1)}, f32[16,256]{1,0:T(8,128)S(1)}, u32[]{:S(2)}, u32[]{:S(2)}) collective-permute-start(f32[16,256]{1,0:T(8,128)S(1)} %get-tuple-element.47), channel_id=1, source_target_pairs={{16,0},{24,8},{32,16},{40,24},{48,32},{56,40},{64,48},{72,56},{80,... | collective-permute-start | bytes 49160 | tf_op jit(solution)/shard_map/ppermute | solution.py:826
  69.4 5.5 %all-to-all-done = f32[256,1,384]{2,1,0:T(1,128)S(1)} async-done(((f32[256,1,384]{2,1,0:T(1,128)}), f32[256,1,384]{2,1,0:T(1,128)S(1)}, u32[]{:S(2)}, u32[]{:S(2)}) %all-to-all-start) | async-done | bytes 393248 | tf_op jit(solution)/shard_map/all_to_all | solution.py:840
  75.0 2.0 %copy-done = bf16[14048,128]{1,0:T(8,128)(2,1)S(1)} copy-done((bf16[14048,128]{1,0:T(8,128)(2,1)S(1)}, bf16[14048,128]{1,0:T(8,128)(2,1)}, u32[]{:S(2)}) %copy-start) | copy-done | bytes 3596312
  77.0 10.0 %shard_map.131 = (f32[256,256]{1,0:T(8,128)S(1)}, f32[256,384]{1,0:T(8,128)S(1)}, f32[256,384]{1,0:T(8,128)S(1)}, f32[32,384]{1,0:T(8,128)S(1)}, f32[32,384]{1,0:T(8,128)S(1)}) custom-call(f32[832,128]{1,0:T(8,128)S(1)} %copy-done.8, bf16[14048,128]{1,0:T(8,128)(2,1)S(1)} %copy-done, f32[256,384]{1,0:T(8,128)S(1)} %bitcast.4, ...), custom_call_target="tpu_custom_call" | custom-call | tf_op jit(solution)/shard_map/pallas_call | solution.py:371
  87.1 0.7 collective-permute-start.12
  87.7 4.2 %collective-permute-start.13 = (f32[32,384]{1,0:T(8,128)S(1)}, f32[32,384]{1,0:T(8,128)S(1)}, u32[]{:S(2)}, u32[]{:S(2)}) collective-permute-start(f32[32,384]{1,0:T(8,128)S(1)} %get-tuple-element.52), channel_id=1, source_target_pairs={{8,0},{16,8},{24,16},{32,24},{40,32},{48,40},{56,48},{64,56},{72,6... | collective-permute-start | bytes 147464 | tf_op jit(solution)/shard_map/ppermute | solution.py:826
  91.9 1.5 %collective-permute-done.12.refs_5_ = f32[32,384]{1,0:T(8,128)S(1)} collective-permute-done((f32[32,384]{1,0:T(8,128)S(1)}, f32[32,384]{1,0:T(8,128)S(1)}, u32[]{:S(2)}, u32[]{:S(2)}) %collective-permute-start.12) | collective-permute-done | bytes 49184 | tf_op jit(solution)/shard_map/ppermute | solution.py:826
  93.4 1.6 %shard_map.132 = f32[16,16,256]{2,1,0:T(8,128)} custom-call(f32[528,128]{1,0:T(8,128)S(1)} %copy-done.4, bf16[2176,128]{1,0:T(8,128)(2,1)S(1)} %copy-done.7, f32[256,256]{1,0:T(8,128)S(1)} %get-tuple-element.48.refs_2_, f32[256,384]{1,0:T(8,128)S(1)} %get-tuple-element.49.refs_3_, f32[256,384]{1,0:T(8,128)S(1)} %get-tuple-element.50.refs_4_, ...), custom_call_target="tpu_custom_call" | custom-call | tf_op jit(solution)/shard_map/pallas_call | solution.py:371
  (33 shorter events, 0.1 us)
Async XLA Ops:
  0.0 34.1 %copy-start.1 = (bf16[6048,128]{1,0:T(8,128)(2,1)S(1)}, bf16[6048,128]{1,0:T(8,128)(2,1)}, u32[]{:S(2)}) copy-start(bf16[6048,128]{1,0:T(8,128)(2,1)} %constant.27.clone.refs_1_) | copy-start | bytes 4644868
  1.1 4.6 %collective-permute-start.1 = (f32[16,16,128]{2,1,0:T(8,128)S(1)}, f32[16,16,128]{2,1,0:T(8,128)S(1)}, u32[]{:S(2)}, u32[]{:S(2)}) collective-permute-start(f32[16,16,128]{2,1,0:T(8,128)S(1)} %get-tuple-element.53), channel_id=1, source_target_pairs={{7,0},{0,1},{1,2},{2,3},{3,4},{4,5},{5,6},{6,7},{15,8},{8,9},{9,10... | collective-permute-start | bytes 393224 | tf_op jit(solution)/shard_map/ppermute | solution.py:826
  3.7 4.7 %collective-permute-start = (f32[16,16,128]{2,1,0:T(8,128)S(1)}, f32[16,16,128]{2,1,0:T(8,128)S(1)}, u32[]{:S(2)}, u32[]{:S(2)}) collective-permute-start(f32[16,16,128]{2,1,0:T(8,128)S(1)} %get-tuple-element.54), channel_id=1, source_target_pairs={{1,0},{2,1},{3,2},{4,3},{5,4},{6,5},{7,6},{0,7},{9,8},{10,9},{11,1... | collective-permute-start | bytes 393224 | tf_op jit(solution)/shard_map/ppermute | solution.py:826
  8.4 1.0 %copy-start.5 = (f32[16,16,256]{2,1,0:T(8,128)S(1)}, f32[16,16,256]{2,1,0:T(8,128)}, u32[]{:S(2)}) copy-start(f32[16,16,256]{2,1,0:T(8,128)} %refs_2_.1) | copy-start | bytes 786436
  9.4 0.9 copy-start.11
  10.3 0.8 copy-start.12
  11.6 10.2 %collective-permute-start.2 = (f32[32,512]{1,0:T(8,128)S(1)}, f32[32,512]{1,0:T(8,128)S(1)}, u32[]{:S(2)}, u32[]{:S(2)}) collective-permute-start(f32[32,512]{1,0:T(8,128)S(1)} %get-tuple-element.30), channel_id=1, source_target_pairs={{248,0},{0,8},{8,16},{16,24},{24,32},{32,40},{40,48},{48,56},{56,6... | collective-permute-start | bytes 196616 | tf_op jit(solution)/shard_map/ppermute | solution.py:826
  13.0 8.7 %collective-permute-start.3 = (f32[32,512]{1,0:T(8,128)S(1)}, f32[32,512]{1,0:T(8,128)S(1)}, u32[]{:S(2)}, u32[]{:S(2)}) collective-permute-start(f32[32,512]{1,0:T(8,128)S(1)} %get-tuple-element.31), channel_id=1, source_target_pairs={{8,0},{16,8},{24,16},{32,24},{40,32},{48,40},{56,48},{64,56},{72,6... | collective-permute-start | bytes 196616 | tf_op jit(solution)/shard_map/ppermute | solution.py:826
  21.7 1.0 %copy-start.3 = (f32[528,128]{1,0:T(8,128)S(1)}, f32[528,128]{1,0:T(8,128)}, u32[]{:S(2)}) copy-start(f32[528,128]{1,0:T(8,128)} %constant.24.clone.refs_0_) | copy-start | bytes 811012
  22.7 1.1 %copy-start.6 = (bf16[2560,128]{1,0:T(8,128)(2,1)S(1)}, bf16[2560,128]{1,0:T(8,128)(2,1)}, u32[]{:S(2)}) copy-start(bf16[2560,128]{1,0:T(8,128)(2,1)} %constant.25.clone.refs_1_) | copy-start | bytes 1966084
  23.8 10.3 %copy-start.9 = (f32[816,128]{1,0:T(8,128)S(1)}, f32[816,128]{1,0:T(8,128)}, u32[]{:S(2)}) copy-start(f32[816,128]{1,0:T(8,128)} %constant.26.clone.refs_0_) | copy-start | bytes 1253380
  27.3 6.8 %collective-permute-start.4 = (f32[48,512]{1,0:T(8,128)S(1)}, f32[48,512]{1,0:T(8,128)S(1)}, u32[]{:S(2)}, u32[]{:S(2)}) collective-permute-start(f32[48,512]{1,0:T(8,128)S(1)} %get-tuple-element.35), channel_id=1, source_target_pairs={{248,0},{0,8},{8,16},{16,24},{24,32},{32,40},{40,48},{48,56},{56,6... | collective-permute-start | bytes 294920 | tf_op jit(solution)/shard_map/ppermute | solution.py:826
  27.3 6.8 %collective-permute-start.5 = (f32[48,512]{1,0:T(8,128)S(1)}, f32[48,512]{1,0:T(8,128)S(1)}, u32[]{:S(2)}, u32[]{:S(2)}) collective-permute-start(f32[48,512]{1,0:T(8,128)S(1)} %get-tuple-element.36), channel_id=1, source_target_pairs={{8,0},{16,8},{24,16},{32,24},{40,32},{48,40},{56,48},{64,56},{72,6... | collective-permute-start | bytes 294920 | tf_op jit(solution)/shard_map/ppermute | solution.py:826
  34.1 8.3 %copy-start.2 = (bf16[6016,128]{1,0:T(8,128)(2,1)S(1)}, bf16[6016,128]{1,0:T(8,128)(2,1)}, u32[]{:S(2)}) copy-start(bf16[6016,128]{1,0:T(8,128)(2,1)} %constant.29.clone.refs_1_) | copy-start | bytes 4620292
  34.1 8.3 %copy-start.10 = (f32[288,128]{1,0:T(8,128)S(1)}, f32[288,128]{1,0:T(8,128)}, u32[]{:S(2)}) copy-start(f32[288,128]{1,0:T(8,128)} %constant.28.clone.refs_0_) | copy-start | bytes 442372
  36.5 5.9 %collective-permute-start.6 = (f32[16,256]{1,0:T(8,128)S(1)}, f32[16,256]{1,0:T(8,128)S(1)}, u32[]{:S(2)}, u32[]{:S(2)}) collective-permute-start(f32[16,256]{1,0:T(8,128)S(1)} %get-tuple-element.39), channel_id=1, source_target_pairs={{248,0},{0,8},{8,16},{16,24},{24,32},{32,40},{40,48},{48,56},{56,6... | collective-permute-start | bytes 49160 | tf_op jit(solution)/shard_map/ppermute | solution.py:826
  36.5 5.9 %collective-permute-start.7 = (f32[16,256]{1,0:T(8,128)S(1)}, f32[16,256]{1,0:T(8,128)S(1)}, u32[]{:S(2)}, u32[]{:S(2)}) collective-permute-start(f32[16,256]{1,0:T(8,128)S(1)} %get-tuple-element.40), channel_id=1, source_target_pairs={{8,0},{16,8},{24,16},{32,24},{40,32},{48,40},{56,48},{64,56},{72,6... | collective-permute-start | bytes 49160 | tf_op jit(solution)/shard_map/ppermute | solution.py:826
  43.6 31.4 %copy-start.8 = (f32[832,128]{1,0:T(8,128)S(1)}, f32[832,128]{1,0:T(8,128)}, u32[]{:S(2)}) copy-start(f32[832,128]{1,0:T(8,128)} %constant.30.clone.refs_0_) | copy-start | bytes 1277956
  44.7 30.2 %all-to-all-start = ((f32[256,1,384]{2,1,0:T(1,128)}), f32[256,1,384]{2,1,0:T(1,128)S(1)}, u32[]{:S(2)}, u32[]{:S(2)}) async-start(f32[256,1,384]{2,1,0:T(1,128)} %copy.14), calls=%async_computation | async-start | bytes 786432 | tf_op jit(solution)/shard_map/all_to_all | solution.py:840
  56.8 18.2 %collective-permute-start.9 = (f32[104,256]{1,0:T(8,128)S(1)}, f32[104,256]{1,0:T(8,128)S(1)}, u32[]{:S(2)}, u32[]{:S(2)}) collective-permute-start(f32[104,256]{1,0:T(8,128)S(1)} %get-tuple-element.44.refs_5_), channel_id=1, source_target_pairs={{8,0},{16,8},{24,16},{32,24},{40,32},{48,40},{56,48},{64,56},{72,6... | collective-permute-start | bytes 319496 | tf_op jit(solution)/shard_map/ppermute | solution.py:826
  63.7 11.3 %collective-permute-start.8 = (f32[104,256]{1,0:T(8,128)S(1)}, f32[104,256]{1,0:T(8,128)S(1)}, u32[]{:S(2)}, u32[]{:S(2)}) collective-permute-start(f32[104,256]{1,0:T(8,128)S(1)} %get-tuple-element.45.refs_6_), channel_id=1, source_target_pairs={{248,0},{0,8},{8,16},{16,24},{24,32},{32,40},{40,48},{48,56},{56,6... | collective-permute-start | bytes 319496 | tf_op jit(solution)/shard_map/ppermute | solution.py:826
  63.7 11.3 %collective-permute-start.10 = (f32[16,256]{1,0:T(8,128)S(1)}, f32[16,256]{1,0:T(8,128)S(1)}, u32[]{:S(2)}, u32[]{:S(2)}) collective-permute-start(f32[16,256]{1,0:T(8,128)S(1)} %get-tuple-element.46), channel_id=1, source_target_pairs={{240,0},{248,8},{0,16},{8,24},{16,32},{24,40},{32,48},{40,56},{48,... | collective-permute-start | bytes 49160 | tf_op jit(solution)/shard_map/ppermute | solution.py:826
  63.7 11.3 %collective-permute-start.11 = (f32[16,256]{1,0:T(8,128)S(1)}, f32[16,256]{1,0:T(8,128)S(1)}, u32[]{:S(2)}, u32[]{:S(2)}) collective-permute-start(f32[16,256]{1,0:T(8,128)S(1)} %get-tuple-element.47), channel_id=1, source_target_pairs={{16,0},{24,8},{32,16},{40,24},{48,32},{56,40},{64,48},{72,56},{80,... | collective-permute-start | bytes 49160 | tf_op jit(solution)/shard_map/ppermute | solution.py:826
  75.0 2.0 %copy-start = (bf16[14048,128]{1,0:T(8,128)(2,1)S(1)}, bf16[14048,128]{1,0:T(8,128)(2,1)}, u32[]{:S(2)}) copy-start(bf16[14048,128]{1,0:T(8,128)(2,1)} %constant.31.clone.refs_1_) | copy-start | bytes 10788868
  77.0 16.3 %copy-start.4 = (f32[528,128]{1,0:T(8,128)S(1)}, f32[528,128]{1,0:T(8,128)}, u32[]{:S(2)}) copy-start(f32[528,128]{1,0:T(8,128)} %constant.24.clone.refs_0_) | copy-start | bytes 811012
  77.0 16.3 %copy-start.7 = (bf16[2176,128]{1,0:T(8,128)(2,1)S(1)}, bf16[2176,128]{1,0:T(8,128)(2,1)}, u32[]{:S(2)}) copy-start(bf16[2176,128]{1,0:T(8,128)(2,1)} %constant.32.clone.refs_1_) | copy-start | bytes 1671172
  87.1 6.3 %collective-permute-start.12 = (f32[32,384]{1,0:T(8,128)S(1)}, f32[32,384]{1,0:T(8,128)S(1)}, u32[]{:S(2)}, u32[]{:S(2)}) collective-permute-start(f32[32,384]{1,0:T(8,128)S(1)} %get-tuple-element.51), channel_id=1, source_target_pairs={{248,0},{0,8},{8,16},{16,24},{24,32},{32,40},{40,48},{48,56},{56,6... | collective-permute-start | bytes 147464 | tf_op jit(solution)/shard_map/ppermute | solution.py:826
  87.7 5.6 %collective-permute-start.13 = (f32[32,384]{1,0:T(8,128)S(1)}, f32[32,384]{1,0:T(8,128)S(1)}, u32[]{:S(2)}, u32[]{:S(2)}) collective-permute-start(f32[32,384]{1,0:T(8,128)S(1)} %get-tuple-element.52), channel_id=1, source_target_pairs={{8,0},{16,8},{24,16},{32,24},{40,32},{48,40},{56,48},{64,56},{72,6... | collective-permute-start | bytes 147464 | tf_op jit(solution)/shard_map/ppermute | solution.py:826

commit v3 on v2

--- a/solution.py
+++ b/solution.py
@@ -359,8 +359,15 @@
     return arrays, places
 
 
-def call(body, outs, consts, args, scratch=(), vmem=24):
-    arrays, places = packed(consts)
+def ready(held):
+    def body(c, ins, outs):
+        outs[0][...] = jnp.zeros((8, 128), f32)
+
+    return call(body, [(8, 128)], held, ())[0]
+
+
+def call(body, outs, held, args, scratch=(), vmem=24):
+    arrays, places = held
     n, k = len(arrays), len(args)
 
     def kernel(*refs):
@@ -375,33 +382,27 @@
         out_specs=[spec] * len(outs),
         scratch_shapes=list(scratch),
         compiler_params=pltpu.CompilerParams(vmem_limit_bytes=vmem * MB),
-    )(*[jnp.asarray(a) for a in arrays], *args)
-
-
-def fine_rhs(source, from_right, from_left):
-    c = fine_constants()
+    )(*arrays, *args)
+
+
+def under(c, prefix):
+    return {k[2:]: v for k, v in c.items() if k.startswith(prefix)}
+
+
+def rhs_tables(consts):
     w = np.kron(np.tile(FINE.w, 2), FINE.w)[:, None] * np.tile(FINE.w, 16)[None, :]
-    consts = dict(w=(0.125 * w).astype(np.float32), d1=c["d1"])
-    pair(consts, "pl", plane_matrix(8, *inner_lines(FINE)))
-
+    consts["w"] = (0.125 * w).astype(np.float32)
+
+
+def fine_rhs(held, first, second, from_right, from_left, at_hand):
     def body(c, ins, outs):
-        source, from_right, from_left = ins
+        parts = ins[:4]
         b_out, low, high = outs
         w = tiles(c["w"], 1, 4)
         src = []
         for e in range(2):
             s = slice(8 * e, 8 * e + 8)
-            src.append(
-                jnp.concatenate(
-                    [
-                        source[:, s, :].reshape(128, 256),
-                        from_right[:, s, :].reshape(128, 128),
-                        from_left[:, s, :].reshape(128, 128),
-                    ],
-                    axis=1,
-                )
-                * w
-            )
+            src.append(jnp.concatenate([v[:, s, :].reshape(128, 128) for v in parts], axis=1) * w)
         b = []
         for y in (row_sum(None, src[0], src[1]), row_sum(src[0], src[1], None)):
             y = col_sum(y)
@@ -411,14 +412,17 @@
         face1 = b[1].reshape(16, 8, 512)[:, 7, :]
         b = jnp.concatenate(b, axis=0)
         b_out[...] = b
-        planes = left(c, "pl", split(tiles(c["d1"], 2, 4) * b))
+        planes = left(c, "f_pl", split(tiles(c["f_d1"], 2, 4) * b))
         low[0:16] = face0
         low[16:32] = planes[:16]
         high[0:16] = face1
         high[16:32] = planes[16:]
 
     return call(
-        body, [(256, 512), (32, 512), (32, 512)], consts, (source, from_right, from_left)
+        body,
+        [(256, 512), (32, 512), (32, 512)],
+        held,
+        (first, second, from_right, from_left, at_hand),
     )
 
 
@@ -426,19 +430,22 @@
     return jnp.concatenate([low[at : at + rows], high[at : at + rows]], axis=0)
 
 
-def fine_middle(b, below, above):
-    consts = own_constants()
+def middle_tables(consts):
     consts["f"] = plane_matrix(8, np.eye(8)[0], np.eye(8)[7]).T.astype(ml_dtypes.bfloat16)
     inside = np.ones(8)
     inside[0] = inside[7] = 0.0
     pair(consts, "q", plane_matrix(8, J_FINE[:, 0] * inside, J_FINE[:, 3] * inside))
 
+
+def fine_middle(held, b, below, above):
     def body(c, ins, outs):
         b, below, above = ins
         x_out, r_out, d_out, low, high = outs
         h, l = split(faced(below, above, 0, 16))
         f = c["f"][...]
         b = b[...] + dot(f, h) + dot(f, l)
+        q = {"h": c["qh"], "l": c["ql"]}
+        c = under(c, "f_")
         d1, d2, d3 = (tiles(c[k], 2, 4) for k in ("d1", "d2", "d3"))
         d = d1 * b
         x = d
@@ -457,7 +464,7 @@
         node = row % 8
         outer = ((row < 128) & (node == 0)) | ((row >= 128) & (node == 7))
         r = r - fine_own(split(jnp.where(outer, 0.0, d)), c)
-        plane3 = left(c, "q", split(r))
+        plane3 = left(q, "", split(r))
         for k, plane in enumerate((plane1, plane2, plane3)):
             low[16 * k : 16 * k + 16] = plane[:16]
             high[16 * k : 16 * k + 16] = plane[16:]
@@ -465,14 +472,12 @@
     return call(
         body,
         [(256, 256), (256, 512), (256, 512), (48, 512), (48, 512)],
-        consts,
+        held,
         (b, below, above),
     )
 
 
-def fine_last(x, r, d, below, above):
-    consts = {"f_" + k: v for k, v in own_constants().items()}
-    consts.update({"m_" + k: v for k, v in mid_own_constants().items()})
+def last_tables(consts):
     kappa = float(np.sum(J_FINE[1:7, 0] * FINE.k[1:7, 0]))
     t = kappa * plane_matrix(8, np.eye(8)[0], np.eye(8)[7])
     pair(consts, "e", t * np.tile(0.5 * FINE.w_z, 2)[:, None])
@@ -489,11 +494,12 @@
     t = sum_matrix(64, 4, True) @ blocks(J_FINE.T @ np.diag(FINE.m_p), 64)
     pair(consts, "rc", t.T)
 
+
+def fine_last(held, x, r, d, below, above):
     def body(c, ins, outs):
         x, r, d, below, above = ins
         x0, r0, b_out, r1_out, low, high = outs
-        f = {k[2:]: v for k, v in c.items() if k.startswith("f_")}
-        m = {k[2:]: v for k, v in c.items() if k.startswith("m_")}
+        f, m = under(c, "f_"), under(c, "m_")
         wc = tiles(f["wc"], 1, 4)
         change = wc * left(f, "pf", split(faced(below, above, 0, 16)))
         r = r[...] - change
@@ -521,13 +527,12 @@
     return call(
         body,
         [(256, 256), (256, 384), (64, 256), (64, 256), (16, 256), (16, 256)],
-        consts,
+        held,
         (x, r, d, below, above),
     )
 
 
-def mid_last(b, r1, below, above):
-    consts = mid_own_constants()
+def share_tables(consts):
     top = np.zeros((3, 4))
     top[0, 0] = top[1, 1] = top[1, 2] = top[2, 3] = 1.0
     jz = top @ blocks(J_MID.T, 2)
@@ -545,7 +550,7 @@
             t[4 * v : 4 * v + 4, v] += (J_MID.T @ part)[0]
             at = (4 * v - 4) % 256
             t[at : at + 4, v] += (J_MID.T @ part)[1]
-        return np.tile(t, (1, 12))
+        return np.tile(t, (1, 4))
 
     wz, wr = blocks(np.diag(MID.w), 2), np.diag(MID.w)
     kz = blocks(MID.k, 2)
@@ -562,8 +567,11 @@
         np.concatenate([across(np.diag(MID.m_p)), -across(wr), -across(MID.k)], axis=0),
     )
 
+
+def mid_last(held, b, r1, below, above):
     def body(c, ins, outs):
         b, r1, below, above = ins
+        down, c = c, under(c, "m_")
         chunk, lo, hi, lo2, hi2 = outs
         d1, d2, d3 = (tiles(c[k], 2, 1) for k in ("d1", "d2", "d3"))
         d = d1 * b[...]
@@ -576,13 +584,13 @@
         x = x + d
         parts = split(d)
         t = jnp.concatenate(
-            [left(c, "sm", split(r)), left(c, "s1", parts), left(c, "s2", parts)], axis=1
+            [left(down, "sm", split(r)), left(down, "s1", parts), left(down, "s2", parts)], axis=1
         )
-        t = right(c, "sc", split(t))
+        t = right(down, "sc", split(t))
+        t = jnp.concatenate([t, t, t], axis=1)
         q = lax.broadcasted_iota(jnp.int32, t.shape, 0)
         lane = lax.broadcasted_iota(jnp.int32, t.shape, 1) // 32
-        t = jnp.sum(jnp.where(q == lane, t, 0.0), axis=0, keepdims=True)
-        chunk[...] = jnp.broadcast_to(t, chunk.shape)
+        chunk[...] = jnp.sum(jnp.where(q == lane, t, 0.0), axis=0, keepdims=True)
         plane1 = left(c, "pl", parts)
         r = r - mid_own(d, c)
         plane2 = left(c, "pl", split(d1 * r))
@@ -595,30 +603,31 @@
 
     return call(
         body,
-        [(256, 384), (104, 256), (104, 256), (16, 256), (16, 256)],
-        consts,
+        [(1, 384), (104, 256), (104, 256), (16, 256), (16, 256)],
+        held,
         (b, r1, below, above),
     )
 
 
-def coarse_constants():
-    kz = np.zeros((4, 4))
-    kz[:3, :3] = [[0.5, -0.5, 0.0], [-0.5, 1.0, -0.5], [0.0, -0.5, 0.5]]
-    wz = np.array([1.0, 2.0, 1.0, 0.0])
-    near = np.eye(32, k=1) + np.eye(32, k=-1)
-    inner = 2.0 * np.kron(kz, np.eye(32)) + np.kron(np.diag(wz), 2.0 * np.eye(32) - 0.5 * near)
-    up, down = np.zeros((32, 32)), np.zeros((32, 32))
-    up[0, 31] = -0.5
-    down[31, 0] = -0.5
-    matrix = np.concatenate([inner, np.kron(np.diag(wz), up), np.kron(np.diag(wz), down)], axis=0)
-    return dict(
-        g_m=matrix.astype(ml_dtypes.bfloat16),
-        g_wz=np.repeat(wz, 32)[None, :].astype(np.float32),
-    )
-
-
-def coarse_solve(g, c):
-    m, wz = c["g_m"][...], c["g_wz"][...]
+def coarse_operator():
+    row = lax.broadcasted_iota(jnp.int32, (128, 128), 0)
+    lane = lax.broadcasted_iota(jnp.int32, (128, 128), 1)
+    z, z2 = row >> 5, lane >> 5
+    apart = jnp.abs((row & 31) - (lane & 31))
+    w = jnp.where(z == 1, 2.0, jnp.where(z == 3, 0.0, 1.0))
+    w = jnp.where(z == z2, w, 0.0)
+    next_plane = (jnp.abs(z - z2) == 1) & (z + z2 < 5)
+    inner = jnp.where(apart == 0, 3.0 * w - next_plane.astype(f32), 0.0)
+    inner = inner - jnp.where(apart == 1, 0.5 * w, 0.0)
+    ends = jnp.where(apart == 31, -0.5 * w, 0.0)
+    m = jnp.concatenate([inner, ends], axis=1).astype(bf16)
+    return jnp.concatenate([m, m], axis=0)
+
+
+def coarse_solve(g):
+    m = coarse_operator()
+    plane = lax.broadcasted_iota(jnp.int32, (1, 128), 1) // 32
+    wz = jnp.where(plane == 1, 2.0, jnp.where(plane == 3, 0.0, 1.0))
 
     def after(u):
         return jnp.concatenate([u[8:], u[:8]], axis=0)
@@ -626,30 +635,17 @@
     def before(u):
         return jnp.concatenate([u[-8:], u[:-8]], axis=0)
 
-    def shifted(u, by):
-        return pltpu.roll(u.reshape(32, 8, 128), by, 1).reshape(256, 128)
+    column = lax.broadcasted_iota(jnp.int32, (32, 8, 128), 2) % 32
 
     def columns(u):
-        a = u.astype(bf16)
-        rest = u - a.astype(f32)
-        b = rest.astype(bf16)
-        e = (rest - b.astype(f32)).astype(bf16)
-        t = None
-        for part in (a, b, e):
-            wide_part = part.astype(f32)
-            v = dot(
-                jnp.concatenate(
-                    [
-                        part,
-                        shifted(wide_part, 7).astype(bf16),
-                        shifted(wide_part, 1).astype(bf16),
-                    ],
-                    axis=1,
-                ),
-                m,
-            )
-            t = v if t is None else t + v
-        return t
+        t = dot(jnp.concatenate(split(u), axis=1), m)
+        ends = t[:, 128:].reshape(32, 8, 128)
+        ends = jnp.where(
+            column == 31,
+            pltpu.roll(ends, 7, 1),
+            jnp.where(column == 0, pltpu.roll(ends, 1, 1), 0.0),
+        )
+        return t[:, :128] + ends.reshape(256, 128)
 
     half = -0.5 * wz
     mass = 4.0 * mass_coef * wz
@@ -682,26 +678,20 @@
     return jnp.concatenate(x, axis=1)
 
 
-def second_smoothing(gathered, x0, r0, own_lo, own_hi, below, above, below2, above2):
-    consts = coarse_constants()
-    consts.update({"f_" + k: v for k, v in own_constants().items()})
-    consts.update({"m_" + k: v for k, v in mid_constants().items()})
-    pair(consts, "a", window_operator(MID, 10))
+def second_tables(consts):
+    pair(consts, "a", window_operator(MID, 6))
     pair(consts, "c", closed_operator(MID, 6))
-    pair(consts, "p6", face_matrix(MID, 6))
-    pair(consts, "p3", blocks(face_matrix(MID), 3))
+    pair(consts, "p", np.concatenate([blocks(face_matrix(MID), 3), face_matrix(MID, 6)], axis=1))
     low, high = inner_lines(MID)
-    pair(consts, "pl", plane_matrix(4, high, low))
-    jc = np.zeros((3, 3, 4, 32, 256))
+    pair(consts, "po", plane_matrix(4, high, low))
+    jc = np.zeros((4, 32, 256))
     for e in range(64):
         element = e if e < 48 else e - 64
         for k in range(2):
             v = element + k
             dev, col = v // 32 + 1, v % 32
-            for z in range(3):
-                jc[z, dev, z, col, 4 * e : 4 * e + 4] = J_MID[:, k]
-    jc = jc.reshape(3, 384, 256)
-    pair(consts, "vc", np.concatenate([jc[0], jc[1], jc[2]], axis=1))
+            jc[dev, col, 4 * e : 4 * e + 4] = J_MID[:, k]
+    pair(consts, "vc", jc.reshape(128, 256))
     jz = np.zeros((8, 3))
     jz[:4, :2] += J_MID
     jz[4:, 1:] += J_MID
@@ -711,45 +701,54 @@
             jdr[e, :, :, :, e + k] += np.einsum("zp,a->zap", jz, J_MID[:, k])
     order = [2 * (q % 8) + q // 8 for q in range(16)]
     pair(consts, "vd", jdr[..., order].reshape(320, 48))
-    fc = np.zeros((256, 384))
-    for e in range(48):
-        src = e if e < 40 else e + 16
+    pair(consts, "fo", blocks(J_FINE.T, 32))
+    fc = np.zeros((128, 128))
+    for e in range(16):
+        src = e if e < 8 else e + 16
         fc[4 * src : 4 * src + 4, 8 * e : 8 * e + 8] = J_FINE.T
-    pair(consts, "fc", fc)
+    pair(consts, "fh", fc)
     fd = np.kron(blocks(J_FINE, 2), J_FINE)
     pair(consts, "fd", blocks(fd, 2))
     low, high = inner_lines(FINE)
     pair(consts, "fp", plane_matrix(8, high, low) @ blocks(fd, 2))
 
+
+def second_smoothing(held, gathered, x0, r0, own_lo, own_hi, below, above, below2, above2):
     def body(c, ins, outs):
         gathered, x0, r0, own_lo, own_hi, below, above, below2, above2 = ins
-        s_out, r_out, d_out, low, high, twice, rows = outs
+        s_out, r_out, d_out, low, high, twice = outs
         i, j = lax.axis_index("gx"), lax.axis_index("gy")
-        f = {k[2:]: v for k, v in c.items() if k.startswith("f_")}
-        m = {k[2:]: v for k, v in c.items() if k.startswith("m_")}
-        x2 = coarse_solve(gathered, c)
+        f, m = under(c, "f_"), under(c, "m_")
+        x2 = coarse_solve(gathered)
         twice[0:256] = x2
         twice[256:512] = x2
         first = lax.rem(i + 30, 32)
         picked = twice[pl.ds(pl.multiple_of(first * 8, 8), 64), :].reshape(8, 8, 256)
         sub = lax.broadcasted_iota(jnp.int32, (8, 8, 256), 1)
+        near = []
         for g in range(3):
             v = jnp.sum(jnp.where(sub == lax.rem(j + 7 + g, 8), picked, 0.0), axis=1)
-            for k in range(2):
-                rows[8 * k : 8 * k + 8, 128 * g : 128 * g + 128] = v[:, 128 * k : 128 * k + 128]
-        y = right(c, "vc", split(rows[...]))
-        y = jnp.concatenate([y[:, :256], y[:, 256:512], y[:, 512:]], axis=0)
+            near.append(jnp.concatenate([v[:, :128], v[:, 128:]], axis=0))
+        block = lax.broadcasted_iota(jnp.int32, (16, 128), 1) // 32
+        y = []
+        for z in range(3):
+            v = [pltpu.roll(near[g], (32 * (g - z)) % 128, 1) if g != z else near[g] for g in range(3)]
+            y.append(
+                jnp.where(block == 0, v[0], jnp.where(block == 1, v[1], jnp.where(block == 2, v[2], 0.0)))
+            )
+        y = right(c, "vc", split(jnp.concatenate(y, axis=0)))
         e2 = left(c, "vd", split(y))
 
-        def window(u, size):
+        def window(u):
             h, l = split(u)
-            th, tl = c["ah"][:size, : size + 64], c["al"][:size, : size + 64]
-            t = dot(th, h) + dot(th, l) + dot(tl, h)
-            return mid_apply(t, (h[32:-32], l[32:-32]), m)
+            t = [left(c, "a", (h[k : k + 192], l[k : k + 192])) for k in range(0, len(u) - 64, 128)]
+            return mid_apply(jnp.concatenate(t, axis=0), (h[32:-32], l[32:-32]), m)
 
         def table(name, count):
             return tiles(m[name], count, 1)
 
+        p3 = {"h": c["ph"][:, :48], "l": c["pl"][:, :48]}
+        p6 = {"h": c["ph"][:, 48:], "l": c["pl"][:, 48:]}
         planes = jnp.concatenate(
             [
                 below2[:8],
@@ -761,22 +760,29 @@
             ],
             axis=0,
         )
-        g = window(e2, 256)
+        g = window(e2)
         r = jnp.concatenate([below[:64], own_lo[:64], above[:64]], axis=0)
-        r = r - m["wc"][...] * left(c, "p3", split(planes)) - g[32:224]
+        r = r - m["wc"][...] * left(p3, "", split(planes)) - g[32:224]
         d = table("d1", 6) * r
         x = jnp.concatenate([below[72:104], own_lo[72:104], own_hi[72:104], above[72:104]], axis=0)
         x = x + e2[96:224] + d[32:160]
         outer = jnp.concatenate([g[:32], g[224:]], axis=0) * table("d1", 2)
-        planes = faced(below2, above2, 8, 8) - left(c, "pl", split(outer))
+        planes = faced(below2, above2, 8, 8) - left(c, "po", split(outer))
         parts = split(d)
-        r = r - mid_apply(left(c, "c", parts) + left(c, "p6", split(planes)), parts, m)
+        r = r - mid_apply(left(c, "c", parts) + left(p6, "", split(planes)), parts, m)
         d = MID.steps[0][0] * d + table("d2", 6) * r
         x = x + d[32:160]
-        r = r[32:160] - window(d, 128)
+        r = r[32:160] - window(d)
         d = MID.steps[1][0] * d[32:160] + table("d3", 4) * r
         x = x + d
-        x = right(c, "fc", split(x))
+        h, l = split(x)
+        x = jnp.concatenate(
+            [
+                right(c, "fo", (h[:, :128], l[:, :128])),
+                right(c, "fh", (h[:, 128:], l[:, 128:])),
+            ],
+            axis=1,
+        )
         e1 = left(c, "fd", split(x[32:96]))
         planes = left(c, "fp", split(jnp.concatenate([x[:32], x[96:]], axis=0)))
         r = r0[...] - fine_own(split(e1), f, planes)
@@ -796,16 +802,15 @@
     return call(
         body,
         [(256, 256), (256, 384), (256, 384), (32, 384), (32, 384)],
-        consts,
+        held,
         (gathered, x0, r0, own_lo, own_hi, below, above, below2, above2),
-        scratch=[pltpu.VMEM((512, 256), f32), pltpu.VMEM((16, 384), f32)],
-    )
-
-
-def last_step(s, r, d, below, above):
-    consts = own_constants()
-
+        scratch=[pltpu.VMEM((512, 256), f32)],
+    )
+
+
+def last_step(held, s, r, d, below, above):
     def body(c, ins, outs):
+        c = under(c, "f_")
         s, r, d, below, above = ins
         (out,) = outs
         change = tiles(c["wc"], 1, 3) * left(c, "pf", split(faced(below, above, 0, 16)))
@@ -818,7 +823,7 @@
         for e in range(2):
             out[:, 8 * e : 8 * e + 8, :] = v[128 * e : 128 * e + 128].reshape(16, 8, 256)
 
-    return call(body, [(16, 16, 256)], consts, (s, r, d, below, above))[0]
+    return call(body, [(16, 16, 256)], held, (s, r, d, below, above))[0]
 
 
 def fetch(value, axis, offset):
@@ -830,18 +835,29 @@
     return fetch(high, "gx", -offset), fetch(low, "gx", offset)
 
 
+def tables(*adds, mid=mid_own_constants):
+    consts = {"f_" + k: v for k, v in own_constants().items()}
+    consts.update({"m_" + k: v for k, v in mid().items()})
+    for add in adds:
+        add(consts)
+    arrays, places = packed(consts)
+    return [jnp.asarray(a) for a in arrays], places
+
+
 def local(source):
-    from_right = fetch(source[:, :, :128], "gy", 1)
-    from_left = fetch(source[:, :, 128:], "gy", -1)
-    b, low, high = fine_rhs(source, from_right, from_left)
-    x, r, d, low, high = fine_middle(b, *both(low, high))
-    x0, r0, b, r1, low, high = fine_last(x, r, d, *both(low, high))
-    chunk, lo, hi, lo2, hi2 = mid_last(b, r1, *both(low, high))
+    first, second = source[:, :, :128], source[:, :, 128:]
+    from_right, from_left = fetch(first, "gy", 1), fetch(second, "gy", -1)
+    held = tables(rhs_tables, middle_tables, last_tables, share_tables)
+    b, low, high = fine_rhs(held, first, second, from_right, from_left, ready(held))
+    x, r, d, low, high = fine_middle(held, b, *both(low, high))
+    x0, r0, b, r1, low, high = fine_last(held, x, r, d, *both(low, high))
+    chunk, lo, hi, lo2, hi2 = mid_last(held, b, r1, *both(low, high))
+    chunk = jnp.broadcast_to(chunk, (lax.axis_size("gx") * lax.axis_size("gy"), 384))
     gathered = lax.all_to_all(chunk, ("gx", "gy"), 0, 0, tiled=True)
     s, r, d, low, high = second_smoothing(
-        gathered, x0, r0, lo, hi, *both(lo, hi), *both(lo2, hi2, 2)
-    )
-    return last_step(s, r, d, *both(low, high))
+        tables(second_tables, mid=mid_constants), gathered, x0, r0, lo, hi, *both(lo, hi), *both(lo2, hi2, 2)
+    )
+    return last_step(tables(mid=dict), s, r, d, *both(low, high))
 
 
 def solution(mesh):

time: 95.3 us -> 87 us (0.913)
  local copies, waits for them, and re-layouts: 8.98 us -> 5.58 us
  waiting for transfers between devices: 16.4 us -> 13 us
  Pallas kernels: 19.2 us -> 16.8 us
    unnamed x27 -> x13, local copies, waits for them, and re-layouts: 6.72 us -> 3.65 us
    ppermute x14, waiting for transfers between devices: 10.9 us -> 8.25 us  [fetch(): lax.ppermute(value, axis, [((i + offset) % count, i) for i in range(count)])]
    pallas_call x6 -> x7, Pallas kernels: 19.2 us -> 16.8 us  [call(): pl.pallas_call(kernel, out_shape=[jax.ShapeDtypeStruct(s, f32) for s in o...]
    all_to_all x1 -> x0, local copies, waits for them, and re-layouts: 1.16 us -> none  [local(): gathered = lax.all_to_all(chunk, ('gx', 'gy'), 0, 0, tiled=True)]
  transfers between devices with their start and end apart: 15 -> 15, of which waited for: 7 -> 6; matrix products, arithmetic and copies ran while one was open for 0% -> 1% of each run, Pallas kernels for 0% -> 0%
where the time goes in v3:
time: 87 us; the launch traced here: 86.7 us
  starting transfers between devices  51.1 us (59%)
  Pallas kernels  16.8 us (19%)
  waiting for transfers between devices  13 us (15%)
  local copies, waits for them, and re-layouts  5.58 us (6%)
    ppermute x14, starting transfers between devices, fetch(): lax.ppermute(value, axis, [((i + offset) % count, i) for i in range(count)])  38.2 us
    pallas_call x7, Pallas kernels, call(): pl.pallas_call(kernel, out_shape=[jax.ShapeDtypeStruct(s, f32) for s in o...  16.8 us
    all_to_all x1, starting transfers between devices, local(): gathered = lax.all_to_all(chunk, ('gx', 'gy'), 0, 0, tiled=True)  12.9 us
    ppermute x14, waiting for transfers between devices, fetch(): lax.ppermute(value, axis, [((i + offset) % count, i) for i in range(count)])  8.25 us
    all_to_all x1, waiting for transfers between devices, local(): gathered = lax.all_to_all(chunk, ('gx', 'gy'), 0, 0, tiled=True)  4.78 us
    unnamed x13, local copies, waits for them, and re-layouts  3.65 us
  transfers between devices with their start and end apart: 15, of which 6 were waited for; matrix products, arithmetic and copies ran while one was open for 1% of the time, Pallas kernels for 0%

profile of v3, /device:TPU:1, one launch (start us, length us, event | category | flops | bytes accessed | tf_op | source)
XLA Modules:
  0.0 86.7 jit_solution(9063992803355145391)
XLA Ops:
  0.0 1.0 %fusion = (f32[16,16,128]{2,1,0:T(8,128)S(1)}, f32[16,16,128]{2,1,0:T(8,128)S(1)}) fusion(f32[16,16,256]{2,1,0:T(8,128)} %param.7), kind=kLoop, calls=%fused_computation.1 | loop fusion | bytes 524288 | tf_op jit(solution)/shard_map/slice | solution.py:848
  1.0 2.6 %collective-permute-start.1 = (f32[16,16,128]{2,1,0:T(8,128)S(1)}, f32[16,16,128]{2,1,0:T(8,128)S(1)}, u32[]{:S(2)}, u32[]{:S(2)}) collective-permute-start(f32[16,16,128]{2,1,0:T(8,128)S(1)} %get-tuple-element.53.refs_3_), channel_id=1, source_target_pairs={{7,0},{0,1},{1,2},{2,3},{3,4},{4,5},{5,6},{6,7},{15,8},{8,9},{9,10... | collective-permute-start | bytes 393224 | tf_op jit(solution)/shard_map/ppermute | solution.py:831
  3.6 0.7 collective-permute-start
  4.3 1.6 %copy-done = bf16[8064,128]{1,0:T(8,128)(2,1)S(1)} copy-done((bf16[8064,128]{1,0:T(8,128)(2,1)S(1)}, bf16[8064,128]{1,0:T(8,128)(2,1)}, u32[]{:S(2)}) %copy-start) | copy-done | bytes 2064408
  5.8 1.0 %copy-done.1 = f32[944,128]{1,0:T(8,128)S(1)} copy-done((f32[944,128]{1,0:T(8,128)S(1)}, f32[944,128]{1,0:T(8,128)}, u32[]{:S(2)}) %copy-start.1) | copy-done | bytes 483352
  6.9 1.4 %collective-permute-done.refs_4_ = f32[16,16,128]{2,1,0:T(8,128)S(1)} collective-permute-done((f32[16,16,128]{2,1,0:T(8,128)S(1)}, f32[16,16,128]{2,1,0:T(8,128)S(1)}, u32[]{:S(2)}, u32[]{:S(2)}) %collective-permute-start) | collective-permute-done | bytes 131104 | tf_op jit(solution)/shard_map/ppermute | solution.py:831
  8.3 0.6 shard_map.74
  8.8 1.4 %collective-permute-start.2 = (f32[32,512]{1,0:T(8,128)S(1)}, f32[32,512]{1,0:T(8,128)S(1)}, u32[]{:S(2)}, u32[]{:S(2)}) collective-permute-start(f32[32,512]{1,0:T(8,128)S(1)} %get-tuple-element.30), channel_id=1, source_target_pairs={{248,0},{0,8},{8,16},{16,24},{24,32},{32,40},{40,48},{48,56},{56,6... | collective-permute-start | bytes 196616 | tf_op jit(solution)/shard_map/ppermute | solution.py:831
  10.3 6.5 %collective-permute-start.3 = (f32[32,512]{1,0:T(8,128)S(1)}, f32[32,512]{1,0:T(8,128)S(1)}, u32[]{:S(2)}, u32[]{:S(2)}) collective-permute-start(f32[32,512]{1,0:T(8,128)S(1)} %get-tuple-element.31), channel_id=1, source_target_pairs={{8,0},{16,8},{24,16},{32,24},{40,32},{48,40},{56,48},{64,56},{72,6... | collective-permute-start | bytes 196616 | tf_op jit(solution)/shard_map/ppermute | solution.py:831
  16.7 2.3 %collective-permute-done.2.refs_3_ = f32[32,512]{1,0:T(8,128)S(1)} collective-permute-done((f32[32,512]{1,0:T(8,128)S(1)}, f32[32,512]{1,0:T(8,128)S(1)}, u32[]{:S(2)}, u32[]{:S(2)}) %collective-permute-start.2) | collective-permute-done | bytes 65568 | tf_op jit(solution)/shard_map/ppermute | solution.py:831
  19.0 0.0 collective-permute-done.3.refs_4_
  19.0 3.4 %shard_map.75 = (f32[256,256]{1,0:T(8,128)S(1)}, f32[256,512]{1,0:T(8,128)S(1)}, f32[256,512]{1,0:T(8,128)S(1)}, f32[48,512]{1,0:T(8,128)S(1)}, f32[48,512]{1,0:T(8,128)S(1)}) custom-call(f32[944,128]{1,0:T(8,128)S(1)} %copy-done.1, bf16[8064,128]{1,0:T(8,128)(2,1)S(1)} %copy-done, f32[256,512]{1,0:T(8,128)S(1)} %get-tuple-element.29.refs_2_, ...), custom_call_target="tpu_custom_call" | custom-call | tf_op jit(solution)/shard_map/pallas_call | solution.py:378
  22.5 0.0 collective-permute-start.4
  22.5 4.8 %collective-permute-start.5 = (f32[48,512]{1,0:T(8,128)S(1)}, f32[48,512]{1,0:T(8,128)S(1)}, u32[]{:S(2)}, u32[]{:S(2)}) collective-permute-start(f32[48,512]{1,0:T(8,128)S(1)} %get-tuple-element.36), channel_id=1, source_target_pairs={{8,0},{16,8},{24,16},{32,24},{40,32},{48,40},{56,48},{64,56},{72,6... | collective-permute-start | bytes 294920 | tf_op jit(solution)/shard_map/ppermute | solution.py:831
  27.2 2.0 %collective-permute-done.4.refs_5_ = f32[48,512]{1,0:T(8,128)S(1)} collective-permute-done((f32[48,512]{1,0:T(8,128)S(1)}, f32[48,512]{1,0:T(8,128)S(1)}, u32[]{:S(2)}, u32[]{:S(2)}) %collective-permute-start.4) | collective-permute-done | bytes 98336 | tf_op jit(solution)/shard_map/ppermute | solution.py:831
  29.2 2.4 %shard_map.76 = (f32[256,256]{1,0:T(8,128)S(1)}, f32[256,384]{1,0:T(8,128)S(1)}, f32[64,256]{1,0:T(8,128)S(1)}, f32[64,256]{1,0:T(8,128)S(1)}, f32[16,256]{1,0:T(8,128)S(1)}, /*index=5*/f32[16,256]{1,0:T(8,128)S(1)}) custom-call(f32[944,128]{1,0:T(8,128)S(1)} %copy-done.1, bf16[8064,128]{1,0:T(8,128)(2,1)S(1)} %copy-done, ...), custom_call_target="tpu_custom_call" | custom-call | tf_op jit(solution)/shard_map/pallas_call | solution.py:378
  31.6 4.8 %collective-permute-start.7 = (f32[16,256]{1,0:T(8,128)S(1)}, f32[16,256]{1,0:T(8,128)S(1)}, u32[]{:S(2)}, u32[]{:S(2)}) collective-permute-start(f32[16,256]{1,0:T(8,128)S(1)} %get-tuple-element.40), channel_id=1, source_target_pairs={{8,0},{16,8},{24,16},{32,24},{40,32},{48,40},{56,48},{64,56},{72,6... | collective-permute-start | bytes 49160 | tf_op jit(solution)/shard_map/ppermute | solution.py:831
  36.5 1.1 %collective-permute-done.6.refs_4_ = f32[16,256]{1,0:T(8,128)S(1)} collective-permute-done((f32[16,256]{1,0:T(8,128)S(1)}, f32[16,256]{1,0:T(8,128)S(1)}, u32[]{:S(2)}, u32[]{:S(2)}) %collective-permute-start.6) | collective-permute-done | bytes 16416 | tf_op jit(solution)/shard_map/ppermute | solution.py:831
  37.6 1.0 %shard_map.77 = (f32[1,384]{1,0:T(1,128)S(1)}, f32[104,256]{1,0:T(8,128)S(1)}, f32[104,256]{1,0:T(8,128)S(1)}, f32[16,256]{1,0:T(8,128)S(1)}, f32[16,256]{1,0:T(8,128)S(1)}) custom-call(f32[944,128]{1,0:T(8,128)S(1)} %copy-done.1, bf16[8064,128]{1,0:T(8,128)(2,1)S(1)} %copy-done, f32[64,256]{1,0:T(8,128)S(1)} %get-tuple-element.37.refs_2_, ...), custom_call_target="tpu_custom_call" | custom-call | tf_op jit(solution)/shard_map/pallas_call | solution.py:378
  38.6 0.9 %broadcast_in_dim.2 = f32[256,1,384]{2,1,0:T(1,128)} broadcast(f32[384]{0:T(512)S(1)} %reduce), dimensions={2} | broadcast | bytes 394752 | tf_op jit(solution)/shard_map/broadcast_in_dim | solution.py:855
  39.6 12.9 %all-to-all-start = ((f32[256,1,384]{2,1,0:T(1,128)}), f32[256,1,384]{2,1,0:T(1,128)}, u32[]{:S(2)}, u32[]{:S(2)}) async-start(f32[256,1,384]{2,1,0:T(1,128)} %broadcast_in_dim.2), calls=%async_computation | async-start | bytes 786432 | tf_op jit(solution)/shard_map/all_to_all | solution.py:856
  52.5 6.9 %collective-permute-start.9 = (f32[104,256]{1,0:T(8,128)S(1)}, f32[104,256]{1,0:T(8,128)S(1)}, u32[]{:S(2)}, u32[]{:S(2)}) collective-permute-start(f32[104,256]{1,0:T(8,128)S(1)} %get-tuple-element.44.refs_5_), channel_id=1, source_target_pairs={{8,0},{16,8},{24,16},{32,24},{40,32},{48,40},{56,48},{64,56},{72,6... | collective-permute-start | bytes 319496 | tf_op jit(solution)/shard_map/ppermute | solution.py:831
  59.4 5.7 %collective-permute-start.11 = (f32[16,256]{1,0:T(8,128)S(1)}, f32[16,256]{1,0:T(8,128)S(1)}, u32[]{:S(2)}, u32[]{:S(2)}) collective-permute-start(f32[16,256]{1,0:T(8,128)S(1)} %get-tuple-element.47), channel_id=1, source_target_pairs={{16,0},{24,8},{32,16},{40,24},{48,32},{56,40},{64,48},{72,56},{80,... | collective-permute-start | bytes 49160 | tf_op jit(solution)/shard_map/ppermute | solution.py:831
  65.1 4.8 %all-to-all-done = f32[256,1,384]{2,1,0:T(1,128)} async-done(((f32[256,1,384]{2,1,0:T(1,128)}), f32[256,1,384]{2,1,0:T(1,128)}, u32[]{:S(2)}, u32[]{:S(2)}) %all-to-all-start) | async-done | bytes 393248 | tf_op jit(solution)/shard_map/all_to_all | solution.py:856
  69.8 1.0 %copy.10 = f32[256,1,384]{2,0,1:T(8,128)S(1)} copy(f32[256,1,384]{2,1,0:T(1,128)} %all-to-all-done) | data formatting | bytes 786432
  70.9 0.0 copy-start.3
  70.9 0.0 copy-start.5
  70.9 7.9 %shard_map.78 = (f32[256,256]{1,0:T(8,128)S(1)}, f32[256,384]{1,0:T(8,128)S(1)}, f32[256,384]{1,0:T(8,128)S(1)}, f32[32,384]{1,0:T(8,128)S(1)}, f32[32,384]{1,0:T(8,128)S(1)}) custom-call(f32[816,128]{1,0:T(8,128)S(1)} %copy-done.4, bf16[7392,128]{1,0:T(8,128)(2,1)S(1)} %copy-done.2, f32[256,384]{1,0:T(8,128)S(1)} %bitcast.3, ...), custom_call_target="tpu_custom_call" | custom-call | tf_op jit(solution)/shard_map/pallas_call | solution.py:378
  78.8 0.6 collective-permute-start.12
  79.4 4.2 %collective-permute-start.13 = (f32[32,384]{1,0:T(8,128)S(1)}, f32[32,384]{1,0:T(8,128)S(1)}, u32[]{:S(2)}, u32[]{:S(2)}) collective-permute-start(f32[32,384]{1,0:T(8,128)S(1)} %get-tuple-element.52), channel_id=1, source_target_pairs={{8,0},{16,8},{24,16},{32,24},{40,32},{48,40},{56,48},{64,56},{72,6... | collective-permute-start | bytes 147464 | tf_op jit(solution)/shard_map/ppermute | solution.py:831
  83.6 1.5 %collective-permute-done.12.refs_5_ = f32[32,384]{1,0:T(8,128)S(1)} collective-permute-done((f32[32,384]{1,0:T(8,128)S(1)}, f32[32,384]{1,0:T(8,128)S(1)}, u32[]{:S(2)}, u32[]{:S(2)}) %collective-permute-start.12) | collective-permute-done | bytes 49184 | tf_op jit(solution)/shard_map/ppermute | solution.py:831
  85.1 1.6 %shard_map.79 = f32[16,16,256]{2,1,0:T(8,128)} custom-call(f32[528,128]{1,0:T(8,128)S(1)} %copy-done.5, bf16[2176,128]{1,0:T(8,128)(2,1)S(1)} %copy-done.3, f32[256,256]{1,0:T(8,128)S(1)} %get-tuple-element.48.refs_2_, f32[256,384]{1,0:T(8,128)S(1)} %get-tuple-element.49.refs_3_, f32[256,384]{1,0:T(8,128)S(1)} %get-tuple-element.50.refs_4_, ...), custom_call_target="tpu_custom_call" | custom-call | tf_op jit(solution)/shard_map/pallas_call | solution.py:378
  (21 shorter events, 0.1 us)
Async XLA Ops:
  1.0 5.9 %collective-permute-start.1 = (f32[16,16,128]{2,1,0:T(8,128)S(1)}, f32[16,16,128]{2,1,0:T(8,128)S(1)}, u32[]{:S(2)}, u32[]{:S(2)}) collective-permute-start(f32[16,16,128]{2,1,0:T(8,128)S(1)} %get-tuple-element.53.refs_3_), channel_id=1, source_target_pairs={{7,0},{0,1},{1,2},{2,3},{3,4},{4,5},{5,6},{6,7},{15,8},{8,9},{9,10... | collective-permute-start | bytes 393224 | tf_op jit(solution)/shard_map/ppermute | solution.py:831
  3.6 4.7 %collective-permute-start = (f32[16,16,128]{2,1,0:T(8,128)S(1)}, f32[16,16,128]{2,1,0:T(8,128)S(1)}, u32[]{:S(2)}, u32[]{:S(2)}) collective-permute-start(f32[16,16,128]{2,1,0:T(8,128)S(1)} %get-tuple-element.54.refs_2_), channel_id=1, source_target_pairs={{1,0},{2,1},{3,2},{4,3},{5,4},{6,5},{7,6},{0,7},{9,8},{10,9},{11,1... | collective-permute-start | bytes 393224 | tf_op jit(solution)/shard_map/ppermute | solution.py:831
  4.3 1.6 %copy-start = (bf16[8064,128]{1,0:T(8,128)(2,1)S(1)}, bf16[8064,128]{1,0:T(8,128)(2,1)}, u32[]{:S(2)}) copy-start(bf16[8064,128]{1,0:T(8,128)(2,1)} %constant.13.clone.refs_1_) | copy-start | bytes 6193156
  5.8 1.0 %copy-start.1 = (f32[944,128]{1,0:T(8,128)S(1)}, f32[944,128]{1,0:T(8,128)}, u32[]{:S(2)}) copy-start(f32[944,128]{1,0:T(8,128)} %constant.12.clone.refs_0_) | copy-start | bytes 1449988
  8.8 10.2 %collective-permute-start.2 = (f32[32,512]{1,0:T(8,128)S(1)}, f32[32,512]{1,0:T(8,128)S(1)}, u32[]{:S(2)}, u32[]{:S(2)}) collective-permute-start(f32[32,512]{1,0:T(8,128)S(1)} %get-tuple-element.30), channel_id=1, source_target_pairs={{248,0},{0,8},{8,16},{16,24},{24,32},{32,40},{40,48},{48,56},{56,6... | collective-permute-start | bytes 196616 | tf_op jit(solution)/shard_map/ppermute | solution.py:831
  10.3 8.7 %collective-permute-start.3 = (f32[32,512]{1,0:T(8,128)S(1)}, f32[32,512]{1,0:T(8,128)S(1)}, u32[]{:S(2)}, u32[]{:S(2)}) collective-permute-start(f32[32,512]{1,0:T(8,128)S(1)} %get-tuple-element.31), channel_id=1, source_target_pairs={{8,0},{16,8},{24,16},{32,24},{40,32},{48,40},{56,48},{64,56},{72,6... | collective-permute-start | bytes 196616 | tf_op jit(solution)/shard_map/ppermute | solution.py:831
  22.5 6.8 %collective-permute-start.4 = (f32[48,512]{1,0:T(8,128)S(1)}, f32[48,512]{1,0:T(8,128)S(1)}, u32[]{:S(2)}, u32[]{:S(2)}) collective-permute-start(f32[48,512]{1,0:T(8,128)S(1)} %get-tuple-element.35), channel_id=1, source_target_pairs={{248,0},{0,8},{8,16},{16,24},{24,32},{32,40},{40,48},{48,56},{56,6... | collective-permute-start | bytes 294920 | tf_op jit(solution)/shard_map/ppermute | solution.py:831
  22.5 6.8 %collective-permute-start.5 = (f32[48,512]{1,0:T(8,128)S(1)}, f32[48,512]{1,0:T(8,128)S(1)}, u32[]{:S(2)}, u32[]{:S(2)}) collective-permute-start(f32[48,512]{1,0:T(8,128)S(1)} %get-tuple-element.36), channel_id=1, source_target_pairs={{8,0},{16,8},{24,16},{32,24},{40,32},{48,40},{56,48},{64,56},{72,6... | collective-permute-start | bytes 294920 | tf_op jit(solution)/shard_map/ppermute | solution.py:831
  31.6 5.9 %collective-permute-start.6 = (f32[16,256]{1,0:T(8,128)S(1)}, f32[16,256]{1,0:T(8,128)S(1)}, u32[]{:S(2)}, u32[]{:S(2)}) collective-permute-start(f32[16,256]{1,0:T(8,128)S(1)} %get-tuple-element.39), channel_id=1, source_target_pairs={{248,0},{0,8},{8,16},{16,24},{24,32},{32,40},{40,48},{48,56},{56,6... | collective-permute-start | bytes 49160 | tf_op jit(solution)/shard_map/ppermute | solution.py:831
  31.6 5.9 %collective-permute-start.7 = (f32[16,256]{1,0:T(8,128)S(1)}, f32[16,256]{1,0:T(8,128)S(1)}, u32[]{:S(2)}, u32[]{:S(2)}) collective-permute-start(f32[16,256]{1,0:T(8,128)S(1)} %get-tuple-element.40), channel_id=1, source_target_pairs={{8,0},{16,8},{24,16},{32,24},{40,32},{48,40},{56,48},{64,56},{72,6... | collective-permute-start | bytes 49160 | tf_op jit(solution)/shard_map/ppermute | solution.py:831
  37.6 33.4 %copy-start.2 = (bf16[7392,128]{1,0:T(8,128)(2,1)S(1)}, bf16[7392,128]{1,0:T(8,128)(2,1)}, u32[]{:S(2)}) copy-start(bf16[7392,128]{1,0:T(8,128)(2,1)} %constant.15.clone.refs_1_) | copy-start | bytes 5677060
  37.6 33.4 %copy-start.4 = (f32[816,128]{1,0:T(8,128)S(1)}, f32[816,128]{1,0:T(8,128)}, u32[]{:S(2)}) copy-start(f32[816,128]{1,0:T(8,128)} %constant.14.clone.refs_0_) | copy-start | bytes 1253380
  39.6 30.3 %all-to-all-start = ((f32[256,1,384]{2,1,0:T(1,128)}), f32[256,1,384]{2,1,0:T(1,128)}, u32[]{:S(2)}, u32[]{:S(2)}) async-start(f32[256,1,384]{2,1,0:T(1,128)} %broadcast_in_dim.2), calls=%async_computation | async-start | bytes 786432 | tf_op jit(solution)/shard_map/all_to_all | solution.py:856
  52.5 18.4 %collective-permute-start.9 = (f32[104,256]{1,0:T(8,128)S(1)}, f32[104,256]{1,0:T(8,128)S(1)}, u32[]{:S(2)}, u32[]{:S(2)}) collective-permute-start(f32[104,256]{1,0:T(8,128)S(1)} %get-tuple-element.44.refs_5_), channel_id=1, source_target_pairs={{8,0},{16,8},{24,16},{32,24},{40,32},{48,40},{56,48},{64,56},{72,6... | collective-permute-start | bytes 319496 | tf_op jit(solution)/shard_map/ppermute | solution.py:831
  59.4 11.6 %collective-permute-start.8 = (f32[104,256]{1,0:T(8,128)S(1)}, f32[104,256]{1,0:T(8,128)S(1)}, u32[]{:S(2)}, u32[]{:S(2)}) collective-permute-start(f32[104,256]{1,0:T(8,128)S(1)} %get-tuple-element.45.refs_6_), channel_id=1, source_target_pairs={{248,0},{0,8},{8,16},{16,24},{24,32},{32,40},{40,48},{48,56},{56,6... | collective-permute-start | bytes 319496 | tf_op jit(solution)/shard_map/ppermute | solution.py:831
  59.4 11.5 %collective-permute-start.10 = (f32[16,256]{1,0:T(8,128)S(1)}, f32[16,256]{1,0:T(8,128)S(1)}, u32[]{:S(2)}, u32[]{:S(2)}) collective-permute-start(f32[16,256]{1,0:T(8,128)S(1)} %get-tuple-element.46), channel_id=1, source_target_pairs={{240,0},{248,8},{0,16},{8,24},{16,32},{24,40},{32,48},{40,56},{48,... | collective-permute-start | bytes 49160 | tf_op jit(solution)/shard_map/ppermute | solution.py:831
  59.4 11.5 %collective-permute-start.11 = (f32[16,256]{1,0:T(8,128)S(1)}, f32[16,256]{1,0:T(8,128)S(1)}, u32[]{:S(2)}, u32[]{:S(2)}) collective-permute-start(f32[16,256]{1,0:T(8,128)S(1)} %get-tuple-element.47), channel_id=1, source_target_pairs={{16,0},{24,8},{32,16},{40,24},{48,32},{56,40},{64,48},{72,56},{80,... | collective-permute-start | bytes 49160 | tf_op jit(solution)/shard_map/ppermute | solution.py:831
  70.9 14.2 %copy-start.3 = (bf16[2176,128]{1,0:T(8,128)(2,1)S(1)}, bf16[2176,128]{1,0:T(8,128)(2,1)}, u32[]{:S(2)}) copy-start(bf16[2176,128]{1,0:T(8,128)(2,1)} %constant.17.clone.refs_1_) | copy-start | bytes 1671172
  70.9 14.2 %copy-start.5 = (f32[528,128]{1,0:T(8,128)S(1)}, f32[528,128]{1,0:T(8,128)}, u32[]{:S(2)}) copy-start(f32[528,128]{1,0:T(8,128)} %constant.16.clone.refs_0_) | copy-start | bytes 811012
  78.8 6.3 %collective-permute-start.12 = (f32[32,384]{1,0:T(8,128)S(1)}, f32[32,384]{1,0:T(8,128)S(1)}, u32[]{:S(2)}, u32[]{:S(2)}) collective-permute-start(f32[32,384]{1,0:T(8,128)S(1)} %get-tuple-element.51), channel_id=1, source_target_pairs={{248,0},{0,8},{8,16},{16,24},{24,32},{32,40},{40,48},{48,56},{56,6... | collective-permute-start | bytes 147464 | tf_op jit(solution)/shard_map/ppermute | solution.py:831
  79.4 5.7 %collective-permute-start.13 = (f32[32,384]{1,0:T(8,128)S(1)}, f32[32,384]{1,0:T(8,128)S(1)}, u32[]{:S(2)}, u32[]{:S(2)}) collective-permute-start(f32[32,384]{1,0:T(8,128)S(1)} %get-tuple-element.52), channel_id=1, source_target_pairs={{8,0},{16,8},{24,16},{32,24},{40,32},{48,40},{56,48},{64,56},{72,6... | collective-permute-start | bytes 147464 | tf_op jit(solution)/shard_map/ppermute | solution.py:831

commit v4 on v3

--- a/solution.py
+++ b/solution.py
@@ -179,12 +179,21 @@
     return tensor_rows(level, k_r.reshape(rows, n, rows, n), rows)[size:-size]
 
 
-def plane_matrix(n, low, high, count=2):
+def plane_matrix(n, low, high, count=2, weight=None):
     t = np.zeros((2, 2 * n, count, 2 * n, n))
     for z in range(2 * n):
-        t[0, z, 0, z] = low
-        t[1, z, count - 1, z] = high
+        t[0, z, 0, z] = low * (1.0 if weight is None else weight[z])
+        t[1, z, count - 1, z] = high * (1.0 if weight is None else weight[z])
     return t.reshape(4 * n, count * 2 * n * n)
+
+
+def row_planes(level):
+    return plane_matrix(level.n, *inner_lines(level), weight=0.5 * level.w_z)
+
+
+def beside_planes(level):
+    low, high = inner_lines(level)
+    return plane_matrix(level.n, high, low, weight=0.5 * level.w_z)
 
 
 def inner_lines(level):
@@ -196,9 +205,7 @@
 
 def face_matrix(level, count=2):
     n = level.n
-    first, last = np.eye(n)[0], np.eye(n)[-1]
-    t = plane_matrix(n, first, last, count).T
-    return t * np.tile(0.5 * level.w_z, 2)[None, :]
+    return plane_matrix(n, np.eye(n)[0], np.eye(n)[-1], count).T
 
 
 def pair(consts, name, matrix):
@@ -220,8 +227,7 @@
 def own_constants():
     c = fine_constants()
     pair(c, "m", closed_operator(FINE, 2))
-    pair(c, "pl", plane_matrix(8, *inner_lines(FINE)))
-    pair(c, "pf", face_matrix(FINE))
+    pair(c, "pl", row_planes(FINE))
     return c
 
 
@@ -241,8 +247,8 @@
 def mid_own_constants():
     c = mid_constants()
     pair(c, "m", closed_operator(MID, 2))
-    pair(c, "pl", plane_matrix(4, *inner_lines(MID)))
-    pair(c, "pf", face_matrix(MID))
+    pair(c, "pl", row_planes(MID))
+    c["pf"] = face_matrix(MID).astype(ml_dtypes.bfloat16)
     return c
 
 
@@ -259,6 +265,32 @@
     h, l = parts
     th, tl = c[name + "h"][...], c[name + "l"][...]
     return dot(th, h) + dot(th, l) + dot(tl, h)
+
+
+def lefts(tables, parts):
+    h, l = parts
+    th = jnp.concatenate([c[name + "h"][...] for c, name in tables], axis=0)
+    tl = jnp.concatenate([c[name + "l"][...] for c, name in tables], axis=0)
+    t = dot(th, h) + dot(th, l) + dot(tl, h)
+    out, at = [], 0
+    for c, name in tables:
+        rows = c[name + "h"].shape[0]
+        out.append(t[at : at + rows])
+        at += rows
+    return out
+
+
+def on_faces(planes):
+    cube = (32, 8, planes.shape[1])
+    which = lax.broadcasted_iota(jnp.int32, cube, 0)
+    node = lax.broadcasted_iota(jnp.int32, cube, 1)
+    outer = ((which < 16) & (node == 0)) | ((which >= 16) & (node == 7))
+    return jnp.where(outer, planes.reshape(32, 1, -1), 0.0).reshape(256, -1)
+
+
+def mid_faces(table, planes):
+    h, l = split(planes)
+    return dot(table, h) + dot(table, l)
 
 
 def right(c, name, parts):
@@ -306,12 +338,13 @@
     return col_sum(jnp.concatenate(y, axis=1))
 
 
-def fine_own(parts, c, planes=None):
+def fine_own(parts, c, planes=None, more=()):
     lanes = parts[0].shape[1] // 128
-    t = left(c, "m", parts)
+    t, *rest = lefts([(c, "m"), *more], parts)
     if planes is not None:
-        t = t + left(c, "pf", split(planes))
-    return tiles(c["wc"], 1, lanes) * t + tiles(c["cf"], 2, lanes) * col_stiff(parts, c["kc"][...])
+        t = t + on_faces(planes)
+    a = tiles(c["wc"], 1, lanes) * t + tiles(c["cf"], 2, lanes) * col_stiff(parts, c["kc"][...])
+    return (a, *rest) if more else a
 
 
 def mid_apply(t, parts, c):
@@ -323,7 +356,7 @@
     parts = split(u)
     t = left(c, "m", parts)
     if planes is not None:
-        t = t + left(c, "pf", split(planes))
+        t = t + mid_faces(c["pf"][...], planes)
     return mid_apply(t, parts, c)
 
 
@@ -430,48 +463,52 @@
     return jnp.concatenate([low[at : at + rows], high[at : at + rows]], axis=0)
 
 
+def rhs_depth():
+    return MID.sum_z @ blocks(J_FINE.T, 2) @ np.diag(FINE.m_z)
+
+
 def middle_tables(consts):
-    consts["f"] = plane_matrix(8, np.eye(8)[0], np.eye(8)[7]).T.astype(ml_dtypes.bfloat16)
     inside = np.ones(8)
     inside[0] = inside[7] = 0.0
-    pair(consts, "q", plane_matrix(8, J_FINE[:, 0] * inside, J_FINE[:, 3] * inside))
+    q = plane_matrix(8, J_FINE[:, 0] * inside, J_FINE[:, 3] * inside)
+    q = blocks(rhs_depth(), 2) @ q
+    pair(consts, "q", q)
+    outer = np.zeros((2, 16, 8))
+    outer[0, :, 0] = outer[1, :, 7] = 1.0
+    pair(consts, "qm", (q @ closed_operator(FINE, 2)) * (1.0 - outer.reshape(1, 256)))
+    pair(consts, "qc", q * np.tile(0.5 * np.kron(FINE.w_z, FINE.w_p), 2)[None, :])
 
 
 def fine_middle(held, b, below, above):
     def body(c, ins, outs):
         b, below, above = ins
         x_out, r_out, d_out, low, high = outs
-        h, l = split(faced(below, above, 0, 16))
-        f = c["f"][...]
-        b = b[...] + dot(f, h) + dot(f, l)
-        q = {"h": c["qh"], "l": c["ql"]}
-        c = under(c, "f_")
-        d1, d2, d3 = (tiles(c[k], 2, 4) for k in ("d1", "d2", "d3"))
+        b = b[...] + on_faces(faced(below, above, 0, 16))
+        f = under(c, "f_")
+        d1, d2, d3 = (tiles(f[k], 2, 4) for k in ("d1", "d2", "d3"))
         d = d1 * b
         x = d
-        r = b - fine_own(split(d), c, faced(below, above, 16, 16))
+        r = b - fine_own(split(d), f, faced(below, above, 16, 16))
         d = FINE.steps[0][0] * d + d2 * r
         x_out[...] = (x + d)[:, :256]
-        parts = split(d)
-        plane1 = left(c, "pl", parts)
-        r = r - fine_own(parts, c)
+        a, plane1 = fine_own(split(d), f, more=[(f, "pl")])
+        r = r - a
         d = FINE.steps[1][0] * d + d3 * r
         r_out[...] = r
         d_out[...] = d
         parts = split(d)
-        plane2 = left(c, "pl", parts)
-        row = lax.broadcasted_iota(jnp.int32, d.shape, 0)
-        node = row % 8
-        outer = ((row < 128) & (node == 0)) | ((row >= 128) & (node == 7))
-        r = r - fine_own(split(jnp.where(outer, 0.0, d)), c)
-        plane3 = left(q, "", split(r))
-        for k, plane in enumerate((plane1, plane2, plane3)):
+        plane2, rows, columns = lefts([(f, "pl"), (c, "qm"), (c, "qc")], parts)
+        plane3 = left(c, "q", split(r)) - tiles(f["wc"], 1, 4) * rows
+        plane3 = plane3 - col_stiff(split(columns), f["kc"][...])
+        for k, plane in enumerate((plane1, plane2)):
             low[16 * k : 16 * k + 16] = plane[:16]
             high[16 * k : 16 * k + 16] = plane[16:]
+        low[32:40] = plane3[:8]
+        high[32:40] = plane3[8:]
 
     return call(
         body,
-        [(256, 256), (256, 512), (256, 512), (48, 512), (48, 512)],
+        [(256, 256), (256, 512), (256, 512), (40, 512), (40, 512)],
         held,
         (b, below, above),
     )
@@ -479,18 +516,15 @@
 
 def last_tables(consts):
     kappa = float(np.sum(J_FINE[1:7, 0] * FINE.k[1:7, 0]))
-    t = kappa * plane_matrix(8, np.eye(8)[0], np.eye(8)[7])
-    pair(consts, "e", t * np.tile(0.5 * FINE.w_z, 2)[:, None])
-    z = MID.sum_z @ blocks(J_FINE.T, 2) @ np.diag(FINE.m_z)
+    t = kappa * plane_matrix(8, np.eye(8)[0], np.eye(8)[7], weight=0.5 * FINE.w_z)
+    z = rhs_depth()
+    pair(consts, "e", blocks(z, 2) @ t)
     rows = sum_matrix(2, 4, False) @ blocks(J_FINE.T @ np.diag(FINE.m_p), 2)
     rows[0, 0] += 0.5
     rows[-1, -1] += 0.5
     t = np.einsum("zy,eafb->ezafyb", z, rows.reshape(2, 4, 2, 8)).reshape(64, 256)
     pair(consts, "ra", t)
-    t = np.zeros((2, 8, 4, 2, 16))
-    t[0, :, 0, 0] = z
-    t[1, :, 3, 1] = z
-    pair(consts, "rp", t.reshape(64, 32))
+    consts["rp"] = face_matrix(MID).astype(ml_dtypes.bfloat16)
     t = sum_matrix(64, 4, True) @ blocks(J_FINE.T @ np.diag(FINE.m_p), 64)
     pair(consts, "rc", t.T)
 
@@ -501,17 +535,18 @@
         x0, r0, b_out, r1_out, low, high = outs
         f, m = under(c, "f_"), under(c, "m_")
         wc = tiles(f["wc"], 1, 4)
-        change = wc * left(f, "pf", split(faced(below, above, 0, 16)))
+        change = wc * on_faces(faced(below, above, 0, 16))
         r = r[...] - change
         d = d[...] - tiles(f["d3"], 2, 4) * change
         x0[...] = x[...] + d[:, :256]
         parts = split(d)
-        r = r - fine_own(parts, f, faced(below, above, 16, 16))
+        a, inside = fine_own(parts, f, faced(below, above, 16, 16), [(c, "e")])
+        r = r - a
         lane = lax.broadcasted_iota(jnp.int32, (256, 128), 1)
         r0[:, :256] = r[:, :256]
         r0[:, 256:] = jnp.where(lane < 64, r[:, 256:384], r[:, 384:])
-        beyond = faced(below, above, 32, 16) - wc * left(c, "e", parts)
-        b = left(c, "ra", split(r)) + left(c, "rp", split(beyond))
+        beyond = faced(below, above, 32, 8) - wc * inside
+        b = left(c, "ra", split(r)) + mid_faces(c["rp"][...], beyond)
         b = right(c, "rc", split(b))
         b_out[...] = b
         d = tiles(m["d1"], 2, 1) * b
@@ -571,12 +606,12 @@
 def mid_last(held, b, r1, below, above):
     def body(c, ins, outs):
         b, r1, below, above = ins
+        chunk, lo, hi, lo2, hi2 = outs
         down, c = c, under(c, "m_")
-        chunk, lo, hi, lo2, hi2 = outs
         d1, d2, d3 = (tiles(c[k], 2, 1) for k in ("d1", "d2", "d3"))
         d = d1 * b[...]
         x = d
-        r = r1[...] - c["wc"][...] * left(c, "pf", split(faced(below, above, 0, 8)))
+        r = r1[...] - c["wc"][...] * mid_faces(c["pf"][...], faced(below, above, 0, 8))
         d = MID.steps[0][0] * d + d2 * r
         x = x + d
         r = r - mid_own(d, c, faced(below, above, 8, 8))
@@ -584,7 +619,7 @@
         x = x + d
         parts = split(d)
         t = jnp.concatenate(
-            [left(down, "sm", split(r)), left(down, "s1", parts), left(down, "s2", parts)], axis=1
+            [left(down, "sm", split(r)), *lefts([(down, "s1"), (down, "s2")], parts)], axis=1
         )
         t = right(down, "sc", split(t))
         t = jnp.concatenate([t, t, t], axis=1)
@@ -681,9 +716,9 @@
 def second_tables(consts):
     pair(consts, "a", window_operator(MID, 6))
     pair(consts, "c", closed_operator(MID, 6))
-    pair(consts, "p", np.concatenate([blocks(face_matrix(MID), 3), face_matrix(MID, 6)], axis=1))
-    low, high = inner_lines(MID)
-    pair(consts, "po", plane_matrix(4, high, low))
+    t = np.concatenate([blocks(face_matrix(MID), 3), face_matrix(MID, 6)], axis=1)
+    consts["p"] = t.astype(ml_dtypes.bfloat16)
+    pair(consts, "po", beside_planes(MID))
     jc = np.zeros((4, 32, 256))
     for e in range(64):
         element = e if e < 48 else e - 64
@@ -691,7 +726,9 @@
             v = element + k
             dev, col = v // 32 + 1, v % 32
             jc[dev, col, 4 * e : 4 * e + 4] = J_MID[:, k]
-    pair(consts, "vc", jc.reshape(128, 256))
+    jc = jc.reshape(128, 256)
+    pair(consts, "vc", jc)
+    pair(consts, "vk", jc @ (sum_matrix(64, 4, True) @ blocks(MID.k, 64)).T)
     jz = np.zeros((8, 3))
     jz[:4, :2] += J_MID
     jz[4:, 1:] += J_MID
@@ -700,7 +737,9 @@
         for k in range(2):
             jdr[e, :, :, :, e + k] += np.einsum("zp,a->zap", jz, J_MID[:, k])
     order = [2 * (q % 8) + q // 8 for q in range(16)]
-    pair(consts, "vd", jdr[..., order].reshape(320, 48))
+    vd = jdr[..., order].reshape(320, 48)
+    pair(consts, "vd", vd)
+    pair(consts, "va", window_operator(MID, 10) @ vd)
     pair(consts, "fo", blocks(J_FINE.T, 32))
     fc = np.zeros((128, 128))
     for e in range(16):
@@ -709,8 +748,7 @@
     pair(consts, "fh", fc)
     fd = np.kron(blocks(J_FINE, 2), J_FINE)
     pair(consts, "fd", blocks(fd, 2))
-    low, high = inner_lines(FINE)
-    pair(consts, "fp", plane_matrix(8, high, low) @ blocks(fd, 2))
+    pair(consts, "fp", beside_planes(FINE) @ blocks(fd, 2))
 
 
 def second_smoothing(held, gathered, x0, r0, own_lo, own_hi, below, above, below2, above2):
@@ -736,19 +774,14 @@
             y.append(
                 jnp.where(block == 0, v[0], jnp.where(block == 1, v[1], jnp.where(block == 2, v[2], 0.0)))
             )
-        y = right(c, "vc", split(jnp.concatenate(y, axis=0)))
-        e2 = left(c, "vd", split(y))
-
-        def window(u):
-            h, l = split(u)
-            t = [left(c, "a", (h[k : k + 192], l[k : k + 192])) for k in range(0, len(u) - 64, 128)]
-            return mid_apply(jnp.concatenate(t, axis=0), (h[32:-32], l[32:-32]), m)
+        parts = split(jnp.concatenate(y, axis=0))
+        yk = left(c, "vd", split(right(c, "vk", parts)))
+        e2, ya = lefts([(c, "vd"), (c, "va")], split(right(c, "vc", parts)))
+        g = m["wc"][...] * ya + tiles(m["cf"], 8, 1) * yk[32:-32]
 
         def table(name, count):
             return tiles(m[name], count, 1)
 
-        p3 = {"h": c["ph"][:, :48], "l": c["pl"][:, :48]}
-        p6 = {"h": c["ph"][:, 48:], "l": c["pl"][:, 48:]}
         planes = jnp.concatenate(
             [
                 below2[:8],
@@ -760,19 +793,19 @@
             ],
             axis=0,
         )
-        g = window(e2)
         r = jnp.concatenate([below[:64], own_lo[:64], above[:64]], axis=0)
-        r = r - m["wc"][...] * left(p3, "", split(planes)) - g[32:224]
+        r = r - m["wc"][...] * mid_faces(c["p"][:, :48], planes) - g[32:224]
         d = table("d1", 6) * r
         x = jnp.concatenate([below[72:104], own_lo[72:104], own_hi[72:104], above[72:104]], axis=0)
         x = x + e2[96:224] + d[32:160]
         outer = jnp.concatenate([g[:32], g[224:]], axis=0) * table("d1", 2)
         planes = faced(below2, above2, 8, 8) - left(c, "po", split(outer))
         parts = split(d)
-        r = r - mid_apply(left(c, "c", parts) + left(p6, "", split(planes)), parts, m)
+        r = r - mid_apply(left(c, "c", parts) + mid_faces(c["p"][:, 48:], planes), parts, m)
         d = MID.steps[0][0] * d + table("d2", 6) * r
         x = x + d[32:160]
-        r = r[32:160] - window(d)
+        h, l = split(d)
+        r = r[32:160] - mid_apply(left(c, "a", (h, l)), (h[32:-32], l[32:-32]), m)
         d = MID.steps[1][0] * d[32:160] + table("d3", 4) * r
         x = x + d
         h, l = split(x)
@@ -788,9 +821,8 @@
         r = r0[...] - fine_own(split(e1), f, planes)
         d = tiles(f["d1"], 2, 3) * r
         s_out[...] = x0[...] + (e1 + d)[:, :256]
-        parts = split(d)
-        plane1 = left(f, "pl", parts)
-        r = r - fine_own(parts, f)
+        a, plane1 = fine_own(split(d), f, more=[(f, "pl")])
+        r = r - a
         d = FINE.steps[0][0] * d + tiles(f["d2"], 2, 3) * r
         plane2 = left(f, "pl", split(d))
         r_out[...] = r
@@ -813,7 +845,7 @@
         c = under(c, "f_")
         s, r, d, below, above = ins
         (out,) = outs
-        change = tiles(c["wc"], 1, 3) * left(c, "pf", split(faced(below, above, 0, 16)))
+        change = tiles(c["wc"], 1, 3) * on_faces(faced(below, above, 0, 16))
         r = r[...] - change
         d = d[...] - tiles(c["d2"], 2, 3) * change
         r = r - fine_own(split(d), c, faced(below, above, 16, 16))

time: 87 us -> 84.2 us (0.968)
  Pallas kernels: 16.8 us -> 14.3 us
    pallas_call x7, Pallas kernels: 16.8 us -> 14.3 us  [call(): pl.pallas_call(kernel, out_shape=[jax.ShapeDtypeStruct(s, f32) for s in o...]
where the time goes in v4:
time: 84.2 us; the launch traced here: 84 us
  starting transfers between devices  50.9 us (60%)
  Pallas kernels  14.3 us (17%)
  waiting for transfers between devices  13.1 us (16%)
  local copies, waits for them, and re-layouts  5.5 us (7%)
    ppermute x14, starting transfers between devices, fetch(): lax.ppermute(value, axis, [((i + offset) % count, i) for i in range(count)])  38.1 us
    pallas_call x7, Pallas kernels, call(): pl.pallas_call(kernel, out_shape=[jax.ShapeDtypeStruct(s, f32) for s in o...  14.3 us
    all_to_all x1, starting transfers between devices, local(): gathered = lax.all_to_all(chunk, ('gx', 'gy'), 0, 0, tiled=True)  12.7 us
    ppermute x14, waiting for transfers between devices, fetch(): lax.ppermute(value, axis, [((i + offset) % count, i) for i in range(count)])  8.16 us
    all_to_all x1, waiting for transfers between devices, local(): gathered = lax.all_to_all(chunk, ('gx', 'gy'), 0, 0, tiled=True)  4.96 us
    unnamed x13, local copies, waits for them, and re-layouts  3.57 us
  transfers between devices with their start and end apart: 15, of which 6 were waited for; matrix products, arithmetic and copies ran while one was open for 1% of the time, Pallas kernels for 0%

profile of v4, /device:TPU:1, one launch (start us, length us, event | category | flops | bytes accessed | tf_op | source)
XLA Modules:
  0.0 84.0 jit_solution(5181359007614668001)
XLA Ops:
  0.0 1.0 %fusion = (f32[16,16,128]{2,1,0:T(8,128)S(1)}, f32[16,16,128]{2,1,0:T(8,128)S(1)}) fusion(f32[16,16,256]{2,1,0:T(8,128)} %param.7), kind=kLoop, calls=%fused_computation.1 | loop fusion | bytes 524288 | tf_op jit(solution)/shard_map/slice | solution.py:880
  1.0 2.6 %collective-permute-start.1 = (f32[16,16,128]{2,1,0:T(8,128)S(1)}, f32[16,16,128]{2,1,0:T(8,128)S(1)}, u32[]{:S(2)}, u32[]{:S(2)}) collective-permute-start(f32[16,16,128]{2,1,0:T(8,128)S(1)} %get-tuple-element.53.refs_3_), channel_id=1, source_target_pairs={{7,0},{0,1},{1,2},{2,3},{3,4},{4,5},{5,6},{6,7},{15,8},{8,9},{9,10... | collective-permute-start | bytes 393224 | tf_op jit(solution)/shard_map/ppermute | solution.py:863
  3.6 0.7 collective-permute-start
  4.3 1.5 %copy-done = bf16[7168,128]{1,0:T(8,128)(2,1)S(1)} copy-done((bf16[7168,128]{1,0:T(8,128)(2,1)S(1)}, bf16[7168,128]{1,0:T(8,128)(2,1)}, u32[]{:S(2)}) %copy-start) | copy-done | bytes 1835032
  5.8 1.0 %copy-done.1 = f32[944,128]{1,0:T(8,128)S(1)} copy-done((f32[944,128]{1,0:T(8,128)S(1)}, f32[944,128]{1,0:T(8,128)}, u32[]{:S(2)}) %copy-start.1) | copy-done | bytes 483352
  6.8 1.5 %collective-permute-done.refs_4_ = f32[16,16,128]{2,1,0:T(8,128)S(1)} collective-permute-done((f32[16,16,128]{2,1,0:T(8,128)S(1)}, f32[16,16,128]{2,1,0:T(8,128)S(1)}, u32[]{:S(2)}, u32[]{:S(2)}) %collective-permute-start) | collective-permute-done | bytes 131104 | tf_op jit(solution)/shard_map/ppermute | solution.py:863
  8.3 0.6 shard_map.74
  8.8 1.4 %collective-permute-start.2 = (f32[32,512]{1,0:T(8,128)S(1)}, f32[32,512]{1,0:T(8,128)S(1)}, u32[]{:S(2)}, u32[]{:S(2)}) collective-permute-start(f32[32,512]{1,0:T(8,128)S(1)} %get-tuple-element.30), channel_id=1, source_target_pairs={{248,0},{0,8},{8,16},{16,24},{24,32},{32,40},{40,48},{48,56},{56,6... | collective-permute-start | bytes 196616 | tf_op jit(solution)/shard_map/ppermute | solution.py:863
  10.3 6.5 %collective-permute-start.3 = (f32[32,512]{1,0:T(8,128)S(1)}, f32[32,512]{1,0:T(8,128)S(1)}, u32[]{:S(2)}, u32[]{:S(2)}) collective-permute-start(f32[32,512]{1,0:T(8,128)S(1)} %get-tuple-element.31), channel_id=1, source_target_pairs={{8,0},{16,8},{24,16},{32,24},{40,32},{48,40},{56,48},{64,56},{72,6... | collective-permute-start | bytes 196616 | tf_op jit(solution)/shard_map/ppermute | solution.py:863
  16.7 2.3 %collective-permute-done.2.refs_3_ = f32[32,512]{1,0:T(8,128)S(1)} collective-permute-done((f32[32,512]{1,0:T(8,128)S(1)}, f32[32,512]{1,0:T(8,128)S(1)}, u32[]{:S(2)}, u32[]{:S(2)}) %collective-permute-start.2) | collective-permute-done | bytes 65568 | tf_op jit(solution)/shard_map/ppermute | solution.py:863
  19.0 2.3 %shard_map.75 = (f32[256,256]{1,0:T(8,128)S(1)}, f32[256,512]{1,0:T(8,128)S(1)}, f32[256,512]{1,0:T(8,128)S(1)}, f32[40,512]{1,0:T(8,128)S(1)}, f32[40,512]{1,0:T(8,128)S(1)}) custom-call(f32[944,128]{1,0:T(8,128)S(1)} %copy-done.1, bf16[7168,128]{1,0:T(8,128)(2,1)S(1)} %copy-done, f32[256,512]{1,0:T(8,128)S(1)} %get-tuple-element.29.refs_2_, ...), custom_call_target="tpu_custom_call" | custom-call | tf_op jit(solution)/shard_map/pallas_call | solution.py:411
  21.3 0.1 collective-permute-start.4
  21.4 4.8 %collective-permute-start.5 = (f32[40,512]{1,0:T(8,128)S(1)}, f32[40,512]{1,0:T(8,128)S(1)}, u32[]{:S(2)}, u32[]{:S(2)}) collective-permute-start(f32[40,512]{1,0:T(8,128)S(1)} %get-tuple-element.36), channel_id=1, source_target_pairs={{8,0},{16,8},{24,16},{32,24},{40,32},{48,40},{56,48},{64,56},{72,6... | collective-permute-start | bytes 245768 | tf_op jit(solution)/shard_map/ppermute | solution.py:863
  26.2 1.8 %collective-permute-done.4.refs_5_ = f32[40,512]{1,0:T(8,128)S(1)} collective-permute-done((f32[40,512]{1,0:T(8,128)S(1)}, f32[40,512]{1,0:T(8,128)S(1)}, u32[]{:S(2)}, u32[]{:S(2)}) %collective-permute-start.4) | collective-permute-done | bytes 81952 | tf_op jit(solution)/shard_map/ppermute | solution.py:863
  28.0 2.0 %shard_map.76 = (f32[256,256]{1,0:T(8,128)S(1)}, f32[256,384]{1,0:T(8,128)S(1)}, f32[64,256]{1,0:T(8,128)S(1)}, f32[64,256]{1,0:T(8,128)S(1)}, f32[16,256]{1,0:T(8,128)S(1)}, /*index=5*/f32[16,256]{1,0:T(8,128)S(1)}) custom-call(f32[944,128]{1,0:T(8,128)S(1)} %copy-done.1, bf16[7168,128]{1,0:T(8,128)(2,1)S(1)} %copy-done, ...), custom_call_target="tpu_custom_call" | custom-call | tf_op jit(solution)/shard_map/pallas_call | solution.py:411
  30.0 4.8 %collective-permute-start.7 = (f32[16,256]{1,0:T(8,128)S(1)}, f32[16,256]{1,0:T(8,128)S(1)}, u32[]{:S(2)}, u32[]{:S(2)}) collective-permute-start(f32[16,256]{1,0:T(8,128)S(1)} %get-tuple-element.40), channel_id=1, source_target_pairs={{8,0},{16,8},{24,16},{32,24},{40,32},{48,40},{56,48},{64,56},{72,6... | collective-permute-start | bytes 49160 | tf_op jit(solution)/shard_map/ppermute | solution.py:863
  34.8 1.1 %collective-permute-done.6.refs_4_ = f32[16,256]{1,0:T(8,128)S(1)} collective-permute-done((f32[16,256]{1,0:T(8,128)S(1)}, f32[16,256]{1,0:T(8,128)S(1)}, u32[]{:S(2)}, u32[]{:S(2)}) %collective-permute-start.6) | collective-permute-done | bytes 16416 | tf_op jit(solution)/shard_map/ppermute | solution.py:863
  35.9 1.0 %shard_map.77 = (f32[1,384]{1,0:T(1,128)S(1)}, f32[104,256]{1,0:T(8,128)S(1)}, f32[104,256]{1,0:T(8,128)S(1)}, f32[16,256]{1,0:T(8,128)S(1)}, f32[16,256]{1,0:T(8,128)S(1)}) custom-call(f32[944,128]{1,0:T(8,128)S(1)} %copy-done.1, bf16[7168,128]{1,0:T(8,128)(2,1)S(1)} %copy-done, f32[64,256]{1,0:T(8,128)S(1)} %get-tuple-element.37.refs_2_, ...), custom_call_target="tpu_custom_call" | custom-call | tf_op jit(solution)/shard_map/pallas_call | solution.py:411
  36.9 0.9 %broadcast_in_dim.2 = f32[256,1,384]{2,1,0:T(1,128)} broadcast(f32[384]{0:T(512)S(1)} %reduce), dimensions={2} | broadcast | bytes 394752 | tf_op jit(solution)/shard_map/broadcast_in_dim | solution.py:887
  37.8 12.7 %all-to-all-start = ((f32[256,1,384]{2,1,0:T(1,128)}), f32[256,1,384]{2,1,0:T(1,128)}, u32[]{:S(2)}, u32[]{:S(2)}) async-start(f32[256,1,384]{2,1,0:T(1,128)} %broadcast_in_dim.2), calls=%async_computation | async-start | bytes 786432 | tf_op jit(solution)/shard_map/all_to_all | solution.py:888
  50.6 6.7 %collective-permute-start.9 = (f32[104,256]{1,0:T(8,128)S(1)}, f32[104,256]{1,0:T(8,128)S(1)}, u32[]{:S(2)}, u32[]{:S(2)}) collective-permute-start(f32[104,256]{1,0:T(8,128)S(1)} %get-tuple-element.44.refs_5_), channel_id=1, source_target_pairs={{8,0},{16,8},{24,16},{32,24},{40,32},{48,40},{56,48},{64,56},{72,6... | collective-permute-start | bytes 319496 | tf_op jit(solution)/shard_map/ppermute | solution.py:863
  57.3 0.0 collective-permute-start.10
  57.3 5.7 %collective-permute-start.11 = (f32[16,256]{1,0:T(8,128)S(1)}, f32[16,256]{1,0:T(8,128)S(1)}, u32[]{:S(2)}, u32[]{:S(2)}) collective-permute-start(f32[16,256]{1,0:T(8,128)S(1)} %get-tuple-element.47), channel_id=1, source_target_pairs={{16,0},{24,8},{32,16},{40,24},{48,32},{56,40},{64,48},{72,56},{80,... | collective-permute-start | bytes 49160 | tf_op jit(solution)/shard_map/ppermute | solution.py:863
  63.0 5.0 %all-to-all-done = f32[256,1,384]{2,1,0:T(1,128)} async-done(((f32[256,1,384]{2,1,0:T(1,128)}), f32[256,1,384]{2,1,0:T(1,128)}, u32[]{:S(2)}, u32[]{:S(2)}) %all-to-all-start) | async-done | bytes 393248 | tf_op jit(solution)/shard_map/all_to_all | solution.py:888
  67.9 1.0 %copy.10 = f32[256,1,384]{2,0,1:T(8,128)S(1)} copy(f32[256,1,384]{2,1,0:T(1,128)} %all-to-all-done) | data formatting | bytes 786432
  68.9 0.0 copy-start.3
  69.0 0.0 copy-start.5
  69.0 7.4 %shard_map.78 = (f32[256,256]{1,0:T(8,128)S(1)}, f32[256,384]{1,0:T(8,128)S(1)}, f32[256,384]{1,0:T(8,128)S(1)}, f32[32,384]{1,0:T(8,128)S(1)}, f32[32,384]{1,0:T(8,128)S(1)}) custom-call(f32[816,128]{1,0:T(8,128)S(1)} %copy-done.4, bf16[7712,128]{1,0:T(8,128)(2,1)S(1)} %copy-done.2, f32[256,384]{1,0:T(8,128)S(1)} %bitcast.3, ...), custom_call_target="tpu_custom_call" | custom-call | tf_op jit(solution)/shard_map/pallas_call | solution.py:411
  76.4 0.7 collective-permute-start.12
  77.1 4.2 %collective-permute-start.13 = (f32[32,384]{1,0:T(8,128)S(1)}, f32[32,384]{1,0:T(8,128)S(1)}, u32[]{:S(2)}, u32[]{:S(2)}) collective-permute-start(f32[32,384]{1,0:T(8,128)S(1)} %get-tuple-element.52), channel_id=1, source_target_pairs={{8,0},{16,8},{24,16},{32,24},{40,32},{48,40},{56,48},{64,56},{72,6... | collective-permute-start | bytes 147464 | tf_op jit(solution)/shard_map/ppermute | solution.py:863
  81.3 1.5 %collective-permute-done.12.refs_5_ = f32[32,384]{1,0:T(8,128)S(1)} collective-permute-done((f32[32,384]{1,0:T(8,128)S(1)}, f32[32,384]{1,0:T(8,128)S(1)}, u32[]{:S(2)}, u32[]{:S(2)}) %collective-permute-start.12) | collective-permute-done | bytes 49184 | tf_op jit(solution)/shard_map/ppermute | solution.py:863
  82.7 1.2 %shard_map.79 = f32[16,16,256]{2,1,0:T(8,128)} custom-call(f32[528,128]{1,0:T(8,128)S(1)} %copy-done.5, bf16[1664,128]{1,0:T(8,128)(2,1)S(1)} %copy-done.3, f32[256,256]{1,0:T(8,128)S(1)} %get-tuple-element.48.refs_2_, f32[256,384]{1,0:T(8,128)S(1)} %get-tuple-element.49.refs_3_, f32[256,384]{1,0:T(8,128)S(1)} %get-tuple-element.50.refs_4_, ...), custom_call_target="tpu_custom_call" | custom-call | tf_op jit(solution)/shard_map/pallas_call | solution.py:411
  (21 shorter events, 0.1 us)
Async XLA Ops:
  1.0 5.8 %collective-permute-start.1 = (f32[16,16,128]{2,1,0:T(8,128)S(1)}, f32[16,16,128]{2,1,0:T(8,128)S(1)}, u32[]{:S(2)}, u32[]{:S(2)}) collective-permute-start(f32[16,16,128]{2,1,0:T(8,128)S(1)} %get-tuple-element.53.refs_3_), channel_id=1, source_target_pairs={{7,0},{0,1},{1,2},{2,3},{3,4},{4,5},{5,6},{6,7},{15,8},{8,9},{9,10... | collective-permute-start | bytes 393224 | tf_op jit(solution)/shard_map/ppermute | solution.py:863
  3.6 4.7 %collective-permute-start = (f32[16,16,128]{2,1,0:T(8,128)S(1)}, f32[16,16,128]{2,1,0:T(8,128)S(1)}, u32[]{:S(2)}, u32[]{:S(2)}) collective-permute-start(f32[16,16,128]{2,1,0:T(8,128)S(1)} %get-tuple-element.54.refs_2_), channel_id=1, source_target_pairs={{1,0},{2,1},{3,2},{4,3},{5,4},{6,5},{7,6},{0,7},{9,8},{10,9},{11,1... | collective-permute-start | bytes 393224 | tf_op jit(solution)/shard_map/ppermute | solution.py:863
  4.3 1.5 %copy-start = (bf16[7168,128]{1,0:T(8,128)(2,1)S(1)}, bf16[7168,128]{1,0:T(8,128)(2,1)}, u32[]{:S(2)}) copy-start(bf16[7168,128]{1,0:T(8,128)(2,1)} %constant.13.clone.refs_1_) | copy-start | bytes 5505028
  5.8 1.0 %copy-start.1 = (f32[944,128]{1,0:T(8,128)S(1)}, f32[944,128]{1,0:T(8,128)}, u32[]{:S(2)}) copy-start(f32[944,128]{1,0:T(8,128)} %constant.12.clone.refs_0_) | copy-start | bytes 1449988
  8.8 10.2 %collective-permute-start.2 = (f32[32,512]{1,0:T(8,128)S(1)}, f32[32,512]{1,0:T(8,128)S(1)}, u32[]{:S(2)}, u32[]{:S(2)}) collective-permute-start(f32[32,512]{1,0:T(8,128)S(1)} %get-tuple-element.30), channel_id=1, source_target_pairs={{248,0},{0,8},{8,16},{16,24},{24,32},{32,40},{40,48},{48,56},{56,6... | collective-permute-start | bytes 196616 | tf_op jit(solution)/shard_map/ppermute | solution.py:863
  10.3 8.7 %collective-permute-start.3 = (f32[32,512]{1,0:T(8,128)S(1)}, f32[32,512]{1,0:T(8,128)S(1)}, u32[]{:S(2)}, u32[]{:S(2)}) collective-permute-start(f32[32,512]{1,0:T(8,128)S(1)} %get-tuple-element.31), channel_id=1, source_target_pairs={{8,0},{16,8},{24,16},{32,24},{40,32},{48,40},{56,48},{64,56},{72,6... | collective-permute-start | bytes 196616 | tf_op jit(solution)/shard_map/ppermute | solution.py:863
  21.3 6.7 %collective-permute-start.4 = (f32[40,512]{1,0:T(8,128)S(1)}, f32[40,512]{1,0:T(8,128)S(1)}, u32[]{:S(2)}, u32[]{:S(2)}) collective-permute-start(f32[40,512]{1,0:T(8,128)S(1)} %get-tuple-element.35), channel_id=1, source_target_pairs={{248,0},{0,8},{8,16},{16,24},{24,32},{32,40},{40,48},{48,56},{56,6... | collective-permute-start | bytes 245768 | tf_op jit(solution)/shard_map/ppermute | solution.py:863
  21.4 6.6 %collective-permute-start.5 = (f32[40,512]{1,0:T(8,128)S(1)}, f32[40,512]{1,0:T(8,128)S(1)}, u32[]{:S(2)}, u32[]{:S(2)}) collective-permute-start(f32[40,512]{1,0:T(8,128)S(1)} %get-tuple-element.36), channel_id=1, source_target_pairs={{8,0},{16,8},{24,16},{32,24},{40,32},{48,40},{56,48},{64,56},{72,6... | collective-permute-start | bytes 245768 | tf_op jit(solution)/shard_map/ppermute | solution.py:863
  30.0 5.9 %collective-permute-start.6 = (f32[16,256]{1,0:T(8,128)S(1)}, f32[16,256]{1,0:T(8,128)S(1)}, u32[]{:S(2)}, u32[]{:S(2)}) collective-permute-start(f32[16,256]{1,0:T(8,128)S(1)} %get-tuple-element.39), channel_id=1, source_target_pairs={{248,0},{0,8},{8,16},{16,24},{24,32},{32,40},{40,48},{48,56},{56,6... | collective-permute-start | bytes 49160 | tf_op jit(solution)/shard_map/ppermute | solution.py:863
  30.0 5.9 %collective-permute-start.7 = (f32[16,256]{1,0:T(8,128)S(1)}, f32[16,256]{1,0:T(8,128)S(1)}, u32[]{:S(2)}, u32[]{:S(2)}) collective-permute-start(f32[16,256]{1,0:T(8,128)S(1)} %get-tuple-element.40), channel_id=1, source_target_pairs={{8,0},{16,8},{24,16},{32,24},{40,32},{48,40},{56,48},{64,56},{72,6... | collective-permute-start | bytes 49160 | tf_op jit(solution)/shard_map/ppermute | solution.py:863
  35.9 33.1 %copy-start.2 = (bf16[7712,128]{1,0:T(8,128)(2,1)S(1)}, bf16[7712,128]{1,0:T(8,128)(2,1)}, u32[]{:S(2)}) copy-start(bf16[7712,128]{1,0:T(8,128)(2,1)} %constant.15.clone.refs_1_) | copy-start | bytes 5922820
  35.9 33.1 %copy-start.4 = (f32[816,128]{1,0:T(8,128)S(1)}, f32[816,128]{1,0:T(8,128)}, u32[]{:S(2)}) copy-start(f32[816,128]{1,0:T(8,128)} %constant.14.clone.refs_0_) | copy-start | bytes 1253380
  37.8 30.1 %all-to-all-start = ((f32[256,1,384]{2,1,0:T(1,128)}), f32[256,1,384]{2,1,0:T(1,128)}, u32[]{:S(2)}, u32[]{:S(2)}) async-start(f32[256,1,384]{2,1,0:T(1,128)} %broadcast_in_dim.2), calls=%async_computation | async-start | bytes 786432 | tf_op jit(solution)/shard_map/all_to_all | solution.py:888
  50.6 18.4 %collective-permute-start.9 = (f32[104,256]{1,0:T(8,128)S(1)}, f32[104,256]{1,0:T(8,128)S(1)}, u32[]{:S(2)}, u32[]{:S(2)}) collective-permute-start(f32[104,256]{1,0:T(8,128)S(1)} %get-tuple-element.44.refs_5_), channel_id=1, source_target_pairs={{8,0},{16,8},{24,16},{32,24},{40,32},{48,40},{56,48},{64,56},{72,6... | collective-permute-start | bytes 319496 | tf_op jit(solution)/shard_map/ppermute | solution.py:863
  57.3 11.7 %collective-permute-start.8 = (f32[104,256]{1,0:T(8,128)S(1)}, f32[104,256]{1,0:T(8,128)S(1)}, u32[]{:S(2)}, u32[]{:S(2)}) collective-permute-start(f32[104,256]{1,0:T(8,128)S(1)} %get-tuple-element.45.refs_6_), channel_id=1, source_target_pairs={{248,0},{0,8},{8,16},{16,24},{24,32},{32,40},{40,48},{48,56},{56,6... | collective-permute-start | bytes 319496 | tf_op jit(solution)/shard_map/ppermute | solution.py:863
  57.3 11.7 %collective-permute-start.10 = (f32[16,256]{1,0:T(8,128)S(1)}, f32[16,256]{1,0:T(8,128)S(1)}, u32[]{:S(2)}, u32[]{:S(2)}) collective-permute-start(f32[16,256]{1,0:T(8,128)S(1)} %get-tuple-element.46), channel_id=1, source_target_pairs={{240,0},{248,8},{0,16},{8,24},{16,32},{24,40},{32,48},{40,56},{48,... | collective-permute-start | bytes 49160 | tf_op jit(solution)/shard_map/ppermute | solution.py:863
  57.3 11.7 %collective-permute-start.11 = (f32[16,256]{1,0:T(8,128)S(1)}, f32[16,256]{1,0:T(8,128)S(1)}, u32[]{:S(2)}, u32[]{:S(2)}) collective-permute-start(f32[16,256]{1,0:T(8,128)S(1)} %get-tuple-element.47), channel_id=1, source_target_pairs={{16,0},{24,8},{32,16},{40,24},{48,32},{56,40},{64,48},{72,56},{80,... | collective-permute-start | bytes 49160 | tf_op jit(solution)/shard_map/ppermute | solution.py:863
  68.9 13.8 %copy-start.3 = (bf16[1664,128]{1,0:T(8,128)(2,1)S(1)}, bf16[1664,128]{1,0:T(8,128)(2,1)}, u32[]{:S(2)}) copy-start(bf16[1664,128]{1,0:T(8,128)(2,1)} %constant.17.clone.refs_1_) | copy-start | bytes 1277956
  69.0 13.8 %copy-start.5 = (f32[528,128]{1,0:T(8,128)S(1)}, f32[528,128]{1,0:T(8,128)}, u32[]{:S(2)}) copy-start(f32[528,128]{1,0:T(8,128)} %constant.16.clone.refs_0_) | copy-start | bytes 811012
  76.4 6.3 %collective-permute-start.12 = (f32[32,384]{1,0:T(8,128)S(1)}, f32[32,384]{1,0:T(8,128)S(1)}, u32[]{:S(2)}, u32[]{:S(2)}) collective-permute-start(f32[32,384]{1,0:T(8,128)S(1)} %get-tuple-element.51), channel_id=1, source_target_pairs={{248,0},{0,8},{8,16},{16,24},{24,32},{32,40},{40,48},{48,56},{56,6... | collective-permute-start | bytes 147464 | tf_op jit(solution)/shard_map/ppermute | solution.py:863
  77.1 5.7 %collective-permute-start.13 = (f32[32,384]{1,0:T(8,128)S(1)}, f32[32,384]{1,0:T(8,128)S(1)}, u32[]{:S(2)}, u32[]{:S(2)}) collective-permute-start(f32[32,384]{1,0:T(8,128)S(1)} %get-tuple-element.52), channel_id=1, source_target_pairs={{8,0},{16,8},{24,16},{32,24},{40,32},{48,40},{56,48},{64,56},{72,6... | collective-permute-start | bytes 147464 | tf_op jit(solution)/shard_map/ppermute | solution.py:863

commit v5 on v4

--- a/solution.py
+++ b/solution.py
@@ -219,8 +219,6 @@
         wc=np.tile(FINE.w_p, 16)[None, :].astype(np.float32),
         cf=np.repeat(0.5 * np.kron(FINE.w_z, FINE.w_p)[:, None], 128, axis=1).astype(np.float32),
         d1=(FINE.first * dinv).astype(np.float32),
-        d2=(FINE.steps[0][1] * dinv).astype(np.float32),
-        d3=(FINE.steps[1][1] * dinv).astype(np.float32),
     )
 
 
@@ -237,8 +235,6 @@
         wc=np.tile(MID.w_p, 64)[None, :].astype(np.float32),
         cf=np.repeat(0.5 * np.kron(MID.w_z, MID.w_p)[:, None], 256, axis=1).astype(np.float32),
         d1=(MID.first * dinv).astype(np.float32),
-        d2=(MID.steps[0][1] * dinv).astype(np.float32),
-        d3=(MID.steps[1][1] * dinv).astype(np.float32),
     )
     pair(c, "k", (sum_matrix(64, 4, True) @ blocks(MID.k, 64)).T)
     return c
@@ -306,6 +302,14 @@
     if rows > 1:
         t = jnp.concatenate([t] * rows, axis=0)
     return t
+
+
+def damping(level, c, step, rows, lanes):
+    t = c["d1"][...]
+    if step:
+        t = t * (level.steps[step - 1][1] / level.first)
+    t = jnp.concatenate([t] * lanes, axis=1) if lanes > 1 else t
+    return jnp.concatenate([t] * rows, axis=0) if rows > 1 else t
 
 
 def row_sum(before, here, after):
@@ -485,7 +489,7 @@
         x_out, r_out, d_out, low, high = outs
         b = b[...] + on_faces(faced(below, above, 0, 16))
         f = under(c, "f_")
-        d1, d2, d3 = (tiles(f[k], 2, 4) for k in ("d1", "d2", "d3"))
+        d1, d2, d3 = (damping(FINE, f, k, 2, 4) for k in range(3))
         d = d1 * b
         x = d
         r = b - fine_own(split(d), f, faced(below, above, 16, 16))
@@ -537,7 +541,7 @@
         wc = tiles(f["wc"], 1, 4)
         change = wc * on_faces(faced(below, above, 0, 16))
         r = r[...] - change
-        d = d[...] - tiles(f["d3"], 2, 4) * change
+        d = d[...] - damping(FINE, f, 2, 2, 4) * change
         x0[...] = x[...] + d[:, :256]
         parts = split(d)
         a, inside = fine_own(parts, f, faced(below, above, 16, 16), [(c, "e")])
@@ -553,7 +557,7 @@
         plane1 = left(m, "pl", split(d))
         r = b - mid_own(d, m)
         r1_out[...] = r
-        d = MID.steps[0][0] * d + tiles(m["d2"], 2, 1) * r
+        d = MID.steps[0][0] * d + damping(MID, m, 1, 2, 1) * r
         plane2 = left(m, "pl", split(d))
         for k, plane in enumerate((plane1, plane2)):
             low[8 * k : 8 * k + 8] = plane[:8]
@@ -608,7 +612,7 @@
         b, r1, below, above = ins
         chunk, lo, hi, lo2, hi2 = outs
         down, c = c, under(c, "m_")
-        d1, d2, d3 = (tiles(c[k], 2, 1) for k in ("d1", "d2", "d3"))
+        d1, d2, d3 = (damping(MID, c, k, 2, 1) for k in range(3))
         d = d1 * b[...]
         x = d
         r = r1[...] - c["wc"][...] * mid_faces(c["pf"][...], faced(below, above, 0, 8))
@@ -625,7 +629,11 @@
         t = jnp.concatenate([t, t, t], axis=1)
         q = lax.broadcasted_iota(jnp.int32, t.shape, 0)
         lane = lax.broadcasted_iota(jnp.int32, t.shape, 1) // 32
-        chunk[...] = jnp.sum(jnp.where(q == lane, t, 0.0), axis=0, keepdims=True)
+        t = jnp.sum(jnp.where(q == lane, t, 0.0), axis=0, keepdims=True)
+        which = lax.broadcasted_iota(jnp.int32, chunk.shape, 0) % 3
+        chunk[...] = jnp.where(
+            which == 0, t[:, :128], jnp.where(which == 1, t[:, 128:256], t[:, 256:])
+        )
         plane1 = left(c, "pl", parts)
         r = r - mid_own(d, c)
         plane2 = left(c, "pl", split(d1 * r))
@@ -638,7 +646,7 @@
 
     return call(
         body,
-        [(1, 384), (104, 256), (104, 256), (16, 256), (16, 256)],
+        [(768, 128), (104, 256), (104, 256), (16, 256), (16, 256)],
         held,
         (b, r1, below, above),
     )
@@ -673,7 +681,10 @@
     column = lax.broadcasted_iota(jnp.int32, (32, 8, 128), 2) % 32
 
     def columns(u):
-        t = dot(jnp.concatenate(split(u), axis=1), m)
+        h = u.astype(bf16)
+        rest = u - h.astype(f32)
+        k, l = split(rest)
+        t = dot(jnp.concatenate([h, k], axis=1), m) + dot(l, m[:128])
         ends = t[:, 128:].reshape(32, 8, 128)
         ends = jnp.where(
             column == 31,
@@ -714,7 +725,6 @@
 
 
 def second_tables(consts):
-    pair(consts, "a", window_operator(MID, 6))
     pair(consts, "c", closed_operator(MID, 6))
     t = np.concatenate([blocks(face_matrix(MID), 3), face_matrix(MID, 6)], axis=1)
     consts["p"] = t.astype(ml_dtypes.bfloat16)
@@ -779,8 +789,8 @@
         e2, ya = lefts([(c, "vd"), (c, "va")], split(right(c, "vc", parts)))
         g = m["wc"][...] * ya + tiles(m["cf"], 8, 1) * yk[32:-32]
 
-        def table(name, count):
-            return tiles(m[name], count, 1)
+        def table(step, count):
+            return damping(MID, m, step, count, 1)
 
         planes = jnp.concatenate(
             [
@@ -795,18 +805,19 @@
         )
         r = jnp.concatenate([below[:64], own_lo[:64], above[:64]], axis=0)
         r = r - m["wc"][...] * mid_faces(c["p"][:, :48], planes) - g[32:224]
-        d = table("d1", 6) * r
+        d = table(0, 6) * r
         x = jnp.concatenate([below[72:104], own_lo[72:104], own_hi[72:104], above[72:104]], axis=0)
         x = x + e2[96:224] + d[32:160]
-        outer = jnp.concatenate([g[:32], g[224:]], axis=0) * table("d1", 2)
+        outer = jnp.concatenate([g[:32], g[224:]], axis=0) * table(0, 2)
         planes = faced(below2, above2, 8, 8) - left(c, "po", split(outer))
         parts = split(d)
         r = r - mid_apply(left(c, "c", parts) + mid_faces(c["p"][:, 48:], planes), parts, m)
-        d = MID.steps[0][0] * d + table("d2", 6) * r
+        d = MID.steps[0][0] * d + table(1, 6) * r
         x = x + d[32:160]
         h, l = split(d)
-        r = r[32:160] - mid_apply(left(c, "a", (h, l)), (h[32:-32], l[32:-32]), m)
-        d = MID.steps[1][0] * d[32:160] + table("d3", 4) * r
+        inner = {"h": c["ch"][32:160], "l": c["cl"][32:160]}
+        r = r[32:160] - mid_apply(left(inner, "", (h, l)), (h[32:-32], l[32:-32]), m)
+        d = MID.steps[1][0] * d[32:160] + table(2, 4) * r
         x = x + d
         h, l = split(x)
         x = jnp.concatenate(
@@ -823,7 +834,7 @@
         s_out[...] = x0[...] + (e1 + d)[:, :256]
         a, plane1 = fine_own(split(d), f, more=[(f, "pl")])
         r = r - a
-        d = FINE.steps[0][0] * d + tiles(f["d2"], 2, 3) * r
+        d = FINE.steps[0][0] * d + damping(FINE, f, 1, 2, 3) * r
         plane2 = left(f, "pl", split(d))
         r_out[...] = r
         d_out[...] = d
@@ -847,10 +858,10 @@
         (out,) = outs
         change = tiles(c["wc"], 1, 3) * on_faces(faced(below, above, 0, 16))
         r = r[...] - change
-        d = d[...] - tiles(c["d2"], 2, 3) * change
+        d = d[...] - damping(FINE, c, 1, 2, 3) * change
         r = r - fine_own(split(d), c, faced(below, above, 16, 16))
         v = s[...] + d[:, :256]
-        d = FINE.steps[1][0] * d + tiles(c["d3"], 2, 3) * r
+        d = FINE.steps[1][0] * d + damping(FINE, c, 2, 2, 3) * r
         v = v + d[:, :256]
         for e in range(2):
             out[:, 8 * e : 8 * e + 8, :] = v[128 * e : 128 * e + 128].reshape(16, 8, 256)
@@ -884,8 +895,7 @@
     x, r, d, low, high = fine_middle(held, b, *both(low, high))
     x0, r0, b, r1, low, high = fine_last(held, x, r, d, *both(low, high))
     chunk, lo, hi, lo2, hi2 = mid_last(held, b, r1, *both(low, high))
-    chunk = jnp.broadcast_to(chunk, (lax.axis_size("gx") * lax.axis_size("gy"), 384))
-    gathered = lax.all_to_all(chunk, ("gx", "gy"), 0, 0, tiled=True)
+    gathered = lax.all_to_all(chunk.reshape(256, 384), ("gx", "gy"), 0, 0, tiled=True)
     s, r, d, low, high = second_smoothing(
         tables(second_tables, mid=mid_constants), gathered, x0, r0, lo, hi, *both(lo, hi), *both(lo2, hi2, 2)
     )

time: 84.2 us -> 84.5 us (level)
  Pallas kernels: 14.3 us -> 15.7 us
  local copies, waits for them, and re-layouts: 5.5 us -> 4.48 us
    pallas_call x7, Pallas kernels: 14.3 us -> 15.7 us  [call(): pl.pallas_call(kernel, out_shape=[jax.ShapeDtypeStruct(s, f32) for s in o...]
    broadcast_in_dim x1 -> x0, local copies, waits for them, and re-layouts: 0.95 us -> none  [local(): jnp.broadcast_to(chunk, (lax.axis_size('gx') * lax.axis_size('gy'), 384))]
where the time goes in v5:
time: 84.5 us; the launch traced here: 84.3 us
  starting transfers between devices  50.9 us (60%)
  Pallas kernels  15.7 us (19%)
  waiting for transfers between devices  13.1 us (16%)
  local copies, waits for them, and re-layouts  4.48 us (5%)
    ppermute x14, starting transfers between devices, fetch(): lax.ppermute(value, axis, [((i + offset) % count, i) for i in range(count)])  38.2 us
    pallas_call x7, Pallas kernels, call(): pl.pallas_call(kernel, out_shape=[jax.ShapeDtypeStruct(s, f32) for s in o...  15.7 us
    all_to_all x1, starting transfers between devices, local(): lax.all_to_all(chunk.reshape(256, 384), ('gx', 'gy'), 0, 0, tiled=True)  12.7 us
    ppermute x14, waiting for transfers between devices, fetch(): lax.ppermute(value, axis, [((i + offset) % count, i) for i in range(count)])  8.22 us
    all_to_all x1, waiting for transfers between devices, local(): lax.all_to_all(chunk.reshape(256, 384), ('gx', 'gy'), 0, 0, tiled=True)  4.84 us
    unnamed x13, local copies, waits for them, and re-layouts  3.5 us
  transfers between devices with their start and end apart: 15, of which 6 were waited for; matrix products, arithmetic and copies ran while one was open for 1% of the time, Pallas kernels for 0%

profile of v5, /device:TPU:1, one launch (start us, length us, event | category | flops | bytes accessed | tf_op | source)
XLA Modules:
  0.0 84.3 jit_solution(3315682830140058988)
XLA Ops:
  0.0 1.0 %fusion = (f32[16,16,128]{2,1,0:T(8,128)S(1)}, f32[16,16,128]{2,1,0:T(8,128)S(1)}) fusion(f32[16,16,256]{2,1,0:T(8,128)} %param.7), kind=kLoop, calls=%fused_computation.1 | loop fusion | bytes 524288 | tf_op jit(solution)/shard_map/slice | solution.py:891
  1.0 2.6 %collective-permute-start.1 = (f32[16,16,128]{2,1,0:T(8,128)S(1)}, f32[16,16,128]{2,1,0:T(8,128)S(1)}, u32[]{:S(2)}, u32[]{:S(2)}) collective-permute-start(f32[16,16,128]{2,1,0:T(8,128)S(1)} %get-tuple-element.53.refs_3_), channel_id=1, source_target_pairs={{7,0},{0,1},{1,2},{2,3},{3,4},{4,5},{5,6},{6,7},{15,8},{8,9},{9,10... | collective-permute-start | bytes 393224 | tf_op jit(solution)/shard_map/ppermute | solution.py:874
  3.6 0.7 collective-permute-start
  4.3 1.5 %copy-done = bf16[7168,128]{1,0:T(8,128)(2,1)S(1)} copy-done((bf16[7168,128]{1,0:T(8,128)(2,1)S(1)}, bf16[7168,128]{1,0:T(8,128)(2,1)}, u32[]{:S(2)}) %copy-start) | copy-done | bytes 1835032
  5.8 1.0 %copy-done.1 = f32[560,128]{1,0:T(8,128)S(1)} copy-done((f32[560,128]{1,0:T(8,128)S(1)}, f32[560,128]{1,0:T(8,128)}, u32[]{:S(2)}) %copy-start.1) | copy-done | bytes 286744
  6.7 1.6 %collective-permute-done.refs_4_ = f32[16,16,128]{2,1,0:T(8,128)S(1)} collective-permute-done((f32[16,16,128]{2,1,0:T(8,128)S(1)}, f32[16,16,128]{2,1,0:T(8,128)S(1)}, u32[]{:S(2)}, u32[]{:S(2)}) %collective-permute-start) | collective-permute-done | bytes 131104 | tf_op jit(solution)/shard_map/ppermute | solution.py:874
  8.3 0.6 shard_map.74
  8.8 1.4 %collective-permute-start.2 = (f32[32,512]{1,0:T(8,128)S(1)}, f32[32,512]{1,0:T(8,128)S(1)}, u32[]{:S(2)}, u32[]{:S(2)}) collective-permute-start(f32[32,512]{1,0:T(8,128)S(1)} %get-tuple-element.30), channel_id=1, source_target_pairs={{248,0},{0,8},{8,16},{16,24},{24,32},{32,40},{40,48},{48,56},{56,6... | collective-permute-start | bytes 196616 | tf_op jit(solution)/shard_map/ppermute | solution.py:874
  10.3 6.5 %collective-permute-start.3 = (f32[32,512]{1,0:T(8,128)S(1)}, f32[32,512]{1,0:T(8,128)S(1)}, u32[]{:S(2)}, u32[]{:S(2)}) collective-permute-start(f32[32,512]{1,0:T(8,128)S(1)} %get-tuple-element.31), channel_id=1, source_target_pairs={{8,0},{16,8},{24,16},{32,24},{40,32},{48,40},{56,48},{64,56},{72,6... | collective-permute-start | bytes 196616 | tf_op jit(solution)/shard_map/ppermute | solution.py:874
  16.7 2.3 %collective-permute-done.2.refs_3_ = f32[32,512]{1,0:T(8,128)S(1)} collective-permute-done((f32[32,512]{1,0:T(8,128)S(1)}, f32[32,512]{1,0:T(8,128)S(1)}, u32[]{:S(2)}, u32[]{:S(2)}) %collective-permute-start.2) | collective-permute-done | bytes 65568 | tf_op jit(solution)/shard_map/ppermute | solution.py:874
  19.0 2.3 %shard_map.75 = (f32[256,256]{1,0:T(8,128)S(1)}, f32[256,512]{1,0:T(8,128)S(1)}, f32[256,512]{1,0:T(8,128)S(1)}, f32[40,512]{1,0:T(8,128)S(1)}, f32[40,512]{1,0:T(8,128)S(1)}) custom-call(f32[560,128]{1,0:T(8,128)S(1)} %copy-done.1, bf16[7168,128]{1,0:T(8,128)(2,1)S(1)} %copy-done, f32[256,512]{1,0:T(8,128)S(1)} %get-tuple-element.29.refs_2_, ...), custom_call_target="tpu_custom_call" | custom-call | tf_op jit(solution)/shard_map/pallas_call | solution.py:415
  21.3 0.1 collective-permute-start.4
  21.4 4.8 %collective-permute-start.5 = (f32[40,512]{1,0:T(8,128)S(1)}, f32[40,512]{1,0:T(8,128)S(1)}, u32[]{:S(2)}, u32[]{:S(2)}) collective-permute-start(f32[40,512]{1,0:T(8,128)S(1)} %get-tuple-element.36), channel_id=1, source_target_pairs={{8,0},{16,8},{24,16},{32,24},{40,32},{48,40},{56,48},{64,56},{72,6... | collective-permute-start | bytes 245768 | tf_op jit(solution)/shard_map/ppermute | solution.py:874
  26.2 1.8 %collective-permute-done.4.refs_5_ = f32[40,512]{1,0:T(8,128)S(1)} collective-permute-done((f32[40,512]{1,0:T(8,128)S(1)}, f32[40,512]{1,0:T(8,128)S(1)}, u32[]{:S(2)}, u32[]{:S(2)}) %collective-permute-start.4) | collective-permute-done | bytes 81952 | tf_op jit(solution)/shard_map/ppermute | solution.py:874
  28.0 0.0 collective-permute-done.5.refs_6_
  28.0 2.0 %shard_map.76 = (f32[256,256]{1,0:T(8,128)S(1)}, f32[256,384]{1,0:T(8,128)S(1)}, f32[64,256]{1,0:T(8,128)S(1)}, f32[64,256]{1,0:T(8,128)S(1)}, f32[16,256]{1,0:T(8,128)S(1)}, /*index=5*/f32[16,256]{1,0:T(8,128)S(1)}) custom-call(f32[560,128]{1,0:T(8,128)S(1)} %copy-done.1, bf16[7168,128]{1,0:T(8,128)(2,1)S(1)} %copy-done, ...), custom_call_target="tpu_custom_call" | custom-call | tf_op jit(solution)/shard_map/pallas_call | solution.py:415
  30.0 4.8 %collective-permute-start.7 = (f32[16,256]{1,0:T(8,128)S(1)}, f32[16,256]{1,0:T(8,128)S(1)}, u32[]{:S(2)}, u32[]{:S(2)}) collective-permute-start(f32[16,256]{1,0:T(8,128)S(1)} %get-tuple-element.40), channel_id=1, source_target_pairs={{8,0},{16,8},{24,16},{32,24},{40,32},{48,40},{56,48},{64,56},{72,6... | collective-permute-start | bytes 49160 | tf_op jit(solution)/shard_map/ppermute | solution.py:874
  34.8 1.1 %collective-permute-done.6.refs_4_ = f32[16,256]{1,0:T(8,128)S(1)} collective-permute-done((f32[16,256]{1,0:T(8,128)S(1)}, f32[16,256]{1,0:T(8,128)S(1)}, u32[]{:S(2)}, u32[]{:S(2)}) %collective-permute-start.6) | collective-permute-done | bytes 16416 | tf_op jit(solution)/shard_map/ppermute | solution.py:874
  35.9 1.7 %shard_map.77 = (f32[768,128]{1,0:T(8,128)}, f32[104,256]{1,0:T(8,128)S(1)}, f32[104,256]{1,0:T(8,128)S(1)}, f32[16,256]{1,0:T(8,128)S(1)}, f32[16,256]{1,0:T(8,128)S(1)}) custom-call(f32[560,128]{1,0:T(8,128)S(1)} %copy-done.1, bf16[7168,128]{1,0:T(8,128)(2,1)S(1)} %copy-done, f32[64,256]{1,0:T(8,128)S(1)} %get-tuple-element.37.refs_2_, ...), custom_call_target="tpu_custom_call" | custom-call | tf_op jit(solution)/shard_map/pallas_call | solution.py:415
  37.6 12.7 %all-to-all-start = ((f32[256,1,384]{2,1,0:T(1,128)}), f32[256,1,384]{2,1,0:T(1,128)}, u32[]{:S(2)}, u32[]{:S(2)}) async-start(f32[256,1,384]{2,1,0:T(1,128)} %bitcast), calls=%async_computation | async-start | bytes 786432 | tf_op jit(solution)/shard_map/all_to_all | solution.py:898
  50.4 6.7 %collective-permute-start.9 = (f32[104,256]{1,0:T(8,128)S(1)}, f32[104,256]{1,0:T(8,128)S(1)}, u32[]{:S(2)}, u32[]{:S(2)}) collective-permute-start(f32[104,256]{1,0:T(8,128)S(1)} %get-tuple-element.44.refs_5_), channel_id=1, source_target_pairs={{8,0},{16,8},{24,16},{32,24},{40,32},{48,40},{56,48},{64,56},{72,6... | collective-permute-start | bytes 319496 | tf_op jit(solution)/shard_map/ppermute | solution.py:874
  57.1 0.0 collective-permute-start.10
  57.1 5.7 %collective-permute-start.11 = (f32[16,256]{1,0:T(8,128)S(1)}, f32[16,256]{1,0:T(8,128)S(1)}, u32[]{:S(2)}, u32[]{:S(2)}) collective-permute-start(f32[16,256]{1,0:T(8,128)S(1)} %get-tuple-element.47), channel_id=1, source_target_pairs={{16,0},{24,8},{32,16},{40,24},{48,32},{56,40},{64,48},{72,56},{80,... | collective-permute-start | bytes 49160 | tf_op jit(solution)/shard_map/ppermute | solution.py:874
  62.8 4.8 %all-to-all-done = f32[256,1,384]{2,1,0:T(1,128)} async-done(((f32[256,1,384]{2,1,0:T(1,128)}), f32[256,1,384]{2,1,0:T(1,128)}, u32[]{:S(2)}, u32[]{:S(2)}) %all-to-all-start) | async-done | bytes 393248 | tf_op jit(solution)/shard_map/all_to_all | solution.py:898
  67.6 1.0 %copy.11 = f32[256,1,384]{2,0,1:T(8,128)S(1)} copy(f32[256,1,384]{2,1,0:T(1,128)} %all-to-all-done) | data formatting | bytes 786432
  68.6 0.0 copy-start.3
  68.7 0.0 copy-start.5
  68.7 7.9 %shard_map.78 = (f32[256,256]{1,0:T(8,128)S(1)}, f32[256,384]{1,0:T(8,128)S(1)}, f32[256,384]{1,0:T(8,128)S(1)}, f32[32,384]{1,0:T(8,128)S(1)}, f32[32,384]{1,0:T(8,128)S(1)}) custom-call(f32[432,128]{1,0:T(8,128)S(1)} %copy-done.4, bf16[7200,128]{1,0:T(8,128)(2,1)S(1)} %copy-done.2, f32[256,384]{1,0:T(8,128)S(1)} %bitcast.4, ...), custom_call_target="tpu_custom_call" | custom-call | tf_op jit(solution)/shard_map/pallas_call | solution.py:415
  76.7 0.8 collective-permute-start.12
  77.5 4.0 %collective-permute-start.13 = (f32[32,384]{1,0:T(8,128)S(1)}, f32[32,384]{1,0:T(8,128)S(1)}, u32[]{:S(2)}, u32[]{:S(2)}) collective-permute-start(f32[32,384]{1,0:T(8,128)S(1)} %get-tuple-element.52), channel_id=1, source_target_pairs={{8,0},{16,8},{24,16},{32,24},{40,32},{48,40},{56,48},{64,56},{72,6... | collective-permute-start | bytes 147464 | tf_op jit(solution)/shard_map/ppermute | solution.py:874
  81.5 1.5 %collective-permute-done.12.refs_5_ = f32[32,384]{1,0:T(8,128)S(1)} collective-permute-done((f32[32,384]{1,0:T(8,128)S(1)}, f32[32,384]{1,0:T(8,128)S(1)}, u32[]{:S(2)}, u32[]{:S(2)}) %collective-permute-start.12) | collective-permute-done | bytes 49184 | tf_op jit(solution)/shard_map/ppermute | solution.py:874
  83.0 1.2 %shard_map.79 = f32[16,16,256]{2,1,0:T(8,128)} custom-call(f32[272,128]{1,0:T(8,128)S(1)} %copy-done.5, bf16[1664,128]{1,0:T(8,128)(2,1)S(1)} %copy-done.3, f32[256,256]{1,0:T(8,128)S(1)} %get-tuple-element.48.refs_2_, f32[256,384]{1,0:T(8,128)S(1)} %get-tuple-element.49.refs_3_, f32[256,384]{1,0:T(8,128)S(1)} %get-tuple-element.50.refs_4_, ...), custom_call_target="tpu_custom_call" | custom-call | tf_op jit(solution)/shard_map/pallas_call | solution.py:415
  (19 shorter events, 0.0 us)
Async XLA Ops:
  1.0 5.7 %collective-permute-start.1 = (f32[16,16,128]{2,1,0:T(8,128)S(1)}, f32[16,16,128]{2,1,0:T(8,128)S(1)}, u32[]{:S(2)}, u32[]{:S(2)}) collective-permute-start(f32[16,16,128]{2,1,0:T(8,128)S(1)} %get-tuple-element.53.refs_3_), channel_id=1, source_target_pairs={{7,0},{0,1},{1,2},{2,3},{3,4},{4,5},{5,6},{6,7},{15,8},{8,9},{9,10... | collective-permute-start | bytes 393224 | tf_op jit(solution)/shard_map/ppermute | solution.py:874
  3.6 4.7 %collective-permute-start = (f32[16,16,128]{2,1,0:T(8,128)S(1)}, f32[16,16,128]{2,1,0:T(8,128)S(1)}, u32[]{:S(2)}, u32[]{:S(2)}) collective-permute-start(f32[16,16,128]{2,1,0:T(8,128)S(1)} %get-tuple-element.54.refs_2_), channel_id=1, source_target_pairs={{1,0},{2,1},{3,2},{4,3},{5,4},{6,5},{7,6},{0,7},{9,8},{10,9},{11,1... | collective-permute-start | bytes 393224 | tf_op jit(solution)/shard_map/ppermute | solution.py:874
  4.3 1.5 %copy-start = (bf16[7168,128]{1,0:T(8,128)(2,1)S(1)}, bf16[7168,128]{1,0:T(8,128)(2,1)}, u32[]{:S(2)}) copy-start(bf16[7168,128]{1,0:T(8,128)(2,1)} %constant.13.clone.refs_1_) | copy-start | bytes 5505028
  5.8 1.0 %copy-start.1 = (f32[560,128]{1,0:T(8,128)S(1)}, f32[560,128]{1,0:T(8,128)}, u32[]{:S(2)}) copy-start(f32[560,128]{1,0:T(8,128)} %constant.12.clone.refs_0_) | copy-start | bytes 860164
  8.8 10.2 %collective-permute-start.2 = (f32[32,512]{1,0:T(8,128)S(1)}, f32[32,512]{1,0:T(8,128)S(1)}, u32[]{:S(2)}, u32[]{:S(2)}) collective-permute-start(f32[32,512]{1,0:T(8,128)S(1)} %get-tuple-element.30), channel_id=1, source_target_pairs={{248,0},{0,8},{8,16},{16,24},{24,32},{32,40},{40,48},{48,56},{56,6... | collective-permute-start | bytes 196616 | tf_op jit(solution)/shard_map/ppermute | solution.py:874
  10.3 8.7 %collective-permute-start.3 = (f32[32,512]{1,0:T(8,128)S(1)}, f32[32,512]{1,0:T(8,128)S(1)}, u32[]{:S(2)}, u32[]{:S(2)}) collective-permute-start(f32[32,512]{1,0:T(8,128)S(1)} %get-tuple-element.31), channel_id=1, source_target_pairs={{8,0},{16,8},{24,16},{32,24},{40,32},{48,40},{56,48},{64,56},{72,6... | collective-permute-start | bytes 196616 | tf_op jit(solution)/shard_map/ppermute | solution.py:874
  21.3 6.7 %collective-permute-start.4 = (f32[40,512]{1,0:T(8,128)S(1)}, f32[40,512]{1,0:T(8,128)S(1)}, u32[]{:S(2)}, u32[]{:S(2)}) collective-permute-start(f32[40,512]{1,0:T(8,128)S(1)} %get-tuple-element.35), channel_id=1, source_target_pairs={{248,0},{0,8},{8,16},{16,24},{24,32},{32,40},{40,48},{48,56},{56,6... | collective-permute-start | bytes 245768 | tf_op jit(solution)/shard_map/ppermute | solution.py:874
  21.4 6.6 %collective-permute-start.5 = (f32[40,512]{1,0:T(8,128)S(1)}, f32[40,512]{1,0:T(8,128)S(1)}, u32[]{:S(2)}, u32[]{:S(2)}) collective-permute-start(f32[40,512]{1,0:T(8,128)S(1)} %get-tuple-element.36), channel_id=1, source_target_pairs={{8,0},{16,8},{24,16},{32,24},{40,32},{48,40},{56,48},{64,56},{72,6... | collective-permute-start | bytes 245768 | tf_op jit(solution)/shard_map/ppermute | solution.py:874
  30.0 5.9 %collective-permute-start.6 = (f32[16,256]{1,0:T(8,128)S(1)}, f32[16,256]{1,0:T(8,128)S(1)}, u32[]{:S(2)}, u32[]{:S(2)}) collective-permute-start(f32[16,256]{1,0:T(8,128)S(1)} %get-tuple-element.39), channel_id=1, source_target_pairs={{248,0},{0,8},{8,16},{16,24},{24,32},{32,40},{40,48},{48,56},{56,6... | collective-permute-start | bytes 49160 | tf_op jit(solution)/shard_map/ppermute | solution.py:874
  30.0 5.9 %collective-permute-start.7 = (f32[16,256]{1,0:T(8,128)S(1)}, f32[16,256]{1,0:T(8,128)S(1)}, u32[]{:S(2)}, u32[]{:S(2)}) collective-permute-start(f32[16,256]{1,0:T(8,128)S(1)} %get-tuple-element.40), channel_id=1, source_target_pairs={{8,0},{16,8},{24,16},{32,24},{40,32},{48,40},{56,48},{64,56},{72,6... | collective-permute-start | bytes 49160 | tf_op jit(solution)/shard_map/ppermute | solution.py:874
  35.9 32.8 %copy-start.2 = (bf16[7200,128]{1,0:T(8,128)(2,1)S(1)}, bf16[7200,128]{1,0:T(8,128)(2,1)}, u32[]{:S(2)}) copy-start(bf16[7200,128]{1,0:T(8,128)(2,1)} %constant.15.clone.refs_1_) | copy-start | bytes 5529604
  35.9 32.8 %copy-start.4 = (f32[432,128]{1,0:T(8,128)S(1)}, f32[432,128]{1,0:T(8,128)}, u32[]{:S(2)}) copy-start(f32[432,128]{1,0:T(8,128)} %constant.14.clone.refs_0_) | copy-start | bytes 663556
  37.6 30.0 %all-to-all-start = ((f32[256,1,384]{2,1,0:T(1,128)}), f32[256,1,384]{2,1,0:T(1,128)}, u32[]{:S(2)}, u32[]{:S(2)}) async-start(f32[256,1,384]{2,1,0:T(1,128)} %bitcast), calls=%async_computation | async-start | bytes 786432 | tf_op jit(solution)/shard_map/all_to_all | solution.py:898
  50.4 18.3 %collective-permute-start.9 = (f32[104,256]{1,0:T(8,128)S(1)}, f32[104,256]{1,0:T(8,128)S(1)}, u32[]{:S(2)}, u32[]{:S(2)}) collective-permute-start(f32[104,256]{1,0:T(8,128)S(1)} %get-tuple-element.44.refs_5_), channel_id=1, source_target_pairs={{8,0},{16,8},{24,16},{32,24},{40,32},{48,40},{56,48},{64,56},{72,6... | collective-permute-start | bytes 319496 | tf_op jit(solution)/shard_map/ppermute | solution.py:874
  57.1 11.6 %collective-permute-start.8 = (f32[104,256]{1,0:T(8,128)S(1)}, f32[104,256]{1,0:T(8,128)S(1)}, u32[]{:S(2)}, u32[]{:S(2)}) collective-permute-start(f32[104,256]{1,0:T(8,128)S(1)} %get-tuple-element.45.refs_6_), channel_id=1, source_target_pairs={{248,0},{0,8},{8,16},{16,24},{24,32},{32,40},{40,48},{48,56},{56,6... | collective-permute-start | bytes 319496 | tf_op jit(solution)/shard_map/ppermute | solution.py:874
  57.1 11.6 %collective-permute-start.10 = (f32[16,256]{1,0:T(8,128)S(1)}, f32[16,256]{1,0:T(8,128)S(1)}, u32[]{:S(2)}, u32[]{:S(2)}) collective-permute-start(f32[16,256]{1,0:T(8,128)S(1)} %get-tuple-element.46), channel_id=1, source_target_pairs={{240,0},{248,8},{0,16},{8,24},{16,32},{24,40},{32,48},{40,56},{48,... | collective-permute-start | bytes 49160 | tf_op jit(solution)/shard_map/ppermute | solution.py:874
  57.1 11.6 %collective-permute-start.11 = (f32[16,256]{1,0:T(8,128)S(1)}, f32[16,256]{1,0:T(8,128)S(1)}, u32[]{:S(2)}, u32[]{:S(2)}) collective-permute-start(f32[16,256]{1,0:T(8,128)S(1)} %get-tuple-element.47), channel_id=1, source_target_pairs={{16,0},{24,8},{32,16},{40,24},{48,32},{56,40},{64,48},{72,56},{80,... | collective-permute-start | bytes 49160 | tf_op jit(solution)/shard_map/ppermute | solution.py:874
  68.6 14.4 %copy-start.3 = (bf16[1664,128]{1,0:T(8,128)(2,1)S(1)}, bf16[1664,128]{1,0:T(8,128)(2,1)}, u32[]{:S(2)}) copy-start(bf16[1664,128]{1,0:T(8,128)(2,1)} %constant.17.clone.refs_1_) | copy-start | bytes 1277956
  68.7 14.4 %copy-start.5 = (f32[272,128]{1,0:T(8,128)S(1)}, f32[272,128]{1,0:T(8,128)}, u32[]{:S(2)}) copy-start(f32[272,128]{1,0:T(8,128)} %constant.16.clone.refs_0_) | copy-start | bytes 417796
  76.7 6.3 %collective-permute-start.12 = (f32[32,384]{1,0:T(8,128)S(1)}, f32[32,384]{1,0:T(8,128)S(1)}, u32[]{:S(2)}, u32[]{:S(2)}) collective-permute-start(f32[32,384]{1,0:T(8,128)S(1)} %get-tuple-element.51), channel_id=1, source_target_pairs={{248,0},{0,8},{8,16},{16,24},{24,32},{32,40},{40,48},{48,56},{56,6... | collective-permute-start | bytes 147464 | tf_op jit(solution)/shard_map/ppermute | solution.py:874
  77.5 5.5 %collective-permute-start.13 = (f32[32,384]{1,0:T(8,128)S(1)}, f32[32,384]{1,0:T(8,128)S(1)}, u32[]{:S(2)}, u32[]{:S(2)}) collective-permute-start(f32[32,384]{1,0:T(8,128)S(1)} %get-tuple-element.52), channel_id=1, source_target_pairs={{8,0},{16,8},{24,16},{32,24},{40,32},{48,40},{56,48},{64,56},{72,6... | collective-permute-start | bytes 147464 | tf_op jit(solution)/shard_map/ppermute | solution.py:874

commit v6 on v5

--- a/solution.py
+++ b/solution.py
@@ -403,7 +403,7 @@
     return call(body, [(8, 128)], held, ())[0]
 
 
-def call(body, outs, held, args, scratch=(), vmem=24):
+def call(body, outs, held, args, scratch=(), vmem=24, direct=0):
     arrays, places = held
     n, k = len(arrays), len(args)
 
@@ -416,7 +416,7 @@
         kernel,
         out_shape=[jax.ShapeDtypeStruct(s, f32) for s in outs],
         in_specs=[spec] * (n + k),
-        out_specs=[spec] * len(outs),
+        out_specs=[pl.BlockSpec(memory_space=pl.ANY)] * direct + [spec] * (len(outs) - direct),
         scratch_shapes=list(scratch),
         compiler_params=pltpu.CompilerParams(vmem_limit_bytes=vmem * MB),
     )(*arrays, *args)
@@ -610,7 +610,7 @@
 def mid_last(held, b, r1, below, above):
     def body(c, ins, outs):
         b, r1, below, above = ins
-        chunk, lo, hi, lo2, hi2 = outs
+        chunk, lo, hi, lo2, hi2, block, sems = outs
         down, c = c, under(c, "m_")
         d1, d2, d3 = (damping(MID, c, k, 2, 1) for k in range(3))
         d = d1 * b[...]
@@ -630,10 +630,15 @@
         q = lax.broadcasted_iota(jnp.int32, t.shape, 0)
         lane = lax.broadcasted_iota(jnp.int32, t.shape, 1) // 32
         t = jnp.sum(jnp.where(q == lane, t, 0.0), axis=0, keepdims=True)
-        which = lax.broadcasted_iota(jnp.int32, chunk.shape, 0) % 3
-        chunk[...] = jnp.where(
+        which = lax.broadcasted_iota(jnp.int32, block.shape, 0) % 3
+        block[...] = jnp.where(
             which == 0, t[:, :128], jnp.where(which == 1, t[:, 128:256], t[:, 256:])
         )
+        copies = [
+            pltpu.make_async_copy(block, chunk.at[pl.ds(192 * k, 192)], sems.at[k]) for k in range(4)
+        ]
+        for copy in copies:
+            copy.start()
         plane1 = left(c, "pl", parts)
         r = r - mid_own(d, c)
         plane2 = left(c, "pl", split(d1 * r))
@@ -643,12 +648,16 @@
             near[72:104] = x[32 * at : 32 * at + 32]
             far[0:8] = plane1[8 * at : 8 * at + 8]
             far[8:16] = plane2[8 * at : 8 * at + 8]
+        for copy in copies:
+            copy.wait()
 
     return call(
         body,
         [(768, 128), (104, 256), (104, 256), (16, 256), (16, 256)],
         held,
         (b, r1, below, above),
+        scratch=[pltpu.VMEM((192, 128), f32), pltpu.SemaphoreType.DMA((4,))],
+        direct=1,
     )
 
 

time: 84.5 us -> 84.4 us (level)
  no operation moved by 1% of the time
where the time goes in v6:
time: 84.4 us; the launch traced here: 84.1 us
  starting transfers between devices  50.9 us (60%)
  Pallas kernels  15.6 us (18%)
  waiting for transfers between devices  13.1 us (16%)
  local copies, waits for them, and re-layouts  4.48 us (5%)
    ppermute x14, starting transfers between devices, fetch(): lax.ppermute(value, axis, [((i + offset) % count, i) for i in range(count)])  38.2 us
    pallas_call x7, Pallas kernels, call(): pl.pallas_call(kernel, out_shape=[jax.ShapeDtypeStruct(s, f32) for s in o...  15.6 us
    all_to_all x1, starting transfers between devices, local(): lax.all_to_all(chunk.reshape(256, 384), ('gx', 'gy'), 0, 0, tiled=True)  12.7 us
    ppermute x14, waiting for transfers between devices, fetch(): lax.ppermute(value, axis, [((i + offset) % count, i) for i in range(count)])  8.22 us
    all_to_all x1, waiting for transfers between devices, local(): lax.all_to_all(chunk.reshape(256, 384), ('gx', 'gy'), 0, 0, tiled=True)  4.84 us
    unnamed x13, local copies, waits for them, and re-layouts  3.5 us
  transfers between devices with their start and end apart: 15, of which 6 were waited for; matrix products, arithmetic and copies ran while one was open for 1% of the time, Pallas kernels for 0%

profile of v6, /device:TPU:1, one launch (start us, length us, event | category | flops | bytes accessed | tf_op | source)
XLA Modules:
  0.0 84.1 jit_solution(1084718199114727951)
XLA Ops:
  0.0 1.0 %fusion = (f32[16,16,128]{2,1,0:T(8,128)S(1)}, f32[16,16,128]{2,1,0:T(8,128)S(1)}) fusion(f32[16,16,256]{2,1,0:T(8,128)} %param.7), kind=kLoop, calls=%fused_computation.1 | loop fusion | bytes 524288 | tf_op jit(solution)/shard_map/slice | solution.py:900
  1.0 2.6 %collective-permute-start.1 = (f32[16,16,128]{2,1,0:T(8,128)S(1)}, f32[16,16,128]{2,1,0:T(8,128)S(1)}, u32[]{:S(2)}, u32[]{:S(2)}) collective-permute-start(f32[16,16,128]{2,1,0:T(8,128)S(1)} %get-tuple-element.53.refs_3_), channel_id=1, source_target_pairs={{7,0},{0,1},{1,2},{2,3},{3,4},{4,5},{5,6},{6,7},{15,8},{8,9},{9,10... | collective-permute-start | bytes 393224 | tf_op jit(solution)/shard_map/ppermute | solution.py:883
  3.6 0.7 collective-permute-start
  4.3 1.5 %copy-done = bf16[7168,128]{1,0:T(8,128)(2,1)S(1)} copy-done((bf16[7168,128]{1,0:T(8,128)(2,1)S(1)}, bf16[7168,128]{1,0:T(8,128)(2,1)}, u32[]{:S(2)}) %copy-start) | copy-done | bytes 1835032
  5.8 1.0 %copy-done.1 = f32[560,128]{1,0:T(8,128)S(1)} copy-done((f32[560,128]{1,0:T(8,128)S(1)}, f32[560,128]{1,0:T(8,128)}, u32[]{:S(2)}) %copy-start.1) | copy-done | bytes 286744
  6.7 1.6 %collective-permute-done.refs_4_ = f32[16,16,128]{2,1,0:T(8,128)S(1)} collective-permute-done((f32[16,16,128]{2,1,0:T(8,128)S(1)}, f32[16,16,128]{2,1,0:T(8,128)S(1)}, u32[]{:S(2)}, u32[]{:S(2)}) %collective-permute-start) | collective-permute-done | bytes 131104 | tf_op jit(solution)/shard_map/ppermute | solution.py:883
  8.3 0.6 shard_map.74
  8.8 1.4 %collective-permute-start.2 = (f32[32,512]{1,0:T(8,128)S(1)}, f32[32,512]{1,0:T(8,128)S(1)}, u32[]{:S(2)}, u32[]{:S(2)}) collective-permute-start(f32[32,512]{1,0:T(8,128)S(1)} %get-tuple-element.30), channel_id=1, source_target_pairs={{248,0},{0,8},{8,16},{16,24},{24,32},{32,40},{40,48},{48,56},{56,6... | collective-permute-start | bytes 196616 | tf_op jit(solution)/shard_map/ppermute | solution.py:883
  10.3 6.5 %collective-permute-start.3 = (f32[32,512]{1,0:T(8,128)S(1)}, f32[32,512]{1,0:T(8,128)S(1)}, u32[]{:S(2)}, u32[]{:S(2)}) collective-permute-start(f32[32,512]{1,0:T(8,128)S(1)} %get-tuple-element.31), channel_id=1, source_target_pairs={{8,0},{16,8},{24,16},{32,24},{40,32},{48,40},{56,48},{64,56},{72,6... | collective-permute-start | bytes 196616 | tf_op jit(solution)/shard_map/ppermute | solution.py:883
  16.7 2.3 %collective-permute-done.2.refs_3_ = f32[32,512]{1,0:T(8,128)S(1)} collective-permute-done((f32[32,512]{1,0:T(8,128)S(1)}, f32[32,512]{1,0:T(8,128)S(1)}, u32[]{:S(2)}, u32[]{:S(2)}) %collective-permute-start.2) | collective-permute-done | bytes 65568 | tf_op jit(solution)/shard_map/ppermute | solution.py:883
  19.0 2.3 %shard_map.75 = (f32[256,256]{1,0:T(8,128)S(1)}, f32[256,512]{1,0:T(8,128)S(1)}, f32[256,512]{1,0:T(8,128)S(1)}, f32[40,512]{1,0:T(8,128)S(1)}, f32[40,512]{1,0:T(8,128)S(1)}) custom-call(f32[560,128]{1,0:T(8,128)S(1)} %copy-done.1, bf16[7168,128]{1,0:T(8,128)(2,1)S(1)} %copy-done, f32[256,512]{1,0:T(8,128)S(1)} %get-tuple-element.29.refs_2_, ...), custom_call_target="tpu_custom_call" | custom-call | tf_op jit(solution)/shard_map/pallas_call | solution.py:415
  21.3 0.1 collective-permute-start.4
  21.4 4.8 %collective-permute-start.5 = (f32[40,512]{1,0:T(8,128)S(1)}, f32[40,512]{1,0:T(8,128)S(1)}, u32[]{:S(2)}, u32[]{:S(2)}) collective-permute-start(f32[40,512]{1,0:T(8,128)S(1)} %get-tuple-element.36), channel_id=1, source_target_pairs={{8,0},{16,8},{24,16},{32,24},{40,32},{48,40},{56,48},{64,56},{72,6... | collective-permute-start | bytes 245768 | tf_op jit(solution)/shard_map/ppermute | solution.py:883
  26.2 1.8 %collective-permute-done.4.refs_5_ = f32[40,512]{1,0:T(8,128)S(1)} collective-permute-done((f32[40,512]{1,0:T(8,128)S(1)}, f32[40,512]{1,0:T(8,128)S(1)}, u32[]{:S(2)}, u32[]{:S(2)}) %collective-permute-start.4) | collective-permute-done | bytes 81952 | tf_op jit(solution)/shard_map/ppermute | solution.py:883
  28.0 0.0 collective-permute-done.5.refs_6_
  28.0 2.0 %shard_map.76 = (f32[256,256]{1,0:T(8,128)S(1)}, f32[256,384]{1,0:T(8,128)S(1)}, f32[64,256]{1,0:T(8,128)S(1)}, f32[64,256]{1,0:T(8,128)S(1)}, f32[16,256]{1,0:T(8,128)S(1)}, /*index=5*/f32[16,256]{1,0:T(8,128)S(1)}) custom-call(f32[560,128]{1,0:T(8,128)S(1)} %copy-done.1, bf16[7168,128]{1,0:T(8,128)(2,1)S(1)} %copy-done, ...), custom_call_target="tpu_custom_call" | custom-call | tf_op jit(solution)/shard_map/pallas_call | solution.py:415
  30.0 4.8 %collective-permute-start.7 = (f32[16,256]{1,0:T(8,128)S(1)}, f32[16,256]{1,0:T(8,128)S(1)}, u32[]{:S(2)}, u32[]{:S(2)}) collective-permute-start(f32[16,256]{1,0:T(8,128)S(1)} %get-tuple-element.40), channel_id=1, source_target_pairs={{8,0},{16,8},{24,16},{32,24},{40,32},{48,40},{56,48},{64,56},{72,6... | collective-permute-start | bytes 49160 | tf_op jit(solution)/shard_map/ppermute | solution.py:883
  34.8 1.1 %collective-permute-done.6.refs_4_ = f32[16,256]{1,0:T(8,128)S(1)} collective-permute-done((f32[16,256]{1,0:T(8,128)S(1)}, f32[16,256]{1,0:T(8,128)S(1)}, u32[]{:S(2)}, u32[]{:S(2)}) %collective-permute-start.6) | collective-permute-done | bytes 16416 | tf_op jit(solution)/shard_map/ppermute | solution.py:883
  35.9 1.5 %shard_map.77 = (f32[768,128]{1,0:T(8,128)}, f32[104,256]{1,0:T(8,128)S(1)}, f32[104,256]{1,0:T(8,128)S(1)}, f32[16,256]{1,0:T(8,128)S(1)}, f32[16,256]{1,0:T(8,128)S(1)}) custom-call(f32[560,128]{1,0:T(8,128)S(1)} %copy-done.1, bf16[7168,128]{1,0:T(8,128)(2,1)S(1)} %copy-done, f32[64,256]{1,0:T(8,128)S(1)} %get-tuple-element.37.refs_2_, ...), custom_call_target="tpu_custom_call" | custom-call | tf_op jit(solution)/shard_map/pallas_call | solution.py:415
  37.5 12.7 %all-to-all-start = ((f32[256,1,384]{2,1,0:T(1,128)}), f32[256,1,384]{2,1,0:T(1,128)}, u32[]{:S(2)}, u32[]{:S(2)}) async-start(f32[256,1,384]{2,1,0:T(1,128)} %bitcast), calls=%async_computation | async-start | bytes 786432 | tf_op jit(solution)/shard_map/all_to_all | solution.py:907
  50.2 6.7 %collective-permute-start.9 = (f32[104,256]{1,0:T(8,128)S(1)}, f32[104,256]{1,0:T(8,128)S(1)}, u32[]{:S(2)}, u32[]{:S(2)}) collective-permute-start(f32[104,256]{1,0:T(8,128)S(1)} %get-tuple-element.44.refs_5_), channel_id=1, source_target_pairs={{8,0},{16,8},{24,16},{32,24},{40,32},{48,40},{56,48},{64,56},{72,6... | collective-permute-start | bytes 319496 | tf_op jit(solution)/shard_map/ppermute | solution.py:883
  56.9 0.0 collective-permute-start.10
  56.9 5.7 %collective-permute-start.11 = (f32[16,256]{1,0:T(8,128)S(1)}, f32[16,256]{1,0:T(8,128)S(1)}, u32[]{:S(2)}, u32[]{:S(2)}) collective-permute-start(f32[16,256]{1,0:T(8,128)S(1)} %get-tuple-element.47), channel_id=1, source_target_pairs={{16,0},{24,8},{32,16},{40,24},{48,32},{56,40},{64,48},{72,56},{80,... | collective-permute-start | bytes 49160 | tf_op jit(solution)/shard_map/ppermute | solution.py:883
  62.6 4.8 %all-to-all-done = f32[256,1,384]{2,1,0:T(1,128)} async-done(((f32[256,1,384]{2,1,0:T(1,128)}), f32[256,1,384]{2,1,0:T(1,128)}, u32[]{:S(2)}, u32[]{:S(2)}) %all-to-all-start) | async-done | bytes 393248 | tf_op jit(solution)/shard_map/all_to_all | solution.py:907
  67.5 1.0 %copy.11 = f32[256,1,384]{2,0,1:T(8,128)S(1)} copy(f32[256,1,384]{2,1,0:T(1,128)} %all-to-all-done) | data formatting | bytes 786432
  68.5 0.0 copy-start.3
  68.5 0.0 copy-start.5
  68.6 7.9 %shard_map.78 = (f32[256,256]{1,0:T(8,128)S(1)}, f32[256,384]{1,0:T(8,128)S(1)}, f32[256,384]{1,0:T(8,128)S(1)}, f32[32,384]{1,0:T(8,128)S(1)}, f32[32,384]{1,0:T(8,128)S(1)}) custom-call(f32[432,128]{1,0:T(8,128)S(1)} %copy-done.4, bf16[7200,128]{1,0:T(8,128)(2,1)S(1)} %copy-done.2, f32[256,384]{1,0:T(8,128)S(1)} %bitcast.4, ...), custom_call_target="tpu_custom_call" | custom-call | tf_op jit(solution)/shard_map/pallas_call | solution.py:415
  76.5 0.8 collective-permute-start.12
  77.4 4.0 %collective-permute-start.13 = (f32[32,384]{1,0:T(8,128)S(1)}, f32[32,384]{1,0:T(8,128)S(1)}, u32[]{:S(2)}, u32[]{:S(2)}) collective-permute-start(f32[32,384]{1,0:T(8,128)S(1)} %get-tuple-element.52), channel_id=1, source_target_pairs={{8,0},{16,8},{24,16},{32,24},{40,32},{48,40},{56,48},{64,56},{72,6... | collective-permute-start | bytes 147464 | tf_op jit(solution)/shard_map/ppermute | solution.py:883
  81.4 1.5 %collective-permute-done.12.refs_5_ = f32[32,384]{1,0:T(8,128)S(1)} collective-permute-done((f32[32,384]{1,0:T(8,128)S(1)}, f32[32,384]{1,0:T(8,128)S(1)}, u32[]{:S(2)}, u32[]{:S(2)}) %collective-permute-start.12) | collective-permute-done | bytes 49184 | tf_op jit(solution)/shard_map/ppermute | solution.py:883
  82.9 1.2 %shard_map.79 = f32[16,16,256]{2,1,0:T(8,128)} custom-call(f32[272,128]{1,0:T(8,128)S(1)} %copy-done.5, bf16[1664,128]{1,0:T(8,128)(2,1)S(1)} %copy-done.3, f32[256,256]{1,0:T(8,128)S(1)} %get-tuple-element.48.refs_2_, f32[256,384]{1,0:T(8,128)S(1)} %get-tuple-element.49.refs_3_, f32[256,384]{1,0:T(8,128)S(1)} %get-tuple-element.50.refs_4_, ...), custom_call_target="tpu_custom_call" | custom-call | tf_op jit(solution)/shard_map/pallas_call | solution.py:415
  (19 shorter events, 0.0 us)
Async XLA Ops:
  1.0 5.7 %collective-permute-start.1 = (f32[16,16,128]{2,1,0:T(8,128)S(1)}, f32[16,16,128]{2,1,0:T(8,128)S(1)}, u32[]{:S(2)}, u32[]{:S(2)}) collective-permute-start(f32[16,16,128]{2,1,0:T(8,128)S(1)} %get-tuple-element.53.refs_3_), channel_id=1, source_target_pairs={{7,0},{0,1},{1,2},{2,3},{3,4},{4,5},{5,6},{6,7},{15,8},{8,9},{9,10... | collective-permute-start | bytes 393224 | tf_op jit(solution)/shard_map/ppermute | solution.py:883
  3.6 4.7 %collective-permute-start = (f32[16,16,128]{2,1,0:T(8,128)S(1)}, f32[16,16,128]{2,1,0:T(8,128)S(1)}, u32[]{:S(2)}, u32[]{:S(2)}) collective-permute-start(f32[16,16,128]{2,1,0:T(8,128)S(1)} %get-tuple-element.54.refs_2_), channel_id=1, source_target_pairs={{1,0},{2,1},{3,2},{4,3},{5,4},{6,5},{7,6},{0,7},{9,8},{10,9},{11,1... | collective-permute-start | bytes 393224 | tf_op jit(solution)/shard_map/ppermute | solution.py:883
  4.3 1.5 %copy-start = (bf16[7168,128]{1,0:T(8,128)(2,1)S(1)}, bf16[7168,128]{1,0:T(8,128)(2,1)}, u32[]{:S(2)}) copy-start(bf16[7168,128]{1,0:T(8,128)(2,1)} %constant.13.clone.refs_1_) | copy-start | bytes 5505028
  5.8 1.0 %copy-start.1 = (f32[560,128]{1,0:T(8,128)S(1)}, f32[560,128]{1,0:T(8,128)}, u32[]{:S(2)}) copy-start(f32[560,128]{1,0:T(8,128)} %constant.12.clone.refs_0_) | copy-start | bytes 860164
  8.8 10.2 %collective-permute-start.2 = (f32[32,512]{1,0:T(8,128)S(1)}, f32[32,512]{1,0:T(8,128)S(1)}, u32[]{:S(2)}, u32[]{:S(2)}) collective-permute-start(f32[32,512]{1,0:T(8,128)S(1)} %get-tuple-element.30), channel_id=1, source_target_pairs={{248,0},{0,8},{8,16},{16,24},{24,32},{32,40},{40,48},{48,56},{56,6... | collective-permute-start | bytes 196616 | tf_op jit(solution)/shard_map/ppermute | solution.py:883
  10.3 8.7 %collective-permute-start.3 = (f32[32,512]{1,0:T(8,128)S(1)}, f32[32,512]{1,0:T(8,128)S(1)}, u32[]{:S(2)}, u32[]{:S(2)}) collective-permute-start(f32[32,512]{1,0:T(8,128)S(1)} %get-tuple-element.31), channel_id=1, source_target_pairs={{8,0},{16,8},{24,16},{32,24},{40,32},{48,40},{56,48},{64,56},{72,6... | collective-permute-start | bytes 196616 | tf_op jit(solution)/shard_map/ppermute | solution.py:883
  21.3 6.7 %collective-permute-start.4 = (f32[40,512]{1,0:T(8,128)S(1)}, f32[40,512]{1,0:T(8,128)S(1)}, u32[]{:S(2)}, u32[]{:S(2)}) collective-permute-start(f32[40,512]{1,0:T(8,128)S(1)} %get-tuple-element.35), channel_id=1, source_target_pairs={{248,0},{0,8},{8,16},{16,24},{24,32},{32,40},{40,48},{48,56},{56,6... | collective-permute-start | bytes 245768 | tf_op jit(solution)/shard_map/ppermute | solution.py:883
  21.4 6.6 %collective-permute-start.5 = (f32[40,512]{1,0:T(8,128)S(1)}, f32[40,512]{1,0:T(8,128)S(1)}, u32[]{:S(2)}, u32[]{:S(2)}) collective-permute-start(f32[40,512]{1,0:T(8,128)S(1)} %get-tuple-element.36), channel_id=1, source_target_pairs={{8,0},{16,8},{24,16},{32,24},{40,32},{48,40},{56,48},{64,56},{72,6... | collective-permute-start | bytes 245768 | tf_op jit(solution)/shard_map/ppermute | solution.py:883
  30.0 5.9 %collective-permute-start.6 = (f32[16,256]{1,0:T(8,128)S(1)}, f32[16,256]{1,0:T(8,128)S(1)}, u32[]{:S(2)}, u32[]{:S(2)}) collective-permute-start(f32[16,256]{1,0:T(8,128)S(1)} %get-tuple-element.39), channel_id=1, source_target_pairs={{248,0},{0,8},{8,16},{16,24},{24,32},{32,40},{40,48},{48,56},{56,6... | collective-permute-start | bytes 49160 | tf_op jit(solution)/shard_map/ppermute | solution.py:883
  30.0 5.9 %collective-permute-start.7 = (f32[16,256]{1,0:T(8,128)S(1)}, f32[16,256]{1,0:T(8,128)S(1)}, u32[]{:S(2)}, u32[]{:S(2)}) collective-permute-start(f32[16,256]{1,0:T(8,128)S(1)} %get-tuple-element.40), channel_id=1, source_target_pairs={{8,0},{16,8},{24,16},{32,24},{40,32},{48,40},{56,48},{64,56},{72,6... | collective-permute-start | bytes 49160 | tf_op jit(solution)/shard_map/ppermute | solution.py:883
  35.9 32.6 %copy-start.2 = (bf16[7200,128]{1,0:T(8,128)(2,1)S(1)}, bf16[7200,128]{1,0:T(8,128)(2,1)}, u32[]{:S(2)}) copy-start(bf16[7200,128]{1,0:T(8,128)(2,1)} %constant.15.clone.refs_1_) | copy-start | bytes 5529604
  35.9 32.6 %copy-start.4 = (f32[432,128]{1,0:T(8,128)S(1)}, f32[432,128]{1,0:T(8,128)}, u32[]{:S(2)}) copy-start(f32[432,128]{1,0:T(8,128)} %constant.14.clone.refs_0_) | copy-start | bytes 663556
  37.5 30.0 %all-to-all-start = ((f32[256,1,384]{2,1,0:T(1,128)}), f32[256,1,384]{2,1,0:T(1,128)}, u32[]{:S(2)}, u32[]{:S(2)}) async-start(f32[256,1,384]{2,1,0:T(1,128)} %bitcast), calls=%async_computation | async-start | bytes 786432 | tf_op jit(solution)/shard_map/all_to_all | solution.py:907
  50.2 18.3 %collective-permute-start.9 = (f32[104,256]{1,0:T(8,128)S(1)}, f32[104,256]{1,0:T(8,128)S(1)}, u32[]{:S(2)}, u32[]{:S(2)}) collective-permute-start(f32[104,256]{1,0:T(8,128)S(1)} %get-tuple-element.44.refs_5_), channel_id=1, source_target_pairs={{8,0},{16,8},{24,16},{32,24},{40,32},{48,40},{56,48},{64,56},{72,6... | collective-permute-start | bytes 319496 | tf_op jit(solution)/shard_map/ppermute | solution.py:883
  56.9 11.6 %collective-permute-start.8 = (f32[104,256]{1,0:T(8,128)S(1)}, f32[104,256]{1,0:T(8,128)S(1)}, u32[]{:S(2)}, u32[]{:S(2)}) collective-permute-start(f32[104,256]{1,0:T(8,128)S(1)} %get-tuple-element.45.refs_6_), channel_id=1, source_target_pairs={{248,0},{0,8},{8,16},{16,24},{24,32},{32,40},{40,48},{48,56},{56,6... | collective-permute-start | bytes 319496 | tf_op jit(solution)/shard_map/ppermute | solution.py:883
  56.9 11.6 %collective-permute-start.10 = (f32[16,256]{1,0:T(8,128)S(1)}, f32[16,256]{1,0:T(8,128)S(1)}, u32[]{:S(2)}, u32[]{:S(2)}) collective-permute-start(f32[16,256]{1,0:T(8,128)S(1)} %get-tuple-element.46), channel_id=1, source_target_pairs={{240,0},{248,8},{0,16},{8,24},{16,32},{24,40},{32,48},{40,56},{48,... | collective-permute-start | bytes 49160 | tf_op jit(solution)/shard_map/ppermute | solution.py:883
  56.9 11.6 %collective-permute-start.11 = (f32[16,256]{1,0:T(8,128)S(1)}, f32[16,256]{1,0:T(8,128)S(1)}, u32[]{:S(2)}, u32[]{:S(2)}) collective-permute-start(f32[16,256]{1,0:T(8,128)S(1)} %get-tuple-element.47), channel_id=1, source_target_pairs={{16,0},{24,8},{32,16},{40,24},{48,32},{56,40},{64,48},{72,56},{80,... | collective-permute-start | bytes 49160 | tf_op jit(solution)/shard_map/ppermute | solution.py:883
  68.5 14.4 %copy-start.3 = (bf16[1664,128]{1,0:T(8,128)(2,1)S(1)}, bf16[1664,128]{1,0:T(8,128)(2,1)}, u32[]{:S(2)}) copy-start(bf16[1664,128]{1,0:T(8,128)(2,1)} %constant.17.clone.refs_1_) | copy-start | bytes 1277956
  68.5 14.4 %copy-start.5 = (f32[272,128]{1,0:T(8,128)S(1)}, f32[272,128]{1,0:T(8,128)}, u32[]{:S(2)}) copy-start(f32[272,128]{1,0:T(8,128)} %constant.16.clone.refs_0_) | copy-start | bytes 417796
  76.5 6.3 %collective-permute-start.12 = (f32[32,384]{1,0:T(8,128)S(1)}, f32[32,384]{1,0:T(8,128)S(1)}, u32[]{:S(2)}, u32[]{:S(2)}) collective-permute-start(f32[32,384]{1,0:T(8,128)S(1)} %get-tuple-element.51), channel_id=1, source_target_pairs={{248,0},{0,8},{8,16},{16,24},{24,32},{32,40},{40,48},{48,56},{56,6... | collective-permute-start | bytes 147464 | tf_op jit(solution)/shard_map/ppermute | solution.py:883
  77.4 5.5 %collective-permute-start.13 = (f32[32,384]{1,0:T(8,128)S(1)}, f32[32,384]{1,0:T(8,128)S(1)}, u32[]{:S(2)}, u32[]{:S(2)}) collective-permute-start(f32[32,384]{1,0:T(8,128)S(1)} %get-tuple-element.52), channel_id=1, source_target_pairs={{8,0},{16,8},{24,16},{32,24},{40,32},{48,40},{56,48},{64,56},{72,6... | collective-permute-start | bytes 147464 | tf_op jit(solution)/shard_map/ppermute | solution.py:883

commit v7 on v6

--- a/solution.py
+++ b/solution.py
@@ -905,8 +905,9 @@
     x0, r0, b, r1, low, high = fine_last(held, x, r, d, *both(low, high))
     chunk, lo, hi, lo2, hi2 = mid_last(held, b, r1, *both(low, high))
     gathered = lax.all_to_all(chunk.reshape(256, 384), ("gx", "gy"), 0, 0, tiled=True)
+    far = both(lo2, hi2, 2)
     s, r, d, low, high = second_smoothing(
-        tables(second_tables, mid=mid_constants), gathered, x0, r0, lo, hi, *both(lo, hi), *both(lo2, hi2, 2)
+        tables(second_tables, mid=mid_constants), gathered, x0, r0, lo, hi, *both(lo, hi), *far
     )
     return last_step(tables(mid=dict), s, r, d, *both(low, high))
 

time: 84.4 us -> 84.4 us (level)
  no operation moved by 1% of the time
where the time goes in v7:
time: 84.4 us; the launch traced here: 84.1 us
  starting transfers between devices  50.9 us (60%)
  Pallas kernels  15.6 us (18%)
  waiting for transfers between devices  13.1 us (16%)
  local copies, waits for them, and re-layouts  4.48 us (5%)
    ppermute x14, starting transfers between devices, fetch(): lax.ppermute(value, axis, [((i + offset) % count, i) for i in range(count)])  38.2 us
    pallas_call x7, Pallas kernels, call(): pl.pallas_call(kernel, out_shape=[jax.ShapeDtypeStruct(s, f32) for s in o...  15.6 us
    all_to_all x1, starting transfers between devices, local(): lax.all_to_all(chunk.reshape(256, 384), ('gx', 'gy'), 0, 0, tiled=True)  12.7 us
    ppermute x14, waiting for transfers between devices, fetch(): lax.ppermute(value, axis, [((i + offset) % count, i) for i in range(count)])  8.22 us
    all_to_all x1, waiting for transfers between devices, local(): lax.all_to_all(chunk.reshape(256, 384), ('gx', 'gy'), 0, 0, tiled=True)  4.84 us
    unnamed x13, local copies, waits for them, and re-layouts  3.5 us
  transfers between devices with their start and end apart: 15, of which 6 were waited for; matrix products, arithmetic and copies ran while one was open for 1% of the time, Pallas kernels for 0%

profile of v7, /device:TPU:1, one launch (start us, length us, event | category | flops | bytes accessed | tf_op | source)
XLA Modules:
  0.0 84.1 jit_solution(1084718199114727951)
XLA Ops:
  0.0 1.0 %fusion = (f32[16,16,128]{2,1,0:T(8,128)S(1)}, f32[16,16,128]{2,1,0:T(8,128)S(1)}) fusion(f32[16,16,256]{2,1,0:T(8,128)} %param.7), kind=kLoop, calls=%fused_computation.1 | loop fusion | bytes 524288 | tf_op jit(solution)/shard_map/slice | solution.py:900
  1.0 2.6 %collective-permute-start.1 = (f32[16,16,128]{2,1,0:T(8,128)S(1)}, f32[16,16,128]{2,1,0:T(8,128)S(1)}, u32[]{:S(2)}, u32[]{:S(2)}) collective-permute-start(f32[16,16,128]{2,1,0:T(8,128)S(1)} %get-tuple-element.53.refs_3_), channel_id=1, source_target_pairs={{7,0},{0,1},{1,2},{2,3},{3,4},{4,5},{5,6},{6,7},{15,8},{8,9},{9,10... | collective-permute-start | bytes 393224 | tf_op jit(solution)/shard_map/ppermute | solution.py:883
  3.6 0.7 collective-permute-start
  4.3 1.5 %copy-done = bf16[7168,128]{1,0:T(8,128)(2,1)S(1)} copy-done((bf16[7168,128]{1,0:T(8,128)(2,1)S(1)}, bf16[7168,128]{1,0:T(8,128)(2,1)}, u32[]{:S(2)}) %copy-start) | copy-done | bytes 1835032
  5.8 1.0 %copy-done.1 = f32[560,128]{1,0:T(8,128)S(1)} copy-done((f32[560,128]{1,0:T(8,128)S(1)}, f32[560,128]{1,0:T(8,128)}, u32[]{:S(2)}) %copy-start.1) | copy-done | bytes 286744
  6.7 1.6 %collective-permute-done.refs_4_ = f32[16,16,128]{2,1,0:T(8,128)S(1)} collective-permute-done((f32[16,16,128]{2,1,0:T(8,128)S(1)}, f32[16,16,128]{2,1,0:T(8,128)S(1)}, u32[]{:S(2)}, u32[]{:S(2)}) %collective-permute-start) | collective-permute-done | bytes 131104 | tf_op jit(solution)/shard_map/ppermute | solution.py:883
  8.3 0.6 shard_map.74
  8.8 1.4 %collective-permute-start.2 = (f32[32,512]{1,0:T(8,128)S(1)}, f32[32,512]{1,0:T(8,128)S(1)}, u32[]{:S(2)}, u32[]{:S(2)}) collective-permute-start(f32[32,512]{1,0:T(8,128)S(1)} %get-tuple-element.30), channel_id=1, source_target_pairs={{248,0},{0,8},{8,16},{16,24},{24,32},{32,40},{40,48},{48,56},{56,6... | collective-permute-start | bytes 196616 | tf_op jit(solution)/shard_map/ppermute | solution.py:883
  10.3 6.5 %collective-permute-start.3 = (f32[32,512]{1,0:T(8,128)S(1)}, f32[32,512]{1,0:T(8,128)S(1)}, u32[]{:S(2)}, u32[]{:S(2)}) collective-permute-start(f32[32,512]{1,0:T(8,128)S(1)} %get-tuple-element.31), channel_id=1, source_target_pairs={{8,0},{16,8},{24,16},{32,24},{40,32},{48,40},{56,48},{64,56},{72,6... | collective-permute-start | bytes 196616 | tf_op jit(solution)/shard_map/ppermute | solution.py:883
  16.7 2.3 %collective-permute-done.2.refs_3_ = f32[32,512]{1,0:T(8,128)S(1)} collective-permute-done((f32[32,512]{1,0:T(8,128)S(1)}, f32[32,512]{1,0:T(8,128)S(1)}, u32[]{:S(2)}, u32[]{:S(2)}) %collective-permute-start.2) | collective-permute-done | bytes 65568 | tf_op jit(solution)/shard_map/ppermute | solution.py:883
  19.0 2.3 %shard_map.75 = (f32[256,256]{1,0:T(8,128)S(1)}, f32[256,512]{1,0:T(8,128)S(1)}, f32[256,512]{1,0:T(8,128)S(1)}, f32[40,512]{1,0:T(8,128)S(1)}, f32[40,512]{1,0:T(8,128)S(1)}) custom-call(f32[560,128]{1,0:T(8,128)S(1)} %copy-done.1, bf16[7168,128]{1,0:T(8,128)(2,1)S(1)} %copy-done, f32[256,512]{1,0:T(8,128)S(1)} %get-tuple-element.29.refs_2_, ...), custom_call_target="tpu_custom_call" | custom-call | tf_op jit(solution)/shard_map/pallas_call | solution.py:415
  21.3 0.1 collective-permute-start.4
  21.4 4.8 %collective-permute-start.5 = (f32[40,512]{1,0:T(8,128)S(1)}, f32[40,512]{1,0:T(8,128)S(1)}, u32[]{:S(2)}, u32[]{:S(2)}) collective-permute-start(f32[40,512]{1,0:T(8,128)S(1)} %get-tuple-element.36), channel_id=1, source_target_pairs={{8,0},{16,8},{24,16},{32,24},{40,32},{48,40},{56,48},{64,56},{72,6... | collective-permute-start | bytes 245768 | tf_op jit(solution)/shard_map/ppermute | solution.py:883
  26.2 1.8 %collective-permute-done.4.refs_5_ = f32[40,512]{1,0:T(8,128)S(1)} collective-permute-done((f32[40,512]{1,0:T(8,128)S(1)}, f32[40,512]{1,0:T(8,128)S(1)}, u32[]{:S(2)}, u32[]{:S(2)}) %collective-permute-start.4) | collective-permute-done | bytes 81952 | tf_op jit(solution)/shard_map/ppermute | solution.py:883
  28.0 0.0 collective-permute-done.5.refs_6_
  28.0 2.0 %shard_map.76 = (f32[256,256]{1,0:T(8,128)S(1)}, f32[256,384]{1,0:T(8,128)S(1)}, f32[64,256]{1,0:T(8,128)S(1)}, f32[64,256]{1,0:T(8,128)S(1)}, f32[16,256]{1,0:T(8,128)S(1)}, /*index=5*/f32[16,256]{1,0:T(8,128)S(1)}) custom-call(f32[560,128]{1,0:T(8,128)S(1)} %copy-done.1, bf16[7168,128]{1,0:T(8,128)(2,1)S(1)} %copy-done, ...), custom_call_target="tpu_custom_call" | custom-call | tf_op jit(solution)/shard_map/pallas_call | solution.py:415
  30.0 4.8 %collective-permute-start.7 = (f32[16,256]{1,0:T(8,128)S(1)}, f32[16,256]{1,0:T(8,128)S(1)}, u32[]{:S(2)}, u32[]{:S(2)}) collective-permute-start(f32[16,256]{1,0:T(8,128)S(1)} %get-tuple-element.40), channel_id=1, source_target_pairs={{8,0},{16,8},{24,16},{32,24},{40,32},{48,40},{56,48},{64,56},{72,6... | collective-permute-start | bytes 49160 | tf_op jit(solution)/shard_map/ppermute | solution.py:883
  34.8 1.1 %collective-permute-done.6.refs_4_ = f32[16,256]{1,0:T(8,128)S(1)} collective-permute-done((f32[16,256]{1,0:T(8,128)S(1)}, f32[16,256]{1,0:T(8,128)S(1)}, u32[]{:S(2)}, u32[]{:S(2)}) %collective-permute-start.6) | collective-permute-done | bytes 16416 | tf_op jit(solution)/shard_map/ppermute | solution.py:883
  35.9 1.5 %shard_map.77 = (f32[768,128]{1,0:T(8,128)}, f32[104,256]{1,0:T(8,128)S(1)}, f32[104,256]{1,0:T(8,128)S(1)}, f32[16,256]{1,0:T(8,128)S(1)}, f32[16,256]{1,0:T(8,128)S(1)}) custom-call(f32[560,128]{1,0:T(8,128)S(1)} %copy-done.1, bf16[7168,128]{1,0:T(8,128)(2,1)S(1)} %copy-done, f32[64,256]{1,0:T(8,128)S(1)} %get-tuple-element.37.refs_2_, ...), custom_call_target="tpu_custom_call" | custom-call | tf_op jit(solution)/shard_map/pallas_call | solution.py:415
  37.5 12.7 %all-to-all-start = ((f32[256,1,384]{2,1,0:T(1,128)}), f32[256,1,384]{2,1,0:T(1,128)}, u32[]{:S(2)}, u32[]{:S(2)}) async-start(f32[256,1,384]{2,1,0:T(1,128)} %bitcast), calls=%async_computation | async-start | bytes 786432 | tf_op jit(solution)/shard_map/all_to_all | solution.py:907
  50.2 6.7 %collective-permute-start.9 = (f32[104,256]{1,0:T(8,128)S(1)}, f32[104,256]{1,0:T(8,128)S(1)}, u32[]{:S(2)}, u32[]{:S(2)}) collective-permute-start(f32[104,256]{1,0:T(8,128)S(1)} %get-tuple-element.44.refs_5_), channel_id=1, source_target_pairs={{8,0},{16,8},{24,16},{32,24},{40,32},{48,40},{56,48},{64,56},{72,6... | collective-permute-start | bytes 319496 | tf_op jit(solution)/shard_map/ppermute | solution.py:883
  56.9 0.0 collective-permute-start.10
  56.9 5.7 %collective-permute-start.11 = (f32[16,256]{1,0:T(8,128)S(1)}, f32[16,256]{1,0:T(8,128)S(1)}, u32[]{:S(2)}, u32[]{:S(2)}) collective-permute-start(f32[16,256]{1,0:T(8,128)S(1)} %get-tuple-element.47), channel_id=1, source_target_pairs={{16,0},{24,8},{32,16},{40,24},{48,32},{56,40},{64,48},{72,56},{80,... | collective-permute-start | bytes 49160 | tf_op jit(solution)/shard_map/ppermute | solution.py:883
  62.6 4.8 %all-to-all-done = f32[256,1,384]{2,1,0:T(1,128)} async-done(((f32[256,1,384]{2,1,0:T(1,128)}), f32[256,1,384]{2,1,0:T(1,128)}, u32[]{:S(2)}, u32[]{:S(2)}) %all-to-all-start) | async-done | bytes 393248 | tf_op jit(solution)/shard_map/all_to_all | solution.py:907
  67.5 1.0 %copy.11 = f32[256,1,384]{2,0,1:T(8,128)S(1)} copy(f32[256,1,384]{2,1,0:T(1,128)} %all-to-all-done) | data formatting | bytes 786432
  68.5 0.0 copy-start.3
  68.5 0.0 copy-start.5
  68.6 7.9 %shard_map.78 = (f32[256,256]{1,0:T(8,128)S(1)}, f32[256,384]{1,0:T(8,128)S(1)}, f32[256,384]{1,0:T(8,128)S(1)}, f32[32,384]{1,0:T(8,128)S(1)}, f32[32,384]{1,0:T(8,128)S(1)}) custom-call(f32[432,128]{1,0:T(8,128)S(1)} %copy-done.4, bf16[7200,128]{1,0:T(8,128)(2,1)S(1)} %copy-done.2, f32[256,384]{1,0:T(8,128)S(1)} %bitcast.4, ...), custom_call_target="tpu_custom_call" | custom-call | tf_op jit(solution)/shard_map/pallas_call | solution.py:415
  76.5 0.8 collective-permute-start.12
  77.4 4.0 %collective-permute-start.13 = (f32[32,384]{1,0:T(8,128)S(1)}, f32[32,384]{1,0:T(8,128)S(1)}, u32[]{:S(2)}, u32[]{:S(2)}) collective-permute-start(f32[32,384]{1,0:T(8,128)S(1)} %get-tuple-element.52), channel_id=1, source_target_pairs={{8,0},{16,8},{24,16},{32,24},{40,32},{48,40},{56,48},{64,56},{72,6... | collective-permute-start | bytes 147464 | tf_op jit(solution)/shard_map/ppermute | solution.py:883
  81.4 1.5 %collective-permute-done.12.refs_5_ = f32[32,384]{1,0:T(8,128)S(1)} collective-permute-done((f32[32,384]{1,0:T(8,128)S(1)}, f32[32,384]{1,0:T(8,128)S(1)}, u32[]{:S(2)}, u32[]{:S(2)}) %collective-permute-start.12) | collective-permute-done | bytes 49184 | tf_op jit(solution)/shard_map/ppermute | solution.py:883
  82.9 1.2 %shard_map.79 = f32[16,16,256]{2,1,0:T(8,128)} custom-call(f32[272,128]{1,0:T(8,128)S(1)} %copy-done.5, bf16[1664,128]{1,0:T(8,128)(2,1)S(1)} %copy-done.3, f32[256,256]{1,0:T(8,128)S(1)} %get-tuple-element.48.refs_2_, f32[256,384]{1,0:T(8,128)S(1)} %get-tuple-element.49.refs_3_, f32[256,384]{1,0:T(8,128)S(1)} %get-tuple-element.50.refs_4_, ...), custom_call_target="tpu_custom_call" | custom-call | tf_op jit(solution)/shard_map/pallas_call | solution.py:415
  (19 shorter events, 0.0 us)
Async XLA Ops:
  1.0 5.7 %collective-permute-start.1 = (f32[16,16,128]{2,1,0:T(8,128)S(1)}, f32[16,16,128]{2,1,0:T(8,128)S(1)}, u32[]{:S(2)}, u32[]{:S(2)}) collective-permute-start(f32[16,16,128]{2,1,0:T(8,128)S(1)} %get-tuple-element.53.refs_3_), channel_id=1, source_target_pairs={{7,0},{0,1},{1,2},{2,3},{3,4},{4,5},{5,6},{6,7},{15,8},{8,9},{9,10... | collective-permute-start | bytes 393224 | tf_op jit(solution)/shard_map/ppermute | solution.py:883
  3.6 4.7 %collective-permute-start = (f32[16,16,128]{2,1,0:T(8,128)S(1)}, f32[16,16,128]{2,1,0:T(8,128)S(1)}, u32[]{:S(2)}, u32[]{:S(2)}) collective-permute-start(f32[16,16,128]{2,1,0:T(8,128)S(1)} %get-tuple-element.54.refs_2_), channel_id=1, source_target_pairs={{1,0},{2,1},{3,2},{4,3},{5,4},{6,5},{7,6},{0,7},{9,8},{10,9},{11,1... | collective-permute-start | bytes 393224 | tf_op jit(solution)/shard_map/ppermute | solution.py:883
  4.3 1.5 %copy-start = (bf16[7168,128]{1,0:T(8,128)(2,1)S(1)}, bf16[7168,128]{1,0:T(8,128)(2,1)}, u32[]{:S(2)}) copy-start(bf16[7168,128]{1,0:T(8,128)(2,1)} %constant.13.clone.refs_1_) | copy-start | bytes 5505028
  5.8 1.0 %copy-start.1 = (f32[560,128]{1,0:T(8,128)S(1)}, f32[560,128]{1,0:T(8,128)}, u32[]{:S(2)}) copy-start(f32[560,128]{1,0:T(8,128)} %constant.12.clone.refs_0_) | copy-start | bytes 860164
  8.8 10.2 %collective-permute-start.2 = (f32[32,512]{1,0:T(8,128)S(1)}, f32[32,512]{1,0:T(8,128)S(1)}, u32[]{:S(2)}, u32[]{:S(2)}) collective-permute-start(f32[32,512]{1,0:T(8,128)S(1)} %get-tuple-element.30), channel_id=1, source_target_pairs={{248,0},{0,8},{8,16},{16,24},{24,32},{32,40},{40,48},{48,56},{56,6... | collective-permute-start | bytes 196616 | tf_op jit(solution)/shard_map/ppermute | solution.py:883
  10.3 8.7 %collective-permute-start.3 = (f32[32,512]{1,0:T(8,128)S(1)}, f32[32,512]{1,0:T(8,128)S(1)}, u32[]{:S(2)}, u32[]{:S(2)}) collective-permute-start(f32[32,512]{1,0:T(8,128)S(1)} %get-tuple-element.31), channel_id=1, source_target_pairs={{8,0},{16,8},{24,16},{32,24},{40,32},{48,40},{56,48},{64,56},{72,6... | collective-permute-start | bytes 196616 | tf_op jit(solution)/shard_map/ppermute | solution.py:883
  21.3 6.7 %collective-permute-start.4 = (f32[40,512]{1,0:T(8,128)S(1)}, f32[40,512]{1,0:T(8,128)S(1)}, u32[]{:S(2)}, u32[]{:S(2)}) collective-permute-start(f32[40,512]{1,0:T(8,128)S(1)} %get-tuple-element.35), channel_id=1, source_target_pairs={{248,0},{0,8},{8,16},{16,24},{24,32},{32,40},{40,48},{48,56},{56,6... | collective-permute-start | bytes 245768 | tf_op jit(solution)/shard_map/ppermute | solution.py:883
  21.4 6.6 %collective-permute-start.5 = (f32[40,512]{1,0:T(8,128)S(1)}, f32[40,512]{1,0:T(8,128)S(1)}, u32[]{:S(2)}, u32[]{:S(2)}) collective-permute-start(f32[40,512]{1,0:T(8,128)S(1)} %get-tuple-element.36), channel_id=1, source_target_pairs={{8,0},{16,8},{24,16},{32,24},{40,32},{48,40},{56,48},{64,56},{72,6... | collective-permute-start | bytes 245768 | tf_op jit(solution)/shard_map/ppermute | solution.py:883
  30.0 5.9 %collective-permute-start.6 = (f32[16,256]{1,0:T(8,128)S(1)}, f32[16,256]{1,0:T(8,128)S(1)}, u32[]{:S(2)}, u32[]{:S(2)}) collective-permute-start(f32[16,256]{1,0:T(8,128)S(1)} %get-tuple-element.39), channel_id=1, source_target_pairs={{248,0},{0,8},{8,16},{16,24},{24,32},{32,40},{40,48},{48,56},{56,6... | collective-permute-start | bytes 49160 | tf_op jit(solution)/shard_map/ppermute | solution.py:883
  30.0 5.9 %collective-permute-start.7 = (f32[16,256]{1,0:T(8,128)S(1)}, f32[16,256]{1,0:T(8,128)S(1)}, u32[]{:S(2)}, u32[]{:S(2)}) collective-permute-start(f32[16,256]{1,0:T(8,128)S(1)} %get-tuple-element.40), channel_id=1, source_target_pairs={{8,0},{16,8},{24,16},{32,24},{40,32},{48,40},{56,48},{64,56},{72,6... | collective-permute-start | bytes 49160 | tf_op jit(solution)/shard_map/ppermute | solution.py:883
  35.9 32.6 %copy-start.2 = (bf16[7200,128]{1,0:T(8,128)(2,1)S(1)}, bf16[7200,128]{1,0:T(8,128)(2,1)}, u32[]{:S(2)}) copy-start(bf16[7200,128]{1,0:T(8,128)(2,1)} %constant.15.clone.refs_1_) | copy-start | bytes 5529604
  35.9 32.6 %copy-start.4 = (f32[432,128]{1,0:T(8,128)S(1)}, f32[432,128]{1,0:T(8,128)}, u32[]{:S(2)}) copy-start(f32[432,128]{1,0:T(8,128)} %constant.14.clone.refs_0_) | copy-start | bytes 663556
  37.5 30.0 %all-to-all-start = ((f32[256,1,384]{2,1,0:T(1,128)}), f32[256,1,384]{2,1,0:T(1,128)}, u32[]{:S(2)}, u32[]{:S(2)}) async-start(f32[256,1,384]{2,1,0:T(1,128)} %bitcast), calls=%async_computation | async-start | bytes 786432 | tf_op jit(solution)/shard_map/all_to_all | solution.py:907
  50.2 18.3 %collective-permute-start.9 = (f32[104,256]{1,0:T(8,128)S(1)}, f32[104,256]{1,0:T(8,128)S(1)}, u32[]{:S(2)}, u32[]{:S(2)}) collective-permute-start(f32[104,256]{1,0:T(8,128)S(1)} %get-tuple-element.44.refs_5_), channel_id=1, source_target_pairs={{8,0},{16,8},{24,16},{32,24},{40,32},{48,40},{56,48},{64,56},{72,6... | collective-permute-start | bytes 319496 | tf_op jit(solution)/shard_map/ppermute | solution.py:883
  56.9 11.6 %collective-permute-start.8 = (f32[104,256]{1,0:T(8,128)S(1)}, f32[104,256]{1,0:T(8,128)S(1)}, u32[]{:S(2)}, u32[]{:S(2)}) collective-permute-start(f32[104,256]{1,0:T(8,128)S(1)} %get-tuple-element.45.refs_6_), channel_id=1, source_target_pairs={{248,0},{0,8},{8,16},{16,24},{24,32},{32,40},{40,48},{48,56},{56,6... | collective-permute-start | bytes 319496 | tf_op jit(solution)/shard_map/ppermute | solution.py:883
  56.9 11.6 %collective-permute-start.10 = (f32[16,256]{1,0:T(8,128)S(1)}, f32[16,256]{1,0:T(8,128)S(1)}, u32[]{:S(2)}, u32[]{:S(2)}) collective-permute-start(f32[16,256]{1,0:T(8,128)S(1)} %get-tuple-element.46), channel_id=1, source_target_pairs={{240,0},{248,8},{0,16},{8,24},{16,32},{24,40},{32,48},{40,56},{48,... | collective-permute-start | bytes 49160 | tf_op jit(solution)/shard_map/ppermute | solution.py:883
  56.9 11.6 %collective-permute-start.11 = (f32[16,256]{1,0:T(8,128)S(1)}, f32[16,256]{1,0:T(8,128)S(1)}, u32[]{:S(2)}, u32[]{:S(2)}) collective-permute-start(f32[16,256]{1,0:T(8,128)S(1)} %get-tuple-element.47), channel_id=1, source_target_pairs={{16,0},{24,8},{32,16},{40,24},{48,32},{56,40},{64,48},{72,56},{80,... | collective-permute-start | bytes 49160 | tf_op jit(solution)/shard_map/ppermute | solution.py:883
  68.5 14.4 %copy-start.3 = (bf16[1664,128]{1,0:T(8,128)(2,1)S(1)}, bf16[1664,128]{1,0:T(8,128)(2,1)}, u32[]{:S(2)}) copy-start(bf16[1664,128]{1,0:T(8,128)(2,1)} %constant.17.clone.refs_1_) | copy-start | bytes 1277956
  68.5 14.4 %copy-start.5 = (f32[272,128]{1,0:T(8,128)S(1)}, f32[272,128]{1,0:T(8,128)}, u32[]{:S(2)}) copy-start(f32[272,128]{1,0:T(8,128)} %constant.16.clone.refs_0_) | copy-start | bytes 417796
  76.5 6.3 %collective-permute-start.12 = (f32[32,384]{1,0:T(8,128)S(1)}, f32[32,384]{1,0:T(8,128)S(1)}, u32[]{:S(2)}, u32[]{:S(2)}) collective-permute-start(f32[32,384]{1,0:T(8,128)S(1)} %get-tuple-element.51), channel_id=1, source_target_pairs={{248,0},{0,8},{8,16},{16,24},{24,32},{32,40},{40,48},{48,56},{56,6... | collective-permute-start | bytes 147464 | tf_op jit(solution)/shard_map/ppermute | solution.py:883
  77.4 5.5 %collective-permute-start.13 = (f32[32,384]{1,0:T(8,128)S(1)}, f32[32,384]{1,0:T(8,128)S(1)}, u32[]{:S(2)}, u32[]{:S(2)}) collective-permute-start(f32[32,384]{1,0:T(8,128)S(1)} %get-tuple-element.52), channel_id=1, source_target_pairs={{8,0},{16,8},{24,16},{32,24},{40,32},{48,40},{56,48},{64,56},{72,6... | collective-permute-start | bytes 147464 | tf_op jit(solution)/shard_map/ppermute | solution.py:883
